TPU v7x, 256 devices: a whole 4x4x8 slice. The times are simulated.
256 devices in a mesh: seq: 64 (over z, x, core), head: 4 (over y).
Axes of the slice: x: 4, y: 4, z: 8, core: 2. Of those that a mesh axis runs over, the one named last changes fastest.
Arguments:
- query: bfloat16 [16384, 2048], P('seq', 'head'), may hold values from -24 to 24
- key: bfloat16 [16384, 512], P('seq', 'head'), may hold values from -24 to 24
- value: bfloat16 [16384, 512], P('seq', 'head'), may hold values from -6 to 6
- grad_out: bfloat16 [16384, 2048], P('seq', 'head'), may hold values from -6 to 6
- gate_score: int32 [4, 32, 32], P('head'), may hold values from 0 to 1048575
Outputs:
- attended: bfloat16 [16384, 2048], P('seq', 'head')
- grad_query: bfloat16 [16384, 2048], P('seq', 'head')
- grad_key: bfloat16 [16384, 512], P('seq', 'head')
- grad_value: bfloat16 [16384, 512], P('seq', 'head')
All inputs are finite; a program needn't handle non-finite values.
Results may differ from a plain program's by a relative error of at most 0.03.
Values may be sent and summed in bfloat16 or wider, within the bound.
No kernel may reach another device: no remote copies, remote signals or barrier semaphores. Data moves between devices by JAX's collectives and lax.ppermute only.
A program may use at most 192 MiB of HBM per device.

v0:
```python
import functools
import math

import jax
import jax.numpy as jnp
from jax import lax
from jax.experimental import pallas as pl
from jax.experimental.pallas import tpu as pltpu
from jax.sharding import Mesh
from jax.sharding import PartitionSpec as P

HEAD_DIM = 128
GROUP = 4
TOPK = 8
NBLK = 32
HALF = 256
COLS = GROUP * HALF
SCALE = 1.0 / math.sqrt(HEAD_DIM)
SCALE2 = SCALE / math.log(2.0)
NEG = -1e30
MASKED = -3e38
BF = jnp.bfloat16
F32 = jnp.float32
SIZES = {"z": 8, "x": 4}
NT = (((1,), (1,)), ((), ()))
NN = (((1,), (0,)), ((), ()))
CORE_AT = 32
QUAD = 4
VMEM_LIMIT = 24 * 1024 * 1024
STAT = (2, 3, COLS)
ACC = (HEAD_DIM, COLS)
PAIR = (2, COLS, HEAD_DIM)
PIECE = (HALF, 2 * HEAD_DIM)


def dot(a, b, dims):
    return lax.dot_general(a, b, dims, preferred_element_type=F32)


def wide(a):
    return a.astype(F32)


def shift(a, axis, d):
    n = SIZES[axis]
    return lax.ppermute(a, (axis, "core"), [(2 * i + c, 2 * ((i + d * (1 - 2 * c)) % n) + c) for i in range(n) for c in range(2)])


def swap(a):
    return lax.ppermute(a, "core", [(0, 1), (1, 0)])


def keep_mask(off):
    i = lax.broadcasted_iota(jnp.int32, (HALF, HALF), 0)
    j = lax.broadcasted_iota(jnp.int32, (HALF, HALF), 1)
    return (i - j) <= off


def fetch(i, kv_refs, kv_buf):
    for a, ref in enumerate(kv_refs):

        @pl.when(i // QUAD == a)
        def _():
            kv_buf[...] = ref[0]

    return kv_buf[...]


def query_refs(refs):
    return [ref.at[0] for ref in refs]


def grad_refs(refs):
    return [ref.at[1] for ref in refs]


def forward_kernel(base, n, first, last, info, *refs):
    kv_refs, refs = refs[:n], refs[n:]
    q_refs, g_refs, refs = query_refs(refs[:2]), grad_refs(refs[:2]), refs[2:]
    if not first:
        stat_in, acc_in, refs = refs[0], refs[1:3], refs[3:]
    stat_ref, acc_refs, (s_ref, p_ref, kv_buf) = refs[0], refs[1:3], refs[3:]
    i = pl.program_id(0)
    core = info[CORE_AT]

    @pl.when(i == 0)
    def _():
        if first:
            stat_ref[:, 0:1, :] = jnp.full((2, 1, COLS), NEG, F32)
            stat_ref[:, 1:3, :] = jnp.zeros((2, 2, COLS), F32)
            for half in range(2):
                acc_refs[half][...] = jnp.zeros(ACC, F32)
        else:
            stat_ref[...] = stat_in[...]
            for half in range(2):
                acc_refs[half][...] = acc_in[half][...]

    def step(masked):
        kv = fetch(i, kv_refs, kv_buf)
        k = kv[:, :HEAD_DIM]
        vt = jnp.transpose(kv[:, HEAD_DIM:])
        for half in range(2):
            s_ref[:, pl.ds(half * COLS, COLS)] = dot(k, q_refs[half][...], NT)
        for half in range(2):
            acc = acc_refs[half]
            if masked:
                keep = keep_mask(jnp.where(i == 0, half * HALF * (1 - 2 * core), HALF))
            for h in range(GROUP):
                cols = pl.ds(h * HALF, HALF)
                flat = pl.ds(half * COLS + h * HALF, HALF)
                s = s_ref[:, flat]
                if masked:
                    s = jnp.where(keep, s, MASKED)
                m_old = stat_ref[half, 0:1, cols]
                m_new = jnp.maximum(m_old, jnp.max(s, axis=0, keepdims=True) * SCALE2)
                alpha = jnp.exp2(m_old - m_new)
                p = jnp.exp2(s * SCALE2 - m_new)
                stat_ref[half, 0:1, cols] = m_new
                stat_ref[half, 1:2, cols] = stat_ref[half, 1:2, cols] * alpha + jnp.sum(p, axis=0, keepdims=True)
                acc[:, cols] = acc[:, cols] * alpha
                p_ref[:, flat] = p.astype(BF)
            acc[...] += dot(vt, p_ref[:, pl.ds(half * COLS, COLS)], NN)

    pl.when(info[base + i] > 0)(lambda: step(first))

    if last:

        @pl.when(i == QUAD * n - 1)
        def _():
            eye = (
                lax.broadcasted_iota(jnp.int32, (HEAD_DIM, HEAD_DIM), 0)
                == lax.broadcasted_iota(jnp.int32, (HEAD_DIM, HEAD_DIM), 1)
            ).astype(F32).astype(BF)
            for half in range(2):
                turned = dot(eye, g_refs[half][...], NT)
                stat_ref[half, 2:3, :] = jnp.sum(turned * acc_refs[half][...], axis=0, keepdims=True)


def combine(mine, other, half):
    m0 = mine[half, 0:1, :]
    m1 = other[1 - half, 0:1, :]
    m = jnp.maximum(m0, m1)
    e0 = jnp.exp2(m0 - m)
    e1 = jnp.exp2(m1 - m)
    total = mine[half, 1:2, :] * e0 + other[1 - half, 1:2, :] * e1
    return m + jnp.log2(total), e0 / total, e1 / total


def backward_kernel(base, n, first, masks, info, *refs):
    kv_refs, refs = refs[:n], refs[n:]
    q_refs, g_refs, refs = query_refs(refs[:2]), grad_refs(refs[:2]), refs[2:]
    mine, other, refs = refs[0], refs[1], refs[2:]
    if not first:
        dq_in, refs = refs[:2], refs[2:]
    dq_refs, out_refs, refs = refs[:2], refs[2 : 2 + n], refs[2 + n :]
    row_ref, s_ref, dp_ref, p_ref, ds_ref, kv_buf, out_buf = refs
    i = pl.program_id(0)
    core = info[CORE_AT]

    @pl.when(i == 0)
    def _():
        for half in range(2):
            lse, w0, w1 = combine(mine, other, half)
            row_ref[half, 0:1, :] = lse
            row_ref[half, 1:2, :] = mine[half, 2:3, :] * w0 + other[1 - half, 2:3, :] * w1
            dq_refs[half][...] = jnp.zeros(ACC, F32) if first else dq_in[half][...]

    def step(masked):
        kv = fetch(i, kv_refs, kv_buf)
        k = kv[:, :HEAD_DIM]
        v = kv[:, HEAD_DIM:]
        kt = jnp.transpose(k)
        for half in range(2):
            cols = pl.ds(half * COLS, COLS)
            s_ref[:, cols] = dot(k, q_refs[half][...], NT)
            dp_ref[:, cols] = dot(v, g_refs[half][...], NT)
        for half in range(2):
            if masked:
                keep = keep_mask(jnp.where(i == 0, half * HALF * (1 - 2 * core), HALF))
            for h in range(GROUP):
                cols = pl.ds(h * HALF, HALF)
                flat = pl.ds(half * COLS + h * HALF, HALF)
                p = jnp.exp2(s_ref[:, flat] * SCALE2 - row_ref[half, 0:1, cols])
                if masked:
                    p = jnp.where(keep, p, 0.0)
                p_ref[:, flat] = p.astype(BF)
                ds_ref[:, flat] = (p * (dp_ref[:, flat] - row_ref[half, 1:2, cols])).astype(BF)
            dq_refs[half][...] += dot(kt, ds_ref[:, pl.ds(half * COLS, COLS)], NN)
        dk = jnp.zeros((HALF, HEAD_DIM), F32)
        dv = jnp.zeros((HALF, HEAD_DIM), F32)
        for half in range(2):
            cols = pl.ds(half * COLS, COLS)
            dk = dk + dot(ds_ref[:, cols], q_refs[half][...], NN)
            dv = dv + dot(p_ref[:, cols], g_refs[half][...], NN)
        out_buf[:, :HEAD_DIM] = dk.astype(BF)
        out_buf[:, HEAD_DIM:] = dv.astype(BF)

    live = info[base + i] > 0
    pl.when(live)(lambda: step(masks))

    @pl.when(jnp.logical_not(live))
    def _():
        out_buf[...] = jnp.zeros(PIECE, BF)

    for a, ref in enumerate(out_refs):

        @pl.when(i // QUAD == a)
        def _():
            ref[0] = out_buf[...]


def finish_kernel(mine, other, acc_mine, acc_other, dq_mine, dq_other, att_ref, dq_ref):
    lse, w0, w1 = combine(mine, other, 0)
    for h in range(GROUP):
        cols = slice(h * HALF, (h + 1) * HALF)
        rows = slice(h * HEAD_DIM, (h + 1) * HEAD_DIM)
        out = acc_mine[:, cols] * w0[:, cols] + acc_other[:, cols] * w1[:, cols]
        att_ref[:, rows] = jnp.transpose(out).astype(BF)
        dq_ref[:, rows] = jnp.transpose((dq_mine[:, cols] + dq_other[:, cols]) * SCALE).astype(BF)


def whole(shape):
    return pl.BlockSpec(shape, lambda i, info: (0,) * len(shape))


def piece_specs(n):
    def spec(a):
        return pl.BlockSpec((1,) + PIECE, lambda i, info: (jnp.clip(i - QUAD * a, 0, QUAD - 1), 0, 0))

    return [spec(a) for a in range(n)]


def cost(flops):
    return pl.CostEstimate(flops=flops, bytes_accessed=1 << 16, transcendentals=0)


def forward(base, info, kvs, qg, state, last):
    n = len(kvs)
    first = state is None
    ins = list(kvs) + list(qg) + ([] if first else list(state))
    specs = piece_specs(n) + [whole(PAIR)] * 2
    if not first:
        specs += [whole(STAT), whole(ACC), whole(ACC)]
    return pl.pallas_call(
        functools.partial(forward_kernel, base, n, first, last),
        grid_spec=pltpu.PrefetchScalarGridSpec(
            num_scalar_prefetch=1,
            grid=(QUAD * n,),
            in_specs=specs,
            out_specs=[whole(STAT), whole(ACC), whole(ACC)],
            scratch_shapes=[
                pltpu.VMEM((HALF, 2 * COLS), F32),
                pltpu.VMEM((HALF, 2 * COLS), BF),
                pltpu.VMEM(PIECE, BF),
            ],
        ),
        out_shape=[jax.ShapeDtypeStruct(s, F32) for s in (STAT, ACC, ACC)],
        compiler_params=pltpu.CompilerParams(vmem_limit_bytes=VMEM_LIMIT),
        cost_estimate=cost(200_000_000),
        name="forward",
    )(info, *ins)


def backward(base, info, kvs, qg, mine, other, dq):
    n = len(kvs)
    first = dq is None
    ins = list(kvs) + list(qg) + [mine, other] + ([] if first else list(dq))
    specs = piece_specs(n) + [whole(PAIR)] * 2 + [whole(STAT)] * 2
    if not first:
        specs += [whole(ACC), whole(ACC)]
    wide_shape = (HALF, 2 * COLS)
    res = pl.pallas_call(
        functools.partial(backward_kernel, base, n, first, base == 0),
        grid_spec=pltpu.PrefetchScalarGridSpec(
            num_scalar_prefetch=1,
            grid=(QUAD * n,),
            in_specs=specs,
            out_specs=[whole(ACC), whole(ACC)] + piece_specs(n),
            scratch_shapes=[
                pltpu.VMEM((2, 2, COLS), F32),
                pltpu.VMEM(wide_shape, F32),
                pltpu.VMEM(wide_shape, F32),
                pltpu.VMEM(wide_shape, BF),
                pltpu.VMEM(wide_shape, BF),
                pltpu.VMEM(PIECE, BF),
                pltpu.VMEM(PIECE, BF),
            ],
        ),
        out_shape=[jax.ShapeDtypeStruct(ACC, F32)] * 2 + [jax.ShapeDtypeStruct(a.shape, BF) for a in kvs],
        compiler_params=pltpu.CompilerParams(vmem_limit_bytes=VMEM_LIMIT),
        cost_estimate=cost(200_000_000),
        name="backward",
    )(info, *ins)
    return res[:2], res[2:]


def finish(mine, other, acc_mine, acc_other, dq_mine, dq_other):
    shape = jax.ShapeDtypeStruct((HALF, GROUP * HEAD_DIM), BF)
    return pl.pallas_call(
        finish_kernel,
        in_specs=[VMEM] * 6,
        out_specs=[VMEM] * 2,
        out_shape=[shape, shape],
        compiler_params=SMALL,
        cost_estimate=pl.CostEstimate(flops=1 << 20, bytes_accessed=1 << 16, transcendentals=0),
        name="finish",
    )(mine, other, acc_mine, acc_other, dq_mine, dq_other)


VMEM = pl.BlockSpec(memory_space=pltpu.VMEM)
SMALL = pltpu.CompilerParams(vmem_limit_bytes=8 * 1024 * 1024)


def join_kernel(k_ref, v_ref, out_ref):
    out_ref[:, :HEAD_DIM] = k_ref[...]
    out_ref[:, HEAD_DIM:] = v_ref[...]


def join(k, v):
    return pl.pallas_call(join_kernel, out_shape=jax.ShapeDtypeStruct(PIECE, BF), in_specs=[VMEM] * 2, out_specs=VMEM, compiler_params=SMALL, name="join")(k, v)


def prepare_kernel(query, grad_out, gate, after, qg_ref, gate_ref):
    for h in range(GROUP):
        rows = slice(h * HALF, (h + 1) * HALF)
        cols = slice(h * HEAD_DIM, (h + 1) * HEAD_DIM)
        qg_ref[0, rows, :] = query[:, cols]
        qg_ref[1, rows, :] = grad_out[:, cols]
    gate_ref[...] = gate[...]


def prepare(query, grad_out, gate, after):
    return pl.pallas_call(
        prepare_kernel,
        in_specs=[VMEM] * 3 + [pl.BlockSpec(memory_space=pl.ANY)],
        out_specs=[VMEM] * 2,
        out_shape=[jax.ShapeDtypeStruct(PAIR, BF), jax.ShapeDtypeStruct(gate.shape, jnp.int32)],
        cost_estimate=cost(100_000_000),
        compiler_params=SMALL, name="prepare",
    )(query, grad_out, gate, after)


def stack_kernel(*refs):
    for i in range(QUAD):
        refs[-1][i] = refs[i][...]


def stack(*pieces):
    return pl.pallas_call(stack_kernel, out_shape=jax.ShapeDtypeStruct((QUAD,) + PIECE, BF), in_specs=[VMEM] * QUAD, out_specs=VMEM, compiler_params=SMALL, name="stack")(*pieces)


def sum_high_kernel(own, one, three, keep, near_up, near_down, far):
    def total(i):
        return wide(own[i]) + wide(one[i]) + wide(three[i])

    keep[...] = total(0)
    near_down[...] = total(1).astype(BF)
    near_up[...] = total(2).astype(BF)
    far[...] = total(3).astype(BF)


def sum_high(own, one, three):
    shape = jax.ShapeDtypeStruct(PIECE, BF)
    return pl.pallas_call(
        sum_high_kernel,
        in_specs=[VMEM] * 3,
        out_specs=[VMEM] * 4,
        out_shape=[jax.ShapeDtypeStruct(PIECE, F32), shape, shape, shape],
        cost_estimate=cost(100_000_000),
        compiler_params=SMALL, name="sum_high",
    )(own, one, three)


def sum_low_kernel(own, one, three, keep, down, far, up, own_out, near_down, near_up, two_down, two_up):
    def total(i):
        return wide(own[i]) + wide(one[i]) + wide(three[i])

    own_out[...] = total(0)
    near_down[...] = total(1).astype(BF)
    near_up[...] = total(2).astype(BF)
    two_down[...] = (total(3) + wide(down[...]) + wide(far[...])).astype(BF)
    two_up[...] = (keep[...] + wide(up[...])).astype(BF)


def sum_low(own, one, three, keep, down, far, up):
    shape = jax.ShapeDtypeStruct(PIECE, BF)
    return pl.pallas_call(
        sum_low_kernel,
        in_specs=[VMEM] * 7,
        out_specs=[VMEM] * 5,
        out_shape=[jax.ShapeDtypeStruct(PIECE, F32), shape, shape, shape, shape],
        cost_estimate=cost(100_000_000),
        compiler_params=SMALL, name="sum_low",
    )(own, one, three, keep, down, far, up)


def close_kernel(own, a, b, c, d, dk_ref, dv_ref):
    total = own[...] + wide(a[...]) + wide(b[...]) + wide(c[...]) + wide(d[...])
    dk_ref[...] = (total[:, :HEAD_DIM] * SCALE).astype(BF)
    dv_ref[...] = total[:, HEAD_DIM:].astype(BF)


def close(own, parts):
    shape = jax.ShapeDtypeStruct((HALF, HEAD_DIM), BF)
    return pl.pallas_call(
        close_kernel, out_shape=[shape, shape], in_specs=[VMEM] * 5, out_specs=[VMEM] * 2, compiler_params=SMALL, name="close"
    )(own, *parts)


def plan(gate):
    z = lax.axis_index("z")
    x = lax.axis_index("x")
    own = z * 4 + x
    totals = gate + lax.ppermute(gate, "head", [(0, 1), (1, 0), (2, 3), (3, 2)])
    totals = totals + lax.ppermute(totals, "head", [(0, 2), (2, 0), (1, 3), (3, 1)])
    row = lax.dynamic_slice_in_dim(totals, own, 1, 0)[0]
    columns = jnp.arange(NBLK, dtype=jnp.int32)
    ranked = jnp.where(columns < own, row * NBLK + columns, -1)
    rank = jnp.sum((ranked[None, :] > ranked[:, None]).astype(jnp.int32), axis=1)
    used = ((rank < TOPK) & (ranked >= 0)) | (columns == own)
    core = lax.axis_index("core")
    way = 1 - 2 * core
    dz = (way * (z - columns // 4)) % 8
    dx = (way * (x - columns % 4)) % 4
    pos = jnp.where(dz == 0, 0, jnp.where(dz <= 4, 2 * dz - 1, 2 * (8 - dz)))
    place = dx * 8 + pos
    live = jnp.sum((place[None, :] == columns[:, None]) & used[None, :], axis=1, dtype=jnp.int32)
    return jnp.concatenate([live, core[None]])


def on_device(query, key, value, grad_out, gate_score):
    piece = join(key, value)
    a1, b1 = shift(piece, "z", 1), shift(piece, "z", -1)
    a2, b2 = shift(piece, "z", 2), shift(piece, "z", -2)
    a3, b3, a4 = shift(a2, "z", 1), shift(b2, "z", -1), shift(a2, "z", 2)
    low0 = stack(piece, a1, b1, a2)
    high0 = stack(b2, a3, b3, a4)
    low1, high1 = shift(low0, "x", 1), shift(high0, "x", 1)
    low2, high2 = shift(low1, "x", 1), shift(high1, "x", 1)
    low3, high3 = shift(low0, "x", -1), shift(high0, "x", -1)

    qg, gate = prepare(query, grad_out, gate_score[0], a3)
    info = plan(gate)
    qg = (qg, swap(qg))

    state = forward(0, info, [low0, high0], qg, None, False)
    state = forward(8, info, [low1, high1], qg, state, False)
    state = forward(24, info, [low3, high3], qg, state, False)
    mine, acc, acc_away = forward(16, info, [low2, high2], qg, state, True)
    other = swap(mine)
    acc_other = swap(acc_away)

    dq, (low2, high2) = backward(16, info, [low2, high2], qg, mine, other, None)
    high2, low2 = shift(high2, "x", -1), shift(low2, "x", -1)
    dq, (low3, high3) = backward(24, info, [low3, high3], qg, mine, other, dq)
    high3, low3 = shift(high3, "x", 1), shift(low3, "x", 1)
    dq, (low1, high1) = backward(8, info, [low1, high1], qg, mine, other, dq)
    high1 = shift((wide(high1) + wide(high2)).astype(BF), "x", -1)
    low1 = shift((wide(low1) + wide(low2)).astype(BF), "x", -1)
    dq, (low0, high0) = backward(0, info, [low0, high0], qg, mine, other, dq)

    keep, up, down, far = sum_high(high0, high1, high3)
    down, far, up = shift(down, "z", -1), shift(far, "z", -2), shift(up, "z", 1)
    own, near_down, near_up, two_down, two_up = sum_low(low0, low1, low3, keep, down, far, up)
    parts = [
        shift(two_up, "z", 2),
        shift(two_down, "z", -2),
        shift(near_down, "z", -1),
        shift(near_up, "z", 1),
    ]
    grad_key, grad_value = close(own, parts)
    attended, grad_query = finish(mine, other, acc, acc_other, dq[0], swap(dq[1]))
    return (attended, grad_query, grad_key, grad_value)


def solution(mesh):
    devices = mesh.devices.reshape(8, 4, 2, 4)
    split = Mesh(devices, ("z", "x", "core", "head"))
    spec = P(("z", "x", "core"), "head")
    return jax.shard_map(
        on_device,
        mesh=split,
        in_specs=(spec, spec, spec, spec, P("head", None, None)),
        out_specs=(spec, spec, spec, spec),
        check_vma=False,
    )
```

profile of v0, /device:TPU:1, one launch (start us, length us, event | category | flops | bytes accessed | tf_op | source)
XLA Modules:
  0.0 132.6 jit_solution(700009389799880000)
XLA Ops:
  0.6 0.8 copy-done.2
  1.5 0.8 copy-done.3
  2.3 3.9 %collective-permute-start.8 = (bf16[256,256]{1,0:T(8,128)(2,1)S(1)}, bf16[256,256]{1,0:T(8,128)(2,1)S(1)}, u32[]{:S(2)}, u32[]{:S(2)}) collective-permute-start(bf16[256,256]{1,0:T(8,128)(2,1)S(1)} %join.1.refs_0_), channel_id=1, source_target_pairs={{0,192},{4,68},{32,224},{36,100},{64,0},{68,132},{96,32},{100,164}... | collective-permute-start | bytes 393224 | tf_op jit(solution)/shard_map/ppermute | solution.py:46
  6.2 3.1 %collective-permute-start = (bf16[256,256]{1,0:T(8,128)(2,1)S(1)}, bf16[256,256]{1,0:T(8,128)(2,1)S(1)}, u32[]{:S(2)}, u32[]{:S(2)}) collective-permute-start(bf16[256,256]{1,0:T(8,128)(2,1)S(1)} %join.1.refs_0_), channel_id=1, source_target_pairs={{0,64},{4,196},{32,96},{36,228},{64,128},{68,4},{96,160},{100,36},... | collective-permute-start | bytes 393224 | tf_op jit(solution)/shard_map/ppermute | solution.py:46
  9.4 0.7 collective-permute-start.5
  10.1 1.9 %collective-permute-start.4 = (bf16[256,256]{1,0:T(8,128)(2,1)S(1)}, bf16[256,256]{1,0:T(8,128)(2,1)S(1)}, u32[]{:S(2)}, u32[]{:S(2)}) collective-permute-start(bf16[256,256]{1,0:T(8,128)(2,1)S(1)} %join.1.refs_0_), channel_id=1, source_target_pairs={{0,32},{4,228},{32,64},{36,4},{64,96},{68,36},{96,128},{100,68},{1... | collective-permute-start | bytes 393224 | tf_op jit(solution)/shard_map/ppermute | solution.py:46
  12.0 1.8 %collective-permute-start.9 = (bf16[256,256]{1,0:T(8,128)(2,1)S(1)}, bf16[256,256]{1,0:T(8,128)(2,1)S(1)}, u32[]{:S(2)}, u32[]{:S(2)}) collective-permute-start(bf16[256,256]{1,0:T(8,128)(2,1)S(1)} %collective-permute-done.8.refs_0_), channel_id=1, source_target_pairs={{0,224},{4,36},{32,0},{36,68},{64,32},{68,100},{96,64},{100,132},{... | collective-permute-start | bytes 393224 | tf_op jit(solution)/shard_map/ppermute | solution.py:46
  13.9 1.9 %collective-permute-done.refs_3_ = bf16[256,256]{1,0:T(8,128)(2,1)S(1)} collective-permute-done((bf16[256,256]{1,0:T(8,128)(2,1)S(1)}, bf16[256,256]{1,0:T(8,128)(2,1)S(1)}, u32[]{:S(2)}, u32[]{:S(2)}) %collective-permute-start) | collective-permute-done | bytes 131104 | tf_op jit(solution)/shard_map/ppermute | solution.py:46
  15.8 0.8 collective-permute-start.10
  16.6 3.7 %collective-permute-start.1 = (bf16[256,256]{1,0:T(8,128)(2,1)S(1)}, bf16[256,256]{1,0:T(8,128)(2,1)S(1)}, u32[]{:S(2)}, u32[]{:S(2)}) collective-permute-start(bf16[256,256]{1,0:T(8,128)(2,1)S(1)} %collective-permute-done.refs_3_), channel_id=1, source_target_pairs={{0,32},{4,228},{32,64},{36,4},{64,96},{68,36},{96,128},{100,68},{1... | collective-permute-start | bytes 393224 | tf_op jit(solution)/shard_map/ppermute | solution.py:46
  20.5 1.7 %collective-permute-start.6 = (bf16[4,256,256]{2,1,0:T(8,128)(2,1)S(1)}, bf16[4,256,256]{2,1,0:T(8,128)(2,1)S(1)}, u32[]{:S(2)}, u32[]{:S(2)}) collective-permute-start(bf16[4,256,256]{2,1,0:T(8,128)(2,1)S(1)} %stack.2.refs_0_), channel_id=1, source_target_pairs={{0,8},{4,28},{8,16},{12,4},{16,24},{20,12},{24,0},{28,20},{1,9},{5... | collective-permute-start | bytes 1572872 | tf_op jit(solution)/shard_map/ppermute | solution.py:46
  22.1 0.9 collective-permute-done.10.refs_3_
  23.1 2.1 %collective-permute-done.1.after.refs_1_ = bf16[256,256]{1,0:T(8,128)(2,1)S(1)} collective-permute-done((bf16[256,256]{1,0:T(8,128)(2,1)S(1)}, bf16[256,256]{1,0:T(8,128)(2,1)S(1)}, u32[]{:S(2)}, u32[]{:S(2)}) %collective-permute-start.1) | collective-permute-done | bytes 131104 | tf_op jit(solution)/shard_map/ppermute | solution.py:46
  25.2 2.4 %collective-permute-start.11 = (bf16[4,256,256]{2,1,0:T(8,128)(2,1)S(1)}, bf16[4,256,256]{2,1,0:T(8,128)(2,1)S(1)}, u32[]{:S(2)}, u32[]{:S(2)}) collective-permute-start(bf16[4,256,256]{2,1,0:T(8,128)(2,1)S(1)} %stack.3.refs_1_), channel_id=1, source_target_pairs={{0,8},{4,28},{8,16},{12,4},{16,24},{20,12},{24,0},{28,20},{1,9},{5... | collective-permute-start | bytes 1572872 | tf_op jit(solution)/shard_map/ppermute | solution.py:46
  27.6 0.1 prepare.1
  27.7 1.4 %collective-permute-start.2 = (s32[32,32]{1,0:T(8,128)S(1)}, s32[32,32]{1,0:T(8,128)S(1)}, u32[]{:S(2)}, u32[]{:S(2)}) collective-permute-start(s32[32,32]{1,0:T(8,128)S(1)} %get-tuple-element.47), channel_id=1, source_target_pairs={{0,1},{1,0},{2,3},{3,2},{4,5},{5,4},{6,7},{7,6},{8,9},{9,8},{10,11... | collective-permute-start | bytes 12296 | tf_op jit(solution)/shard_map/ppermute | solution.py:414
  29.1 1.6 %collective-permute-done.2 = s32[32,32]{1,0:T(8,128)S(1)} collective-permute-done((s32[32,32]{1,0:T(8,128)S(1)}, s32[32,32]{1,0:T(8,128)S(1)}, u32[]{:S(2)}, u32[]{:S(2)}) %collective-permute-start.2) | collective-permute-done | bytes 4128 | tf_op jit(solution)/shard_map/ppermute | solution.py:414
  30.7 2.9 %collective-permute-start.3 = (s32[32,32]{1,0:T(8,128)S(1)}, s32[32,32]{1,0:T(8,128)S(1)}, u32[]{:S(2)}, u32[]{:S(2)}) collective-permute-start(s32[32,32]{1,0:T(8,128)S(1)} %add.77), channel_id=1, source_target_pairs={{0,2},{2,0},{1,3},{3,1},{4,6},{6,4},{5,7},{7,5},{8,10},{10,8},{9,1... | collective-permute-start | bytes 12296 | tf_op jit(solution)/shard_map/ppermute | solution.py:415
  33.6 0.1 collective-permute-start.14
  33.7 0.2 collective-permute-start.15
  33.9 0.9 collective-permute-done.3
  34.8 5.3 %collective-permute-start.13 = (bf16[2,1024,128]{2,1,0:T(8,128)(2,1)S(1)}, bf16[2,1024,128]{2,1,0:T(8,128)(2,1)S(1)}, u32[]{:S(2)}, u32[]{:S(2)}) collective-permute-start(bf16[2,1024,128]{2,1,0:T(8,128)(2,1)S(1)} %get-tuple-element.48.refs_2_), channel_id=1, source_target_pairs={{0,4},{4,0},{1,5},{5,1},{2,6},{6,2},{3,7},{7,3},{8,12},{12,8},{9,1... | collective-permute-start | bytes 1572872 | tf_op jit(solution)/shard_map/ppermute | solution.py:50
  40.1 0.7 collective-permute-start.7
  40.7 0.8 collective-permute-start.12
  41.6 0.2 convert_reduce_fusion.1
  41.8 0.1 convert_reduce_fusion
  42.0 2.0 %forward.4 = (f32[2,3,1024]{2,1,0:T(4,128)S(1)}, f32[128,1024]{1,0:T(8,128)S(1)}, f32[128,1024]{1,0:T(8,128)S(1)}) custom-call(s32[33]{0:T(128)S(1)} %pad_add_fusion.info, bf16[4,256,256]{2,1,0:T(8,128)(2,1)S(1)} %stack.2.refs_0_, bf16[4,256,256]{2,1,0:T(8,128)(2,1)S(1)} %stack.3.refs_1_, bf16[2,1024,128]{2,1,0:T(8,128)(2,1)S(1)} %get-tuple-element.48.refs_2_, ...), custom_call_target="tpu_custom_call" | custom-call | flops 200000000 | bytes 65536 | tf_op jit(solution)/shard_map/forward/pallas_call | solution.py:244
  43.9 0.8 forward.5
  44.8 10.0 %collective-permute-done.15.refs_1_ = bf16[4,256,256]{2,1,0:T(8,128)(2,1)S(1)} collective-permute-done((bf16[4,256,256]{2,1,0:T(8,128)(2,1)S(1)}, bf16[4,256,256]{2,1,0:T(8,128)(2,1)S(1)}, u32[]{:S(2)}, u32[]{:S(2)}) %collective-permute-start.15) | collective-permute-done | bytes 524320 | tf_op jit(solution)/shard_map/ppermute | solution.py:46
  54.8 0.8 forward.6
  55.7 6.4 %collective-permute-done.12.refs_1_ = bf16[4,256,256]{2,1,0:T(8,128)(2,1)S(1)} collective-permute-done((bf16[4,256,256]{2,1,0:T(8,128)(2,1)S(1)}, bf16[4,256,256]{2,1,0:T(8,128)(2,1)S(1)}, u32[]{:S(2)}, u32[]{:S(2)}) %collective-permute-start.12) | collective-permute-done | bytes 524320 | tf_op jit(solution)/shard_map/ppermute | solution.py:46
  62.1 1.2 forward.7
  63.3 0.1 collective-permute-start.16
  63.4 1.2 collective-permute-done.16.refs_5_.other
  64.6 1.1 backward.4
  65.6 1.3 collective-permute-start.22
  66.9 3.6 %collective-permute-start.19 = (bf16[4,256,256]{2,1,0:T(8,128)(2,1)S(1)}, bf16[4,256,256]{2,1,0:T(8,128)(2,1)S(1)}, u32[]{:S(2)}, u32[]{:S(2)}) collective-permute-start(bf16[4,256,256]{2,1,0:T(8,128)(2,1)S(1)} %get-tuple-element.73), channel_id=1, source_target_pairs={{0,24},{4,12},{8,0},{12,20},{16,8},{20,28},{24,16},{28,4},{1,25},{... | collective-permute-start | bytes 1572872 | tf_op jit(solution)/shard_map/ppermute | solution.py:46
  70.5 1.1 backward.5
  71.6 2.7 %collective-permute-start.21 = (bf16[4,256,256]{2,1,0:T(8,128)(2,1)S(1)}, bf16[4,256,256]{2,1,0:T(8,128)(2,1)S(1)}, u32[]{:S(2)}, u32[]{:S(2)}) collective-permute-start(bf16[4,256,256]{2,1,0:T(8,128)(2,1)S(1)} %get-tuple-element.74), channel_id=1, source_target_pairs={{0,8},{4,28},{8,16},{12,4},{16,24},{20,12},{24,0},{28,20},{1,9},{5... | collective-permute-start | bytes 1572872 | tf_op jit(solution)/shard_map/ppermute | solution.py:46
  74.2 1.5 %collective-permute-start.24 = (bf16[4,256,256]{2,1,0:T(8,128)(2,1)S(1)}, bf16[4,256,256]{2,1,0:T(8,128)(2,1)S(1)}, u32[]{:S(2)}, u32[]{:S(2)}) collective-permute-start(bf16[4,256,256]{2,1,0:T(8,128)(2,1)S(1)} %get-tuple-element.78), channel_id=1, source_target_pairs={{0,8},{4,28},{8,16},{12,4},{16,24},{20,12},{24,0},{28,20},{1,9},{5... | collective-permute-start | bytes 1572872 | tf_op jit(solution)/shard_map/ppermute | solution.py:46
  75.7 1.1 backward.6
  76.8 2.1 %collective-permute-done.22 = bf16[4,256,256]{2,1,0:T(8,128)(2,1)S(1)} collective-permute-done((bf16[4,256,256]{2,1,0:T(8,128)(2,1)S(1)}, bf16[4,256,256]{2,1,0:T(8,128)(2,1)S(1)}, u32[]{:S(2)}, u32[]{:S(2)}) %collective-permute-start.22) | collective-permute-done | bytes 524320 | tf_op jit(solution)/shard_map/ppermute | solution.py:46
  78.8 0.1 add_convert_fusion
  79.1 11.0 %collective-permute-done.19 = bf16[4,256,256]{2,1,0:T(8,128)(2,1)S(1)} collective-permute-done((bf16[4,256,256]{2,1,0:T(8,128)(2,1)S(1)}, bf16[4,256,256]{2,1,0:T(8,128)(2,1)S(1)}, u32[]{:S(2)}, u32[]{:S(2)}) %collective-permute-start.19) | collective-permute-done | bytes 524320 | tf_op jit(solution)/shard_map/ppermute | solution.py:46
  90.1 0.1 add_convert_fusion.1
  90.2 0.1 collective-permute-start.20
  90.3 7.1 %collective-permute-start.17 = (f32[128,1024]{1,0:T(8,128)S(1)}, f32[128,1024]{1,0:T(8,128)S(1)}, u32[]{:S(2)}, u32[]{:S(2)}) collective-permute-start(f32[128,1024]{1,0:T(8,128)S(1)} %get-tuple-element.60), channel_id=1, source_target_pairs={{0,4},{4,0},{1,5},{5,1},{2,6},{6,2},{3,7},{7,3},{8,12},{12,8},{9,1... | collective-permute-start | bytes 1572872 | tf_op jit(solution)/shard_map/ppermute | solution.py:50
  97.4 2.7 %backward.7 = (f32[128,1024]{1,0:T(8,128)S(1)}, f32[128,1024]{1,0:T(8,128)S(1)}, bf16[4,256,256]{2,1,0:T(8,128)(2,1)S(1)}, bf16[4,256,256]{2,1,0:T(8,128)(2,1)S(1)}) custom-call(s32[33]{0:T(128)S(1)} %pad_add_fusion.info, bf16[4,256,256]{2,1,0:T(8,128)(2,1)S(1)} %stack.2.refs_0_, bf16[4,256,256]{2,1,0:T(8,128)(2,1)S(1)} %stack.3.refs_1_, ...), custom_call_target="tpu_custom_call" | custom-call | flops 200000000 | bytes 65536 | tf_op jit(solution)/shard_map/backward/pallas_call | solution.py:272
  100.2 0.4 collective-permute-start.18
  100.6 0.2 sum_high.1
  100.8 4.2 %collective-permute-start.25 = (bf16[256,256]{1,0:T(8,128)(2,1)S(1)}, bf16[256,256]{1,0:T(8,128)(2,1)S(1)}, u32[]{:S(2)}, u32[]{:S(2)}) collective-permute-start(bf16[256,256]{1,0:T(8,128)(2,1)S(1)} %get-tuple-element.80), channel_id=1, source_target_pairs={{0,224},{4,36},{32,0},{36,68},{64,32},{68,100},{96,64},{100,132},{... | collective-permute-start | bytes 393224 | tf_op jit(solution)/shard_map/ppermute | solution.py:46
  105.0 4.6 %collective-permute-start.26 = (bf16[256,256]{1,0:T(8,128)(2,1)S(1)}, bf16[256,256]{1,0:T(8,128)(2,1)S(1)}, u32[]{:S(2)}, u32[]{:S(2)}) collective-permute-start(bf16[256,256]{1,0:T(8,128)(2,1)S(1)} %get-tuple-element.81), channel_id=1, source_target_pairs={{0,192},{4,68},{32,224},{36,100},{64,0},{68,132},{96,32},{100,164}... | collective-permute-start | bytes 393224 | tf_op jit(solution)/shard_map/ppermute | solution.py:46
  109.6 4.4 %collective-permute-start.27 = (bf16[256,256]{1,0:T(8,128)(2,1)S(1)}, bf16[256,256]{1,0:T(8,128)(2,1)S(1)}, u32[]{:S(2)}, u32[]{:S(2)}) collective-permute-start(bf16[256,256]{1,0:T(8,128)(2,1)S(1)} %get-tuple-element.82), channel_id=1, source_target_pairs={{0,32},{4,228},{32,64},{36,4},{64,96},{68,36},{96,128},{100,68},{1... | collective-permute-start | bytes 393224 | tf_op jit(solution)/shard_map/ppermute | solution.py:46
  114.0 0.3 collective-permute-done.25.down
  114.3 4.8 %collective-permute-done.26.far = bf16[256,256]{1,0:T(8,128)(2,1)S(1)} collective-permute-done((bf16[256,256]{1,0:T(8,128)(2,1)S(1)}, bf16[256,256]{1,0:T(8,128)(2,1)S(1)}, u32[]{:S(2)}, u32[]{:S(2)}) %collective-permute-start.26) | collective-permute-done | bytes 131104 | tf_op jit(solution)/shard_map/ppermute | solution.py:46
  119.1 0.2 sum_low.1
  119.4 1.4 %collective-permute-start.28 = (bf16[256,256]{1,0:T(8,128)(2,1)S(1)}, bf16[256,256]{1,0:T(8,128)(2,1)S(1)}, u32[]{:S(2)}, u32[]{:S(2)}) collective-permute-start(bf16[256,256]{1,0:T(8,128)(2,1)S(1)} %get-tuple-element.84), channel_id=1, source_target_pairs={{0,64},{4,196},{32,96},{36,228},{64,128},{68,4},{96,160},{100,36},... | collective-permute-start | bytes 393224 | tf_op jit(solution)/shard_map/ppermute | solution.py:46
  120.8 1.0 collective-permute-start.29
  121.8 1.1 collective-permute-start.30
  122.9 2.4 %collective-permute-start.31 = (bf16[256,256]{1,0:T(8,128)(2,1)S(1)}, bf16[256,256]{1,0:T(8,128)(2,1)S(1)}, u32[]{:S(2)}, u32[]{:S(2)}) collective-permute-start(bf16[256,256]{1,0:T(8,128)(2,1)S(1)} %get-tuple-element.87), channel_id=1, source_target_pairs={{0,32},{4,228},{32,64},{36,4},{64,96},{68,36},{96,128},{100,68},{1... | collective-permute-start | bytes 393224 | tf_op jit(solution)/shard_map/ppermute | solution.py:46
  125.3 1.0 finish.1
  126.3 4.4 %collective-permute-done.29.b = bf16[256,256]{1,0:T(8,128)(2,1)S(1)} collective-permute-done((bf16[256,256]{1,0:T(8,128)(2,1)S(1)}, bf16[256,256]{1,0:T(8,128)(2,1)S(1)}, u32[]{:S(2)}, u32[]{:S(2)}) %collective-permute-start.29) | collective-permute-done | bytes 131104 | tf_op jit(solution)/shard_map/ppermute | solution.py:46
  130.7 1.1 collective-permute-done.30.c
  131.9 0.7 close.1
  (36 shorter events, 0.4 us)
Async XLA Ops:
  0.6 0.8 copy-start.2
  1.5 0.8 copy-start.3
  2.3 9.7 %collective-permute-start.8 = (bf16[256,256]{1,0:T(8,128)(2,1)S(1)}, bf16[256,256]{1,0:T(8,128)(2,1)S(1)}, u32[]{:S(2)}, u32[]{:S(2)}) collective-permute-start(bf16[256,256]{1,0:T(8,128)(2,1)S(1)} %join.1.refs_0_), channel_id=1, source_target_pairs={{0,192},{4,68},{32,224},{36,100},{64,0},{68,132},{96,32},{100,164}... | collective-permute-start | bytes 393224 | tf_op jit(solution)/shard_map/ppermute | solution.py:46
  6.2 9.6 %collective-permute-start = (bf16[256,256]{1,0:T(8,128)(2,1)S(1)}, bf16[256,256]{1,0:T(8,128)(2,1)S(1)}, u32[]{:S(2)}, u32[]{:S(2)}) collective-permute-start(bf16[256,256]{1,0:T(8,128)(2,1)S(1)} %join.1.refs_0_), channel_id=1, source_target_pairs={{0,64},{4,196},{32,96},{36,228},{64,128},{68,4},{96,160},{100,36},... | collective-permute-start | bytes 393224 | tf_op jit(solution)/shard_map/ppermute | solution.py:46
  9.4 11.0 %collective-permute-start.5 = (bf16[256,256]{1,0:T(8,128)(2,1)S(1)}, bf16[256,256]{1,0:T(8,128)(2,1)S(1)}, u32[]{:S(2)}, u32[]{:S(2)}) collective-permute-start(bf16[256,256]{1,0:T(8,128)(2,1)S(1)} %join.1.refs_0_), channel_id=1, source_target_pairs={{0,224},{4,36},{32,0},{36,68},{64,32},{68,100},{96,64},{100,132},{... | collective-permute-start | bytes 393224 | tf_op jit(solution)/shard_map/ppermute | solution.py:46
  10.1 10.3 %collective-permute-start.4 = (bf16[256,256]{1,0:T(8,128)(2,1)S(1)}, bf16[256,256]{1,0:T(8,128)(2,1)S(1)}, u32[]{:S(2)}, u32[]{:S(2)}) collective-permute-start(bf16[256,256]{1,0:T(8,128)(2,1)S(1)} %join.1.refs_0_), channel_id=1, source_target_pairs={{0,32},{4,228},{32,64},{36,4},{64,96},{68,36},{96,128},{100,68},{1... | collective-permute-start | bytes 393224 | tf_op jit(solution)/shard_map/ppermute | solution.py:46
  12.0 10.1 %collective-permute-start.9 = (bf16[256,256]{1,0:T(8,128)(2,1)S(1)}, bf16[256,256]{1,0:T(8,128)(2,1)S(1)}, u32[]{:S(2)}, u32[]{:S(2)}) collective-permute-start(bf16[256,256]{1,0:T(8,128)(2,1)S(1)} %collective-permute-done.8.refs_0_), channel_id=1, source_target_pairs={{0,224},{4,36},{32,0},{36,68},{64,32},{68,100},{96,64},{100,132},{... | collective-permute-start | bytes 393224 | tf_op jit(solution)/shard_map/ppermute | solution.py:46
  15.8 7.3 %collective-permute-start.10 = (bf16[256,256]{1,0:T(8,128)(2,1)S(1)}, bf16[256,256]{1,0:T(8,128)(2,1)S(1)}, u32[]{:S(2)}, u32[]{:S(2)}) collective-permute-start(bf16[256,256]{1,0:T(8,128)(2,1)S(1)} %collective-permute-done.refs_3_), channel_id=1, source_target_pairs={{0,64},{4,196},{32,96},{36,228},{64,128},{68,4},{96,160},{100,36},... | collective-permute-start | bytes 393224 | tf_op jit(solution)/shard_map/ppermute | solution.py:46
  16.6 8.5 %collective-permute-start.1 = (bf16[256,256]{1,0:T(8,128)(2,1)S(1)}, bf16[256,256]{1,0:T(8,128)(2,1)S(1)}, u32[]{:S(2)}, u32[]{:S(2)}) collective-permute-start(bf16[256,256]{1,0:T(8,128)(2,1)S(1)} %collective-permute-done.refs_3_), channel_id=1, source_target_pairs={{0,32},{4,228},{32,64},{36,4},{64,96},{68,36},{96,128},{100,68},{1... | collective-permute-start | bytes 393224 | tf_op jit(solution)/shard_map/ppermute | solution.py:46
  20.4 7.2 %copy-start = (bf16[256,512]{1,0:T(8,128)(2,1)S(1)}, bf16[256,512]{1,0:T(8,128)(2,1)}, u32[]{:S(2)}) copy-start(bf16[256,512]{1,0:T(8,128)(2,1)} %query.1) | copy-start | bytes 786436
  20.4 7.2 %copy-start.1 = (bf16[256,512]{1,0:T(8,128)(2,1)S(1)}, bf16[256,512]{1,0:T(8,128)(2,1)}, u32[]{:S(2)}) copy-start(bf16[256,512]{1,0:T(8,128)(2,1)} %grad_out.1) | copy-start | bytes 786436
  20.4 7.1 %copy-start.4 = (s32[1,32,32]{2,1,0:T(8,128)S(1)}, s32[1,32,32]{2,1,0:T(8,128)}, u32[]{:S(2)}) copy-start(s32[1,32,32]{2,1,0:T(8,128)} %param.9) | copy-start | bytes 12292
  20.5 19.6 %collective-permute-start.6 = (bf16[4,256,256]{2,1,0:T(8,128)(2,1)S(1)}, bf16[4,256,256]{2,1,0:T(8,128)(2,1)S(1)}, u32[]{:S(2)}, u32[]{:S(2)}) collective-permute-start(bf16[4,256,256]{2,1,0:T(8,128)(2,1)S(1)} %stack.2.refs_0_), channel_id=1, source_target_pairs={{0,8},{4,28},{8,16},{12,4},{16,24},{20,12},{24,0},{28,20},{1,9},{5... | collective-permute-start | bytes 1572872 | tf_op jit(solution)/shard_map/ppermute | solution.py:46
  25.2 15.6 %collective-permute-start.11 = (bf16[4,256,256]{2,1,0:T(8,128)(2,1)S(1)}, bf16[4,256,256]{2,1,0:T(8,128)(2,1)S(1)}, u32[]{:S(2)}, u32[]{:S(2)}) collective-permute-start(bf16[4,256,256]{2,1,0:T(8,128)(2,1)S(1)} %stack.3.refs_1_), channel_id=1, source_target_pairs={{0,8},{4,28},{8,16},{12,4},{16,24},{20,12},{24,0},{28,20},{1,9},{5... | collective-permute-start | bytes 1572872 | tf_op jit(solution)/shard_map/ppermute | solution.py:46
  27.7 3.0 %collective-permute-start.2 = (s32[32,32]{1,0:T(8,128)S(1)}, s32[32,32]{1,0:T(8,128)S(1)}, u32[]{:S(2)}, u32[]{:S(2)}) collective-permute-start(s32[32,32]{1,0:T(8,128)S(1)} %get-tuple-element.47), channel_id=1, source_target_pairs={{0,1},{1,0},{2,3},{3,2},{4,5},{5,4},{6,7},{7,6},{8,9},{9,8},{10,11... | collective-permute-start | bytes 12296 | tf_op jit(solution)/shard_map/ppermute | solution.py:414
  30.7 4.1 %collective-permute-start.3 = (s32[32,32]{1,0:T(8,128)S(1)}, s32[32,32]{1,0:T(8,128)S(1)}, u32[]{:S(2)}, u32[]{:S(2)}) collective-permute-start(s32[32,32]{1,0:T(8,128)S(1)} %add.77), channel_id=1, source_target_pairs={{0,2},{2,0},{1,3},{3,1},{4,6},{6,4},{5,7},{7,5},{8,10},{10,8},{9,1... | collective-permute-start | bytes 12296 | tf_op jit(solution)/shard_map/ppermute | solution.py:415
  33.6 11.2 %collective-permute-start.14 = (bf16[4,256,256]{2,1,0:T(8,128)(2,1)S(1)}, bf16[4,256,256]{2,1,0:T(8,128)(2,1)S(1)}, u32[]{:S(2)}, u32[]{:S(2)}) collective-permute-start(bf16[4,256,256]{2,1,0:T(8,128)(2,1)S(1)} %stack.2.refs_0_), channel_id=1, source_target_pairs={{0,24},{4,12},{8,0},{12,20},{16,8},{20,28},{24,16},{28,4},{1,25},{... | collective-permute-start | bytes 1572872 | tf_op jit(solution)/shard_map/ppermute | solution.py:46
  33.7 21.1 %collective-permute-start.15 = (bf16[4,256,256]{2,1,0:T(8,128)(2,1)S(1)}, bf16[4,256,256]{2,1,0:T(8,128)(2,1)S(1)}, u32[]{:S(2)}, u32[]{:S(2)}) collective-permute-start(bf16[4,256,256]{2,1,0:T(8,128)(2,1)S(1)} %stack.3.refs_1_), channel_id=1, source_target_pairs={{0,24},{4,12},{8,0},{12,20},{16,8},{20,28},{24,16},{28,4},{1,25},{... | collective-permute-start | bytes 1572872 | tf_op jit(solution)/shard_map/ppermute | solution.py:46
  34.8 7.2 %collective-permute-start.13 = (bf16[2,1024,128]{2,1,0:T(8,128)(2,1)S(1)}, bf16[2,1024,128]{2,1,0:T(8,128)(2,1)S(1)}, u32[]{:S(2)}, u32[]{:S(2)}) collective-permute-start(bf16[2,1024,128]{2,1,0:T(8,128)(2,1)S(1)} %get-tuple-element.48.refs_2_), channel_id=1, source_target_pairs={{0,4},{4,0},{1,5},{5,1},{2,6},{6,2},{3,7},{7,3},{8,12},{12,8},{9,1... | collective-permute-start | bytes 1572872 | tf_op jit(solution)/shard_map/ppermute | solution.py:50
  40.1 15.6 %collective-permute-start.7 = (bf16[4,256,256]{2,1,0:T(8,128)(2,1)S(1)}, bf16[4,256,256]{2,1,0:T(8,128)(2,1)S(1)}, u32[]{:S(2)}, u32[]{:S(2)}) collective-permute-start(bf16[4,256,256]{2,1,0:T(8,128)(2,1)S(1)} %collective-permute-done.6.refs_0_), channel_id=1, source_target_pairs={{0,8},{4,28},{8,16},{12,4},{16,24},{20,12},{24,0},{28,20},{1,9},{5... | collective-permute-start | bytes 1572872 | tf_op jit(solution)/shard_map/ppermute | solution.py:46
  40.7 21.4 %collective-permute-start.12 = (bf16[4,256,256]{2,1,0:T(8,128)(2,1)S(1)}, bf16[4,256,256]{2,1,0:T(8,128)(2,1)S(1)}, u32[]{:S(2)}, u32[]{:S(2)}) collective-permute-start(bf16[4,256,256]{2,1,0:T(8,128)(2,1)S(1)} %collective-permute-done.11.refs_1_), channel_id=1, source_target_pairs={{0,8},{4,28},{8,16},{12,4},{16,24},{20,12},{24,0},{28,20},{1,9},{5... | collective-permute-start | bytes 1572872 | tf_op jit(solution)/shard_map/ppermute | solution.py:46
  63.3 1.3 collective-permute-start.16
  65.6 13.2 %collective-permute-start.22 = (bf16[4,256,256]{2,1,0:T(8,128)(2,1)S(1)}, bf16[4,256,256]{2,1,0:T(8,128)(2,1)S(1)}, u32[]{:S(2)}, u32[]{:S(2)}) collective-permute-start(bf16[4,256,256]{2,1,0:T(8,128)(2,1)S(1)} %get-tuple-element.77), channel_id=1, source_target_pairs={{0,24},{4,12},{8,0},{12,20},{16,8},{20,28},{24,16},{28,4},{1,25},{... | collective-permute-start | bytes 1572872 | tf_op jit(solution)/shard_map/ppermute | solution.py:46
  66.9 23.2 %collective-permute-start.19 = (bf16[4,256,256]{2,1,0:T(8,128)(2,1)S(1)}, bf16[4,256,256]{2,1,0:T(8,128)(2,1)S(1)}, u32[]{:S(2)}, u32[]{:S(2)}) collective-permute-start(bf16[4,256,256]{2,1,0:T(8,128)(2,1)S(1)} %get-tuple-element.73), channel_id=1, source_target_pairs={{0,24},{4,12},{8,0},{12,20},{16,8},{20,28},{24,16},{28,4},{1,25},{... | collective-permute-start | bytes 1572872 | tf_op jit(solution)/shard_map/ppermute | solution.py:46
  71.6 33.4 %collective-permute-start.21 = (bf16[4,256,256]{2,1,0:T(8,128)(2,1)S(1)}, bf16[4,256,256]{2,1,0:T(8,128)(2,1)S(1)}, u32[]{:S(2)}, u32[]{:S(2)}) collective-permute-start(bf16[4,256,256]{2,1,0:T(8,128)(2,1)S(1)} %get-tuple-element.74), channel_id=1, source_target_pairs={{0,8},{4,28},{8,16},{12,4},{16,24},{20,12},{24,0},{28,20},{1,9},{5... | collective-permute-start | bytes 1572872 | tf_op jit(solution)/shard_map/ppermute | solution.py:46
  74.2 25.9 %collective-permute-start.24 = (bf16[4,256,256]{2,1,0:T(8,128)(2,1)S(1)}, bf16[4,256,256]{2,1,0:T(8,128)(2,1)S(1)}, u32[]{:S(2)}, u32[]{:S(2)}) collective-permute-start(bf16[4,256,256]{2,1,0:T(8,128)(2,1)S(1)} %get-tuple-element.78), channel_id=1, source_target_pairs={{0,8},{4,28},{8,16},{12,4},{16,24},{20,12},{24,0},{28,20},{1,9},{5... | collective-permute-start | bytes 1572872 | tf_op jit(solution)/shard_map/ppermute | solution.py:46
  79.0 21.6 %collective-permute-start.23 = (bf16[4,256,256]{2,1,0:T(8,128)(2,1)S(1)}, bf16[4,256,256]{2,1,0:T(8,128)(2,1)S(1)}, u32[]{:S(2)}, u32[]{:S(2)}) collective-permute-start(bf16[4,256,256]{2,1,0:T(8,128)(2,1)S(1)} %add_convert_fusion), channel_id=1, source_target_pairs={{0,24},{4,12},{8,0},{12,20},{16,8},{20,28},{24,16},{28,4},{1,25},{... | collective-permute-start | bytes 1572872 | tf_op jit(solution)/shard_map/ppermute | solution.py:46
  90.2 19.4 %collective-permute-start.20 = (bf16[4,256,256]{2,1,0:T(8,128)(2,1)S(1)}, bf16[4,256,256]{2,1,0:T(8,128)(2,1)S(1)}, u32[]{:S(2)}, u32[]{:S(2)}) collective-permute-start(bf16[4,256,256]{2,1,0:T(8,128)(2,1)S(1)} %add_convert_fusion.1), channel_id=1, source_target_pairs={{0,24},{4,12},{8,0},{12,20},{16,8},{20,28},{24,16},{28,4},{1,25},{... | collective-permute-start | bytes 1572872 | tf_op jit(solution)/shard_map/ppermute | solution.py:46
  90.3 32.6 %collective-permute-start.17 = (f32[128,1024]{1,0:T(8,128)S(1)}, f32[128,1024]{1,0:T(8,128)S(1)}, u32[]{:S(2)}, u32[]{:S(2)}) collective-permute-start(f32[128,1024]{1,0:T(8,128)S(1)} %get-tuple-element.60), channel_id=1, source_target_pairs={{0,4},{4,0},{1,5},{5,1},{2,6},{6,2},{3,7},{7,3},{8,12},{12,8},{9,1... | collective-permute-start | bytes 1572872 | tf_op jit(solution)/shard_map/ppermute | solution.py:50
  100.2 25.1 %collective-permute-start.18 = (f32[128,1024]{1,0:T(8,128)S(1)}, f32[128,1024]{1,0:T(8,128)S(1)}, u32[]{:S(2)}, u32[]{:S(2)}) collective-permute-start(f32[128,1024]{1,0:T(8,128)S(1)} %get-tuple-element.68), channel_id=1, source_target_pairs={{0,4},{4,0},{1,5},{5,1},{2,6},{6,2},{3,7},{7,3},{8,12},{12,8},{9,1... | collective-permute-start | bytes 1572872 | tf_op jit(solution)/shard_map/ppermute | solution.py:50
  100.8 13.5 %collective-permute-start.25 = (bf16[256,256]{1,0:T(8,128)(2,1)S(1)}, bf16[256,256]{1,0:T(8,128)(2,1)S(1)}, u32[]{:S(2)}, u32[]{:S(2)}) collective-permute-start(bf16[256,256]{1,0:T(8,128)(2,1)S(1)} %get-tuple-element.80), channel_id=1, source_target_pairs={{0,224},{4,36},{32,0},{36,68},{64,32},{68,100},{96,64},{100,132},{... | collective-permute-start | bytes 393224 | tf_op jit(solution)/shard_map/ppermute | solution.py:46
  105.0 14.1 %collective-permute-start.26 = (bf16[256,256]{1,0:T(8,128)(2,1)S(1)}, bf16[256,256]{1,0:T(8,128)(2,1)S(1)}, u32[]{:S(2)}, u32[]{:S(2)}) collective-permute-start(bf16[256,256]{1,0:T(8,128)(2,1)S(1)} %get-tuple-element.81), channel_id=1, source_target_pairs={{0,192},{4,68},{32,224},{36,100},{64,0},{68,132},{96,32},{100,164}... | collective-permute-start | bytes 393224 | tf_op jit(solution)/shard_map/ppermute | solution.py:46
  109.6 9.5 %collective-permute-start.27 = (bf16[256,256]{1,0:T(8,128)(2,1)S(1)}, bf16[256,256]{1,0:T(8,128)(2,1)S(1)}, u32[]{:S(2)}, u32[]{:S(2)}) collective-permute-start(bf16[256,256]{1,0:T(8,128)(2,1)S(1)} %get-tuple-element.82), channel_id=1, source_target_pairs={{0,32},{4,228},{32,64},{36,4},{64,96},{68,36},{96,128},{100,68},{1... | collective-permute-start | bytes 393224 | tf_op jit(solution)/shard_map/ppermute | solution.py:46
  119.4 7.0 %collective-permute-start.28 = (bf16[256,256]{1,0:T(8,128)(2,1)S(1)}, bf16[256,256]{1,0:T(8,128)(2,1)S(1)}, u32[]{:S(2)}, u32[]{:S(2)}) collective-permute-start(bf16[256,256]{1,0:T(8,128)(2,1)S(1)} %get-tuple-element.84), channel_id=1, source_target_pairs={{0,64},{4,196},{32,96},{36,228},{64,128},{68,4},{96,160},{100,36},... | collective-permute-start | bytes 393224 | tf_op jit(solution)/shard_map/ppermute | solution.py:46
  120.8 10.0 %collective-permute-start.29 = (bf16[256,256]{1,0:T(8,128)(2,1)S(1)}, bf16[256,256]{1,0:T(8,128)(2,1)S(1)}, u32[]{:S(2)}, u32[]{:S(2)}) collective-permute-start(bf16[256,256]{1,0:T(8,128)(2,1)S(1)} %get-tuple-element.85), channel_id=1, source_target_pairs={{0,192},{4,68},{32,224},{36,100},{64,0},{68,132},{96,32},{100,164}... | collective-permute-start | bytes 393224 | tf_op jit(solution)/shard_map/ppermute | solution.py:46
  121.8 10.1 %collective-permute-start.30 = (bf16[256,256]{1,0:T(8,128)(2,1)S(1)}, bf16[256,256]{1,0:T(8,128)(2,1)S(1)}, u32[]{:S(2)}, u32[]{:S(2)}) collective-permute-start(bf16[256,256]{1,0:T(8,128)(2,1)S(1)} %get-tuple-element.86), channel_id=1, source_target_pairs={{0,224},{4,36},{32,0},{36,68},{64,32},{68,100},{96,64},{100,132},{... | collective-permute-start | bytes 393224 | tf_op jit(solution)/shard_map/ppermute | solution.py:46
  122.9 9.0 %collective-permute-start.31 = (bf16[256,256]{1,0:T(8,128)(2,1)S(1)}, bf16[256,256]{1,0:T(8,128)(2,1)S(1)}, u32[]{:S(2)}, u32[]{:S(2)}) collective-permute-start(bf16[256,256]{1,0:T(8,128)(2,1)S(1)} %get-tuple-element.87), channel_id=1, source_target_pairs={{0,32},{4,228},{32,64},{36,4},{64,96},{68,36},{96,128},{100,68},{1... | collective-permute-start | bytes 393224 | tf_op jit(solution)/shard_map/ppermute | solution.py:46
where the time goes:
time: 134 us; the launch traced here: 133 us
  starting transfers between devices  67.5 us (50%)
  waiting for transfers between devices  48.9 us (36%)
  Pallas kernels  13 us (10%)
  local copies, waits for them, and re-layouts  1.69 us (1%)
    ppermute x26, starting transfers between devices, shift(): lax.ppermute(a, (axis, 'core'), [(2 * i + c, 2 * ((i + d * (1 - 2 * c)) %...  50.3 us
    ppermute x26, waiting for transfers between devices, shift(): lax.ppermute(a, (axis, 'core'), [(2 * i + c, 2 * ((i + d * (1 - 2 * c)) %...  45.2 us
    ppermute x4, starting transfers between devices, swap(): return lax.ppermute(a, 'core', [(0, 1), (1, 0)])  12.9 us
    pallas_call x4, Pallas kernels, backward(): pl.pallas_call(functools.partial(backward_kernel, base, n, first, base ==...  5.89 us
    pallas_call x4, Pallas kernels, forward(): pl.pallas_call(functools.partial(forward_kernel, base, n, first, last), g...  4.76 us
    ppermute x1, starting transfers between devices, plan(): lax.ppermute(totals, 'head', [(0, 2), (2, 0), (1, 3), (3, 1)])  2.91 us
  transfers between devices with their start and end apart: 32, of which 14 were waited for; matrix products, arithmetic and copies ran while one was open for 1% of the time, Pallas kernels for 8%

commit v1 on v0

--- a/solution.py
+++ b/solution.py
@@ -311,13 +311,26 @@
 SMALL = pltpu.CompilerParams(vmem_limit_bytes=8 * 1024 * 1024)
 
 
-def join_kernel(k_ref, v_ref, out_ref):
-    out_ref[:, :HEAD_DIM] = k_ref[...]
-    out_ref[:, HEAD_DIM:] = v_ref[...]
+def join_kernel(k_ref, v_ref, out_ref, sems):
+    copies = [
+        pltpu.make_async_copy(k_ref, out_ref.at[:, pl.ds(0, HEAD_DIM)], sems.at[0]),
+        pltpu.make_async_copy(v_ref, out_ref.at[:, pl.ds(HEAD_DIM, HEAD_DIM)], sems.at[1]),
+    ]
+    for copy in copies:
+        copy.start()
+    for copy in copies:
+        copy.wait()
 
 
 def join(k, v):
-    return pl.pallas_call(join_kernel, out_shape=jax.ShapeDtypeStruct(PIECE, BF), in_specs=[VMEM] * 2, out_specs=VMEM, compiler_params=SMALL, name="join")(k, v)
+    return pl.pallas_call(
+        join_kernel,
+        out_shape=jax.ShapeDtypeStruct(PIECE, BF),
+        in_specs=[pl.BlockSpec(memory_space=pl.ANY)] * 2,
+        out_specs=VMEM,
+        scratch_shapes=[pltpu.SemaphoreType.DMA((2,))],
+        name="join",
+    )(k, v)
 
 
 def prepare_kernel(query, grad_out, gate, after, qg_ref, gate_ref):
@@ -371,27 +384,46 @@
     )(own, one, three)
 
 
-def sum_low_kernel(own, one, three, keep, down, far, up, own_out, near_down, near_up, two_down, two_up):
+def sum_low_kernel(own, one, three, own_out, near_down, near_up, keep):
     def total(i):
         return wide(own[i]) + wide(one[i]) + wide(three[i])
 
     own_out[...] = total(0)
     near_down[...] = total(1).astype(BF)
     near_up[...] = total(2).astype(BF)
-    two_down[...] = (total(3) + wide(down[...]) + wide(far[...])).astype(BF)
-    two_up[...] = (keep[...] + wide(up[...])).astype(BF)
-
-
-def sum_low(own, one, three, keep, down, far, up):
+    keep[...] = total(3)
+
+
+def sum_low(own, one, three):
+    kept = jax.ShapeDtypeStruct(PIECE, F32)
     shape = jax.ShapeDtypeStruct(PIECE, BF)
     return pl.pallas_call(
         sum_low_kernel,
-        in_specs=[VMEM] * 7,
-        out_specs=[VMEM] * 5,
-        out_shape=[jax.ShapeDtypeStruct(PIECE, F32), shape, shape, shape, shape],
+        in_specs=[VMEM] * 3,
+        out_specs=[VMEM] * 4,
+        out_shape=[kept, shape, shape, kept],
         cost_estimate=cost(100_000_000),
-        compiler_params=SMALL, name="sum_low",
-    )(own, one, three, keep, down, far, up)
+        compiler_params=SMALL,
+        name="sum_low",
+    )(own, one, three)
+
+
+def sum_two_kernel(high, low, down, far, up, two_down, two_up):
+    two_down[...] = (low[...] + wide(down[...]) + wide(far[...])).astype(BF)
+    two_up[...] = (high[...] + wide(up[...])).astype(BF)
+
+
+def sum_two(high, low, down, far, up):
+    shape = jax.ShapeDtypeStruct(PIECE, BF)
+    return pl.pallas_call(
+        sum_two_kernel,
+        in_specs=[VMEM] * 5,
+        out_specs=[VMEM] * 2,
+        out_shape=[shape, shape],
+        cost_estimate=cost(100_000_000),
+        compiler_params=SMALL,
+        name="sum_two",
+    )(high, low, down, far, up)
 
 
 def close_kernel(own, a, b, c, d, dk_ref, dv_ref):
@@ -459,14 +491,15 @@
     low1 = shift((wide(low1) + wide(low2)).astype(BF), "x", -1)
     dq, (low0, high0) = backward(0, info, [low0, high0], qg, mine, other, dq)
 
-    keep, up, down, far = sum_high(high0, high1, high3)
+    keep_high, up, down, far = sum_high(high0, high1, high3)
     down, far, up = shift(down, "z", -1), shift(far, "z", -2), shift(up, "z", 1)
-    own, near_down, near_up, two_down, two_up = sum_low(low0, low1, low3, keep, down, far, up)
+    own, near_down, near_up, keep_low = sum_low(low0, low1, low3)
+    two_down, two_up = sum_two(keep_high, keep_low, down, far, up)
     parts = [
+        shift(near_down, "z", -1),
+        shift(near_up, "z", 1),
         shift(two_up, "z", 2),
         shift(two_down, "z", -2),
-        shift(near_down, "z", -1),
-        shift(near_up, "z", 1),
     ]
     grad_key, grad_value = close(own, parts)
     attended, grad_query = finish(mine, other, acc, acc_other, dq[0], swap(dq[1]))

time: 134 us -> 130 us (0.970); the launches traced: 133 us -> 130 us
  starting transfers between devices: 67.5 us -> 65.4 us
  Pallas kernels: 13 us -> 14.5 us
    ppermute x26, starting transfers between devices: 50.3 us -> 48.3 us  [shift(): lax.ppermute(a, (axis, 'core'), [(2 * i + c, 2 * ((i + d * (1 - 2 * c)) %...]
    pallas_call x1, Pallas kernels: 0.02 us -> 1.54 us  [join(): pl.pallas_call(join_kernel, out_shape=jax.ShapeDtypeStruct(PIECE, BF), in...]
where the time goes in v1:
time: 130 us
  starting transfers between devices  65.4 us (50%)
  waiting for transfers between devices  48 us (37%)
  Pallas kernels  14.5 us (11%)
    ppermute x26, starting transfers between devices, shift(): lax.ppermute(a, (axis, 'core'), [(2 * i + c, 2 * ((i + d * (1 - 2 * c)) %...  48.3 us
    ppermute x26, waiting for transfers between devices, shift(): lax.ppermute(a, (axis, 'core'), [(2 * i + c, 2 * ((i + d * (1 - 2 * c)) %...  44.3 us
    ppermute x4, starting transfers between devices, swap(): return lax.ppermute(a, 'core', [(0, 1), (1, 0)])  12.9 us
    pallas_call x4, Pallas kernels, backward(): pl.pallas_call(functools.partial(backward_kernel, base, n, first, base ==...  5.88 us
    pallas_call x4, Pallas kernels, forward(): pl.pallas_call(functools.partial(forward_kernel, base, n, first, last), g...  4.75 us
    ppermute x1, starting transfers between devices, plan(): lax.ppermute(totals, 'head', [(0, 2), (2, 0), (1, 3), (3, 1)])  2.91 us
  transfers between devices with their start and end apart: 32, of which 14 were waited for; matrix products, arithmetic and copies ran while one was open for 1% of the time, Pallas kernels for 8%

profile of v1, /device:TPU:1, one launch (start us, length us, event | category | flops | bytes accessed | tf_op | source)
XLA Modules:
  0.0 130.4 jit_solution(7475535753403234632)
XLA Ops:
  0.6 1.5 %join.1.refs_0_ = bf16[256,256]{1,0:T(8,128)(2,1)} custom-call(bf16[256,128]{1,0:T(8,128)(2,1)} %k_ref.1, bf16[256,128]{1,0:T(8,128)(2,1)} %v_ref.1), custom_call_target="tpu_custom_call" | custom-call | tf_op jit(solution)/shard_map/join/pallas_call | solution.py:326
  2.2 3.9 %collective-permute-start.8 = (bf16[256,256]{1,0:T(8,128)(2,1)}, bf16[256,256]{1,0:T(8,128)(2,1)S(1)}, u32[]{:S(2)}, u32[]{:S(2)}) collective-permute-start(bf16[256,256]{1,0:T(8,128)(2,1)} %join.1.refs_0_), channel_id=1, source_target_pairs={{0,192},{4,68},{32,224},{36,100},{64,0},{68,132},{96,32},{100,164}... | collective-permute-start | bytes 393224 | tf_op jit(solution)/shard_map/ppermute | solution.py:46
  6.1 3.1 %collective-permute-start = (bf16[256,256]{1,0:T(8,128)(2,1)}, bf16[256,256]{1,0:T(8,128)(2,1)S(1)}, u32[]{:S(2)}, u32[]{:S(2)}) collective-permute-start(bf16[256,256]{1,0:T(8,128)(2,1)} %join.1.refs_0_), channel_id=1, source_target_pairs={{0,64},{4,196},{32,96},{36,228},{64,128},{68,4},{96,160},{100,36},... | collective-permute-start | bytes 393224 | tf_op jit(solution)/shard_map/ppermute | solution.py:46
  9.2 0.7 collective-permute-start.5
  9.9 1.9 %collective-permute-start.4 = (bf16[256,256]{1,0:T(8,128)(2,1)}, bf16[256,256]{1,0:T(8,128)(2,1)S(1)}, u32[]{:S(2)}, u32[]{:S(2)}) collective-permute-start(bf16[256,256]{1,0:T(8,128)(2,1)} %join.1.refs_0_), channel_id=1, source_target_pairs={{0,32},{4,228},{32,64},{36,4},{64,96},{68,36},{96,128},{100,68},{1... | collective-permute-start | bytes 393224 | tf_op jit(solution)/shard_map/ppermute | solution.py:46
  11.9 2.0 %collective-permute-start.9 = (bf16[256,256]{1,0:T(8,128)(2,1)S(1)}, bf16[256,256]{1,0:T(8,128)(2,1)S(1)}, u32[]{:S(2)}, u32[]{:S(2)}) collective-permute-start(bf16[256,256]{1,0:T(8,128)(2,1)S(1)} %collective-permute-done.8.refs_0_), channel_id=1, source_target_pairs={{0,224},{4,36},{32,0},{36,68},{64,32},{68,100},{96,64},{100,132},{... | collective-permute-start | bytes 393224 | tf_op jit(solution)/shard_map/ppermute | solution.py:46
  13.9 1.9 %collective-permute-done.refs_3_ = bf16[256,256]{1,0:T(8,128)(2,1)S(1)} collective-permute-done((bf16[256,256]{1,0:T(8,128)(2,1)}, bf16[256,256]{1,0:T(8,128)(2,1)S(1)}, u32[]{:S(2)}, u32[]{:S(2)}) %collective-permute-start) | collective-permute-done | bytes 131104 | tf_op jit(solution)/shard_map/ppermute | solution.py:46
  15.8 0.8 collective-permute-start.10
  16.7 3.8 %collective-permute-start.1 = (bf16[256,256]{1,0:T(8,128)(2,1)S(1)}, bf16[256,256]{1,0:T(8,128)(2,1)S(1)}, u32[]{:S(2)}, u32[]{:S(2)}) collective-permute-start(bf16[256,256]{1,0:T(8,128)(2,1)S(1)} %collective-permute-done.refs_3_), channel_id=1, source_target_pairs={{0,32},{4,228},{32,64},{36,4},{64,96},{68,36},{96,128},{100,68},{1... | collective-permute-start | bytes 393224 | tf_op jit(solution)/shard_map/ppermute | solution.py:46
  20.5 0.9 copy-done
  21.4 1.7 %collective-permute-start.6 = (bf16[4,256,256]{2,1,0:T(8,128)(2,1)S(1)}, bf16[4,256,256]{2,1,0:T(8,128)(2,1)S(1)}, u32[]{:S(2)}, u32[]{:S(2)}) collective-permute-start(bf16[4,256,256]{2,1,0:T(8,128)(2,1)S(1)} %stack.2.refs_0_), channel_id=1, source_target_pairs={{0,8},{4,28},{8,16},{12,4},{16,24},{20,12},{24,0},{28,20},{1,9},{5... | collective-permute-start | bytes 1572872 | tf_op jit(solution)/shard_map/ppermute | solution.py:46
  23.1 2.1 %collective-permute-done.1.after.refs_1_ = bf16[256,256]{1,0:T(8,128)(2,1)S(1)} collective-permute-done((bf16[256,256]{1,0:T(8,128)(2,1)S(1)}, bf16[256,256]{1,0:T(8,128)(2,1)S(1)}, u32[]{:S(2)}, u32[]{:S(2)}) %collective-permute-start.1) | collective-permute-done | bytes 131104 | tf_op jit(solution)/shard_map/ppermute | solution.py:46
  25.2 2.5 %collective-permute-start.11 = (bf16[4,256,256]{2,1,0:T(8,128)(2,1)S(1)}, bf16[4,256,256]{2,1,0:T(8,128)(2,1)S(1)}, u32[]{:S(2)}, u32[]{:S(2)}) collective-permute-start(bf16[4,256,256]{2,1,0:T(8,128)(2,1)S(1)} %stack.3.refs_1_), channel_id=1, source_target_pairs={{0,8},{4,28},{8,16},{12,4},{16,24},{20,12},{24,0},{28,20},{1,9},{5... | collective-permute-start | bytes 1572872 | tf_op jit(solution)/shard_map/ppermute | solution.py:46
  27.7 0.1 prepare.1
  27.8 1.4 %collective-permute-start.2 = (s32[32,32]{1,0:T(8,128)S(1)}, s32[32,32]{1,0:T(8,128)S(1)}, u32[]{:S(2)}, u32[]{:S(2)}) collective-permute-start(s32[32,32]{1,0:T(8,128)S(1)} %get-tuple-element.48), channel_id=1, source_target_pairs={{0,1},{1,0},{2,3},{3,2},{4,5},{5,4},{6,7},{7,6},{8,9},{9,8},{10,11... | collective-permute-start | bytes 12296 | tf_op jit(solution)/shard_map/ppermute | solution.py:446
  29.2 1.6 %collective-permute-done.2 = s32[32,32]{1,0:T(8,128)S(1)} collective-permute-done((s32[32,32]{1,0:T(8,128)S(1)}, s32[32,32]{1,0:T(8,128)S(1)}, u32[]{:S(2)}, u32[]{:S(2)}) %collective-permute-start.2) | collective-permute-done | bytes 4128 | tf_op jit(solution)/shard_map/ppermute | solution.py:446
  30.8 2.9 %collective-permute-start.3 = (s32[32,32]{1,0:T(8,128)S(1)}, s32[32,32]{1,0:T(8,128)S(1)}, u32[]{:S(2)}, u32[]{:S(2)}) collective-permute-start(s32[32,32]{1,0:T(8,128)S(1)} %add.77), channel_id=1, source_target_pairs={{0,2},{2,0},{1,3},{3,1},{4,6},{6,4},{5,7},{7,5},{8,10},{10,8},{9,1... | collective-permute-start | bytes 12296 | tf_op jit(solution)/shard_map/ppermute | solution.py:447
  33.7 0.1 collective-permute-start.14
  33.8 0.2 collective-permute-start.15
  34.0 0.9 collective-permute-done.3
  34.9 5.2 %collective-permute-start.13 = (bf16[2,1024,128]{2,1,0:T(8,128)(2,1)S(1)}, bf16[2,1024,128]{2,1,0:T(8,128)(2,1)S(1)}, u32[]{:S(2)}, u32[]{:S(2)}) collective-permute-start(bf16[2,1024,128]{2,1,0:T(8,128)(2,1)S(1)} %get-tuple-element.49.refs_2_), channel_id=1, source_target_pairs={{0,4},{4,0},{1,5},{5,1},{2,6},{6,2},{3,7},{7,3},{8,12},{12,8},{9,1... | collective-permute-start | bytes 1572872 | tf_op jit(solution)/shard_map/ppermute | solution.py:50
  40.1 0.6 collective-permute-start.7
  40.8 0.9 collective-permute-start.12
  41.6 0.2 convert_reduce_fusion.1
  41.8 0.1 convert_reduce_fusion
  41.9 0.1 pad_add_fusion.info
  42.0 2.0 %forward.4 = (f32[2,3,1024]{2,1,0:T(4,128)S(1)}, f32[128,1024]{1,0:T(8,128)S(1)}, f32[128,1024]{1,0:T(8,128)S(1)}) custom-call(s32[33]{0:T(128)S(1)} %pad_add_fusion.info, bf16[4,256,256]{2,1,0:T(8,128)(2,1)S(1)} %stack.2.refs_0_, bf16[4,256,256]{2,1,0:T(8,128)(2,1)S(1)} %stack.3.refs_1_, bf16[2,1024,128]{2,1,0:T(8,128)(2,1)S(1)} %get-tuple-element.49.refs_2_, ...), custom_call_target="tpu_custom_call" | custom-call | flops 200000000 | bytes 65536 | tf_op jit(solution)/shard_map/forward/pallas_call | solution.py:244
  44.0 0.8 forward.5
  44.8 10.0 %collective-permute-done.15.refs_1_ = bf16[4,256,256]{2,1,0:T(8,128)(2,1)S(1)} collective-permute-done((bf16[4,256,256]{2,1,0:T(8,128)(2,1)S(1)}, bf16[4,256,256]{2,1,0:T(8,128)(2,1)S(1)}, u32[]{:S(2)}, u32[]{:S(2)}) %collective-permute-start.15) | collective-permute-done | bytes 524320 | tf_op jit(solution)/shard_map/ppermute | solution.py:46
  54.8 0.8 forward.6
  55.6 6.5 %collective-permute-done.12.refs_1_ = bf16[4,256,256]{2,1,0:T(8,128)(2,1)S(1)} collective-permute-done((bf16[4,256,256]{2,1,0:T(8,128)(2,1)S(1)}, bf16[4,256,256]{2,1,0:T(8,128)(2,1)S(1)}, u32[]{:S(2)}, u32[]{:S(2)}) %collective-permute-start.12) | collective-permute-done | bytes 524320 | tf_op jit(solution)/shard_map/ppermute | solution.py:46
  62.1 1.2 forward.7
  63.3 0.1 collective-permute-start.16
  63.4 1.2 collective-permute-done.16.refs_5_.other
  64.6 1.1 backward.4
  65.7 1.3 collective-permute-start.24
  66.9 3.6 %collective-permute-start.19 = (bf16[4,256,256]{2,1,0:T(8,128)(2,1)S(1)}, bf16[4,256,256]{2,1,0:T(8,128)(2,1)S(1)}, u32[]{:S(2)}, u32[]{:S(2)}) collective-permute-start(bf16[4,256,256]{2,1,0:T(8,128)(2,1)S(1)} %get-tuple-element.74), channel_id=1, source_target_pairs={{0,24},{4,12},{8,0},{12,20},{16,8},{20,28},{24,16},{28,4},{1,25},{... | collective-permute-start | bytes 1572872 | tf_op jit(solution)/shard_map/ppermute | solution.py:46
  70.5 1.1 backward.5
  71.6 2.6 %collective-permute-start.21 = (bf16[4,256,256]{2,1,0:T(8,128)(2,1)S(1)}, bf16[4,256,256]{2,1,0:T(8,128)(2,1)S(1)}, u32[]{:S(2)}, u32[]{:S(2)}) collective-permute-start(bf16[4,256,256]{2,1,0:T(8,128)(2,1)S(1)} %get-tuple-element.75), channel_id=1, source_target_pairs={{0,8},{4,28},{8,16},{12,4},{16,24},{20,12},{24,0},{28,20},{1,9},{5... | collective-permute-start | bytes 1572872 | tf_op jit(solution)/shard_map/ppermute | solution.py:46
  74.1 1.4 %collective-permute-start.26 = (bf16[4,256,256]{2,1,0:T(8,128)(2,1)S(1)}, bf16[4,256,256]{2,1,0:T(8,128)(2,1)S(1)}, u32[]{:S(2)}, u32[]{:S(2)}) collective-permute-start(bf16[4,256,256]{2,1,0:T(8,128)(2,1)S(1)} %get-tuple-element.82), channel_id=1, source_target_pairs={{0,8},{4,28},{8,16},{12,4},{16,24},{20,12},{24,0},{28,20},{1,9},{5... | collective-permute-start | bytes 1572872 | tf_op jit(solution)/shard_map/ppermute | solution.py:46
  75.6 1.1 backward.6
  76.7 2.1 %collective-permute-done.24 = bf16[4,256,256]{2,1,0:T(8,128)(2,1)S(1)} collective-permute-done((bf16[4,256,256]{2,1,0:T(8,128)(2,1)S(1)}, bf16[4,256,256]{2,1,0:T(8,128)(2,1)S(1)}, u32[]{:S(2)}, u32[]{:S(2)}) %collective-permute-start.24) | collective-permute-done | bytes 524320 | tf_op jit(solution)/shard_map/ppermute | solution.py:46
  78.8 0.1 add_convert_fusion
  78.9 0.1 collective-permute-start.25
  79.0 11.0 %collective-permute-done.19 = bf16[4,256,256]{2,1,0:T(8,128)(2,1)S(1)} collective-permute-done((bf16[4,256,256]{2,1,0:T(8,128)(2,1)S(1)}, bf16[4,256,256]{2,1,0:T(8,128)(2,1)S(1)}, u32[]{:S(2)}, u32[]{:S(2)}) %collective-permute-start.19) | collective-permute-done | bytes 524320 | tf_op jit(solution)/shard_map/ppermute | solution.py:46
  90.0 0.1 add_convert_fusion.1
  90.1 0.1 collective-permute-start.20
  90.2 7.1 %collective-permute-start.17 = (f32[128,1024]{1,0:T(8,128)S(1)}, f32[128,1024]{1,0:T(8,128)S(1)}, u32[]{:S(2)}, u32[]{:S(2)}) collective-permute-start(f32[128,1024]{1,0:T(8,128)S(1)} %get-tuple-element.61), channel_id=1, source_target_pairs={{0,4},{4,0},{1,5},{5,1},{2,6},{6,2},{3,7},{7,3},{8,12},{12,8},{9,1... | collective-permute-start | bytes 1572872 | tf_op jit(solution)/shard_map/ppermute | solution.py:50
  97.3 2.7 %backward.7 = (f32[128,1024]{1,0:T(8,128)S(1)}, f32[128,1024]{1,0:T(8,128)S(1)}, bf16[4,256,256]{2,1,0:T(8,128)(2,1)S(1)}, bf16[4,256,256]{2,1,0:T(8,128)(2,1)S(1)}) custom-call(s32[33]{0:T(128)S(1)} %pad_add_fusion.info, bf16[4,256,256]{2,1,0:T(8,128)(2,1)S(1)} %stack.2.refs_0_, bf16[4,256,256]{2,1,0:T(8,128)(2,1)S(1)} %stack.3.refs_1_, ...), custom_call_target="tpu_custom_call" | custom-call | flops 200000000 | bytes 65536 | tf_op jit(solution)/shard_map/backward/pallas_call | solution.py:272
  100.1 0.4 collective-permute-start.18
  100.5 0.2 sum_high.1
  100.7 4.3 %collective-permute-start.27 = (bf16[256,256]{1,0:T(8,128)(2,1)S(1)}, bf16[256,256]{1,0:T(8,128)(2,1)S(1)}, u32[]{:S(2)}, u32[]{:S(2)}) collective-permute-start(bf16[256,256]{1,0:T(8,128)(2,1)S(1)} %get-tuple-element.85), channel_id=1, source_target_pairs={{0,224},{4,36},{32,0},{36,68},{64,32},{68,100},{96,64},{100,132},{... | collective-permute-start | bytes 393224 | tf_op jit(solution)/shard_map/ppermute | solution.py:46
  105.0 5.1 %collective-permute-start.28 = (bf16[256,256]{1,0:T(8,128)(2,1)S(1)}, bf16[256,256]{1,0:T(8,128)(2,1)S(1)}, u32[]{:S(2)}, u32[]{:S(2)}) collective-permute-start(bf16[256,256]{1,0:T(8,128)(2,1)S(1)} %get-tuple-element.86), channel_id=1, source_target_pairs={{0,192},{4,68},{32,224},{36,100},{64,0},{68,132},{96,32},{100,164}... | collective-permute-start | bytes 393224 | tf_op jit(solution)/shard_map/ppermute | solution.py:46
  110.0 4.0 %collective-permute-start.29 = (bf16[256,256]{1,0:T(8,128)(2,1)S(1)}, bf16[256,256]{1,0:T(8,128)(2,1)S(1)}, u32[]{:S(2)}, u32[]{:S(2)}) collective-permute-start(bf16[256,256]{1,0:T(8,128)(2,1)S(1)} %get-tuple-element.87), channel_id=1, source_target_pairs={{0,32},{4,228},{32,64},{36,4},{64,96},{68,36},{96,128},{100,68},{1... | collective-permute-start | bytes 393224 | tf_op jit(solution)/shard_map/ppermute | solution.py:46
  114.0 0.2 sum_low.1
  114.2 0.1 collective-permute-done.27.down
  114.3 4.7 %collective-permute-done.28.far = bf16[256,256]{1,0:T(8,128)(2,1)S(1)} collective-permute-done((bf16[256,256]{1,0:T(8,128)(2,1)S(1)}, bf16[256,256]{1,0:T(8,128)(2,1)S(1)}, u32[]{:S(2)}, u32[]{:S(2)}) %collective-permute-start.28) | collective-permute-done | bytes 131104 | tf_op jit(solution)/shard_map/ppermute | solution.py:46
  119.0 0.4 collective-permute-done.29.up
  119.4 0.1 sum_two.1
  119.5 3.7 %collective-permute-start.30 = (bf16[256,256]{1,0:T(8,128)(2,1)S(1)}, bf16[256,256]{1,0:T(8,128)(2,1)S(1)}, u32[]{:S(2)}, u32[]{:S(2)}) collective-permute-start(bf16[256,256]{1,0:T(8,128)(2,1)S(1)} %get-tuple-element.88), channel_id=1, source_target_pairs={{0,64},{4,196},{32,96},{36,228},{64,128},{68,4},{96,160},{100,36},... | collective-permute-start | bytes 393224 | tf_op jit(solution)/shard_map/ppermute | solution.py:46
  123.2 1.0 finish.1
  124.2 3.8 %collective-permute-done.30.c = bf16[256,256]{1,0:T(8,128)(2,1)S(1)} collective-permute-done((bf16[256,256]{1,0:T(8,128)(2,1)S(1)}, bf16[256,256]{1,0:T(8,128)(2,1)S(1)}, u32[]{:S(2)}, u32[]{:S(2)}) %collective-permute-start.30) | collective-permute-done | bytes 131104 | tf_op jit(solution)/shard_map/ppermute | solution.py:46
  128.0 1.7 %collective-permute-done.31.d = bf16[256,256]{1,0:T(8,128)(2,1)S(1)} collective-permute-done((bf16[256,256]{1,0:T(8,128)(2,1)S(1)}, bf16[256,256]{1,0:T(8,128)(2,1)S(1)}, u32[]{:S(2)}, u32[]{:S(2)}) %collective-permute-start.31) | collective-permute-done | bytes 131104 | tf_op jit(solution)/shard_map/ppermute | solution.py:46
  129.7 0.7 close.1
  (35 shorter events, 0.2 us)
Async XLA Ops:
  2.2 9.7 %collective-permute-start.8 = (bf16[256,256]{1,0:T(8,128)(2,1)}, bf16[256,256]{1,0:T(8,128)(2,1)S(1)}, u32[]{:S(2)}, u32[]{:S(2)}) collective-permute-start(bf16[256,256]{1,0:T(8,128)(2,1)} %join.1.refs_0_), channel_id=1, source_target_pairs={{0,192},{4,68},{32,224},{36,100},{64,0},{68,132},{96,32},{100,164}... | collective-permute-start | bytes 393224 | tf_op jit(solution)/shard_map/ppermute | solution.py:46
  6.1 9.8 %collective-permute-start = (bf16[256,256]{1,0:T(8,128)(2,1)}, bf16[256,256]{1,0:T(8,128)(2,1)S(1)}, u32[]{:S(2)}, u32[]{:S(2)}) collective-permute-start(bf16[256,256]{1,0:T(8,128)(2,1)} %join.1.refs_0_), channel_id=1, source_target_pairs={{0,64},{4,196},{32,96},{36,228},{64,128},{68,4},{96,160},{100,36},... | collective-permute-start | bytes 393224 | tf_op jit(solution)/shard_map/ppermute | solution.py:46
  9.2 11.2 %collective-permute-start.5 = (bf16[256,256]{1,0:T(8,128)(2,1)}, bf16[256,256]{1,0:T(8,128)(2,1)S(1)}, u32[]{:S(2)}, u32[]{:S(2)}) collective-permute-start(bf16[256,256]{1,0:T(8,128)(2,1)} %join.1.refs_0_), channel_id=1, source_target_pairs={{0,224},{4,36},{32,0},{36,68},{64,32},{68,100},{96,64},{100,132},{... | collective-permute-start | bytes 393224 | tf_op jit(solution)/shard_map/ppermute | solution.py:46
  9.9 10.5 %collective-permute-start.4 = (bf16[256,256]{1,0:T(8,128)(2,1)}, bf16[256,256]{1,0:T(8,128)(2,1)S(1)}, u32[]{:S(2)}, u32[]{:S(2)}) collective-permute-start(bf16[256,256]{1,0:T(8,128)(2,1)} %join.1.refs_0_), channel_id=1, source_target_pairs={{0,32},{4,228},{32,64},{36,4},{64,96},{68,36},{96,128},{100,68},{1... | collective-permute-start | bytes 393224 | tf_op jit(solution)/shard_map/ppermute | solution.py:46
  11.9 11.2 %collective-permute-start.9 = (bf16[256,256]{1,0:T(8,128)(2,1)S(1)}, bf16[256,256]{1,0:T(8,128)(2,1)S(1)}, u32[]{:S(2)}, u32[]{:S(2)}) collective-permute-start(bf16[256,256]{1,0:T(8,128)(2,1)S(1)} %collective-permute-done.8.refs_0_), channel_id=1, source_target_pairs={{0,224},{4,36},{32,0},{36,68},{64,32},{68,100},{96,64},{100,132},{... | collective-permute-start | bytes 393224 | tf_op jit(solution)/shard_map/ppermute | solution.py:46
  15.8 7.3 %collective-permute-start.10 = (bf16[256,256]{1,0:T(8,128)(2,1)S(1)}, bf16[256,256]{1,0:T(8,128)(2,1)S(1)}, u32[]{:S(2)}, u32[]{:S(2)}) collective-permute-start(bf16[256,256]{1,0:T(8,128)(2,1)S(1)} %collective-permute-done.refs_3_), channel_id=1, source_target_pairs={{0,64},{4,196},{32,96},{36,228},{64,128},{68,4},{96,160},{100,36},... | collective-permute-start | bytes 393224 | tf_op jit(solution)/shard_map/ppermute | solution.py:46
  16.7 8.5 %collective-permute-start.1 = (bf16[256,256]{1,0:T(8,128)(2,1)S(1)}, bf16[256,256]{1,0:T(8,128)(2,1)S(1)}, u32[]{:S(2)}, u32[]{:S(2)}) collective-permute-start(bf16[256,256]{1,0:T(8,128)(2,1)S(1)} %collective-permute-done.refs_3_), channel_id=1, source_target_pairs={{0,32},{4,228},{32,64},{36,4},{64,96},{68,36},{96,128},{100,68},{1... | collective-permute-start | bytes 393224 | tf_op jit(solution)/shard_map/ppermute | solution.py:46
  20.4 0.9 copy-start
  21.4 6.3 %copy-start.1 = (bf16[256,512]{1,0:T(8,128)(2,1)S(1)}, bf16[256,512]{1,0:T(8,128)(2,1)}, u32[]{:S(2)}) copy-start(bf16[256,512]{1,0:T(8,128)(2,1)} %query.1) | copy-start | bytes 786436
  21.4 6.3 %copy-start.2 = (bf16[256,512]{1,0:T(8,128)(2,1)S(1)}, bf16[256,512]{1,0:T(8,128)(2,1)}, u32[]{:S(2)}) copy-start(bf16[256,512]{1,0:T(8,128)(2,1)} %grad_out.1) | copy-start | bytes 786436
  21.4 6.3 %copy-start.3 = (s32[1,32,32]{2,1,0:T(8,128)S(1)}, s32[1,32,32]{2,1,0:T(8,128)}, u32[]{:S(2)}) copy-start(s32[1,32,32]{2,1,0:T(8,128)} %param.9) | copy-start | bytes 12292
  21.4 18.7 %collective-permute-start.6 = (bf16[4,256,256]{2,1,0:T(8,128)(2,1)S(1)}, bf16[4,256,256]{2,1,0:T(8,128)(2,1)S(1)}, u32[]{:S(2)}, u32[]{:S(2)}) collective-permute-start(bf16[4,256,256]{2,1,0:T(8,128)(2,1)S(1)} %stack.2.refs_0_), channel_id=1, source_target_pairs={{0,8},{4,28},{8,16},{12,4},{16,24},{20,12},{24,0},{28,20},{1,9},{5... | collective-permute-start | bytes 1572872 | tf_op jit(solution)/shard_map/ppermute | solution.py:46
  25.2 15.5 %collective-permute-start.11 = (bf16[4,256,256]{2,1,0:T(8,128)(2,1)S(1)}, bf16[4,256,256]{2,1,0:T(8,128)(2,1)S(1)}, u32[]{:S(2)}, u32[]{:S(2)}) collective-permute-start(bf16[4,256,256]{2,1,0:T(8,128)(2,1)S(1)} %stack.3.refs_1_), channel_id=1, source_target_pairs={{0,8},{4,28},{8,16},{12,4},{16,24},{20,12},{24,0},{28,20},{1,9},{5... | collective-permute-start | bytes 1572872 | tf_op jit(solution)/shard_map/ppermute | solution.py:46
  27.8 3.0 %collective-permute-start.2 = (s32[32,32]{1,0:T(8,128)S(1)}, s32[32,32]{1,0:T(8,128)S(1)}, u32[]{:S(2)}, u32[]{:S(2)}) collective-permute-start(s32[32,32]{1,0:T(8,128)S(1)} %get-tuple-element.48), channel_id=1, source_target_pairs={{0,1},{1,0},{2,3},{3,2},{4,5},{5,4},{6,7},{7,6},{8,9},{9,8},{10,11... | collective-permute-start | bytes 12296 | tf_op jit(solution)/shard_map/ppermute | solution.py:446
  30.8 4.1 %collective-permute-start.3 = (s32[32,32]{1,0:T(8,128)S(1)}, s32[32,32]{1,0:T(8,128)S(1)}, u32[]{:S(2)}, u32[]{:S(2)}) collective-permute-start(s32[32,32]{1,0:T(8,128)S(1)} %add.77), channel_id=1, source_target_pairs={{0,2},{2,0},{1,3},{3,1},{4,6},{6,4},{5,7},{7,5},{8,10},{10,8},{9,1... | collective-permute-start | bytes 12296 | tf_op jit(solution)/shard_map/ppermute | solution.py:447
  33.7 11.1 %collective-permute-start.14 = (bf16[4,256,256]{2,1,0:T(8,128)(2,1)S(1)}, bf16[4,256,256]{2,1,0:T(8,128)(2,1)S(1)}, u32[]{:S(2)}, u32[]{:S(2)}) collective-permute-start(bf16[4,256,256]{2,1,0:T(8,128)(2,1)S(1)} %stack.2.refs_0_), channel_id=1, source_target_pairs={{0,24},{4,12},{8,0},{12,20},{16,8},{20,28},{24,16},{28,4},{1,25},{... | collective-permute-start | bytes 1572872 | tf_op jit(solution)/shard_map/ppermute | solution.py:46
  33.8 21.0 %collective-permute-start.15 = (bf16[4,256,256]{2,1,0:T(8,128)(2,1)S(1)}, bf16[4,256,256]{2,1,0:T(8,128)(2,1)S(1)}, u32[]{:S(2)}, u32[]{:S(2)}) collective-permute-start(bf16[4,256,256]{2,1,0:T(8,128)(2,1)S(1)} %stack.3.refs_1_), channel_id=1, source_target_pairs={{0,24},{4,12},{8,0},{12,20},{16,8},{20,28},{24,16},{28,4},{1,25},{... | collective-permute-start | bytes 1572872 | tf_op jit(solution)/shard_map/ppermute | solution.py:46
  34.9 7.2 %collective-permute-start.13 = (bf16[2,1024,128]{2,1,0:T(8,128)(2,1)S(1)}, bf16[2,1024,128]{2,1,0:T(8,128)(2,1)S(1)}, u32[]{:S(2)}, u32[]{:S(2)}) collective-permute-start(bf16[2,1024,128]{2,1,0:T(8,128)(2,1)S(1)} %get-tuple-element.49.refs_2_), channel_id=1, source_target_pairs={{0,4},{4,0},{1,5},{5,1},{2,6},{6,2},{3,7},{7,3},{8,12},{12,8},{9,1... | collective-permute-start | bytes 1572872 | tf_op jit(solution)/shard_map/ppermute | solution.py:50
  40.1 15.5 %collective-permute-start.7 = (bf16[4,256,256]{2,1,0:T(8,128)(2,1)S(1)}, bf16[4,256,256]{2,1,0:T(8,128)(2,1)S(1)}, u32[]{:S(2)}, u32[]{:S(2)}) collective-permute-start(bf16[4,256,256]{2,1,0:T(8,128)(2,1)S(1)} %collective-permute-done.6.refs_0_), channel_id=1, source_target_pairs={{0,8},{4,28},{8,16},{12,4},{16,24},{20,12},{24,0},{28,20},{1,9},{5... | collective-permute-start | bytes 1572872 | tf_op jit(solution)/shard_map/ppermute | solution.py:46
  40.8 21.4 %collective-permute-start.12 = (bf16[4,256,256]{2,1,0:T(8,128)(2,1)S(1)}, bf16[4,256,256]{2,1,0:T(8,128)(2,1)S(1)}, u32[]{:S(2)}, u32[]{:S(2)}) collective-permute-start(bf16[4,256,256]{2,1,0:T(8,128)(2,1)S(1)} %collective-permute-done.11.refs_1_), channel_id=1, source_target_pairs={{0,8},{4,28},{8,16},{12,4},{16,24},{20,12},{24,0},{28,20},{1,9},{5... | collective-permute-start | bytes 1572872 | tf_op jit(solution)/shard_map/ppermute | solution.py:46
  63.3 1.3 collective-permute-start.16
  65.7 13.1 %collective-permute-start.24 = (bf16[4,256,256]{2,1,0:T(8,128)(2,1)S(1)}, bf16[4,256,256]{2,1,0:T(8,128)(2,1)S(1)}, u32[]{:S(2)}, u32[]{:S(2)}) collective-permute-start(bf16[4,256,256]{2,1,0:T(8,128)(2,1)S(1)} %get-tuple-element.81), channel_id=1, source_target_pairs={{0,24},{4,12},{8,0},{12,20},{16,8},{20,28},{24,16},{28,4},{1,25},{... | collective-permute-start | bytes 1572872 | tf_op jit(solution)/shard_map/ppermute | solution.py:46
  66.9 23.1 %collective-permute-start.19 = (bf16[4,256,256]{2,1,0:T(8,128)(2,1)S(1)}, bf16[4,256,256]{2,1,0:T(8,128)(2,1)S(1)}, u32[]{:S(2)}, u32[]{:S(2)}) collective-permute-start(bf16[4,256,256]{2,1,0:T(8,128)(2,1)S(1)} %get-tuple-element.74), channel_id=1, source_target_pairs={{0,24},{4,12},{8,0},{12,20},{16,8},{20,28},{24,16},{28,4},{1,25},{... | collective-permute-start | bytes 1572872 | tf_op jit(solution)/shard_map/ppermute | solution.py:46
  71.6 33.4 %collective-permute-start.21 = (bf16[4,256,256]{2,1,0:T(8,128)(2,1)S(1)}, bf16[4,256,256]{2,1,0:T(8,128)(2,1)S(1)}, u32[]{:S(2)}, u32[]{:S(2)}) collective-permute-start(bf16[4,256,256]{2,1,0:T(8,128)(2,1)S(1)} %get-tuple-element.75), channel_id=1, source_target_pairs={{0,8},{4,28},{8,16},{12,4},{16,24},{20,12},{24,0},{28,20},{1,9},{5... | collective-permute-start | bytes 1572872 | tf_op jit(solution)/shard_map/ppermute | solution.py:46
  74.1 25.9 %collective-permute-start.26 = (bf16[4,256,256]{2,1,0:T(8,128)(2,1)S(1)}, bf16[4,256,256]{2,1,0:T(8,128)(2,1)S(1)}, u32[]{:S(2)}, u32[]{:S(2)}) collective-permute-start(bf16[4,256,256]{2,1,0:T(8,128)(2,1)S(1)} %get-tuple-element.82), channel_id=1, source_target_pairs={{0,8},{4,28},{8,16},{12,4},{16,24},{20,12},{24,0},{28,20},{1,9},{5... | collective-permute-start | bytes 1572872 | tf_op jit(solution)/shard_map/ppermute | solution.py:46
  78.9 21.6 %collective-permute-start.25 = (bf16[4,256,256]{2,1,0:T(8,128)(2,1)S(1)}, bf16[4,256,256]{2,1,0:T(8,128)(2,1)S(1)}, u32[]{:S(2)}, u32[]{:S(2)}) collective-permute-start(bf16[4,256,256]{2,1,0:T(8,128)(2,1)S(1)} %add_convert_fusion), channel_id=1, source_target_pairs={{0,24},{4,12},{8,0},{12,20},{16,8},{20,28},{24,16},{28,4},{1,25},{... | collective-permute-start | bytes 1572872 | tf_op jit(solution)/shard_map/ppermute | solution.py:46
  90.1 19.9 %collective-permute-start.20 = (bf16[4,256,256]{2,1,0:T(8,128)(2,1)S(1)}, bf16[4,256,256]{2,1,0:T(8,128)(2,1)S(1)}, u32[]{:S(2)}, u32[]{:S(2)}) collective-permute-start(bf16[4,256,256]{2,1,0:T(8,128)(2,1)S(1)} %add_convert_fusion.1), channel_id=1, source_target_pairs={{0,24},{4,12},{8,0},{12,20},{16,8},{20,28},{24,16},{28,4},{1,25},{... | collective-permute-start | bytes 1572872 | tf_op jit(solution)/shard_map/ppermute | solution.py:46
  90.2 32.9 %collective-permute-start.17 = (f32[128,1024]{1,0:T(8,128)S(1)}, f32[128,1024]{1,0:T(8,128)S(1)}, u32[]{:S(2)}, u32[]{:S(2)}) collective-permute-start(f32[128,1024]{1,0:T(8,128)S(1)} %get-tuple-element.61), channel_id=1, source_target_pairs={{0,4},{4,0},{1,5},{5,1},{2,6},{6,2},{3,7},{7,3},{8,12},{12,8},{9,1... | collective-permute-start | bytes 1572872 | tf_op jit(solution)/shard_map/ppermute | solution.py:50
  100.1 23.1 %collective-permute-start.18 = (f32[128,1024]{1,0:T(8,128)S(1)}, f32[128,1024]{1,0:T(8,128)S(1)}, u32[]{:S(2)}, u32[]{:S(2)}) collective-permute-start(f32[128,1024]{1,0:T(8,128)S(1)} %get-tuple-element.69), channel_id=1, source_target_pairs={{0,4},{4,0},{1,5},{5,1},{2,6},{6,2},{3,7},{7,3},{8,12},{12,8},{9,1... | collective-permute-start | bytes 1572872 | tf_op jit(solution)/shard_map/ppermute | solution.py:50
  100.7 13.6 %collective-permute-start.27 = (bf16[256,256]{1,0:T(8,128)(2,1)S(1)}, bf16[256,256]{1,0:T(8,128)(2,1)S(1)}, u32[]{:S(2)}, u32[]{:S(2)}) collective-permute-start(bf16[256,256]{1,0:T(8,128)(2,1)S(1)} %get-tuple-element.85), channel_id=1, source_target_pairs={{0,224},{4,36},{32,0},{36,68},{64,32},{68,100},{96,64},{100,132},{... | collective-permute-start | bytes 393224 | tf_op jit(solution)/shard_map/ppermute | solution.py:46
  105.0 14.0 %collective-permute-start.28 = (bf16[256,256]{1,0:T(8,128)(2,1)S(1)}, bf16[256,256]{1,0:T(8,128)(2,1)S(1)}, u32[]{:S(2)}, u32[]{:S(2)}) collective-permute-start(bf16[256,256]{1,0:T(8,128)(2,1)S(1)} %get-tuple-element.86), channel_id=1, source_target_pairs={{0,192},{4,68},{32,224},{36,100},{64,0},{68,132},{96,32},{100,164}... | collective-permute-start | bytes 393224 | tf_op jit(solution)/shard_map/ppermute | solution.py:46
  110.0 9.4 %collective-permute-start.29 = (bf16[256,256]{1,0:T(8,128)(2,1)S(1)}, bf16[256,256]{1,0:T(8,128)(2,1)S(1)}, u32[]{:S(2)}, u32[]{:S(2)}) collective-permute-start(bf16[256,256]{1,0:T(8,128)(2,1)S(1)} %get-tuple-element.87), channel_id=1, source_target_pairs={{0,32},{4,228},{32,64},{36,4},{64,96},{68,36},{96,128},{100,68},{1... | collective-permute-start | bytes 393224 | tf_op jit(solution)/shard_map/ppermute | solution.py:46
  114.3 10.0 %collective-permute-start.22 = (bf16[256,256]{1,0:T(8,128)(2,1)S(1)}, bf16[256,256]{1,0:T(8,128)(2,1)S(1)}, u32[]{:S(2)}, u32[]{:S(2)}) collective-permute-start(bf16[256,256]{1,0:T(8,128)(2,1)S(1)} %get-tuple-element.77), channel_id=1, source_target_pairs={{0,224},{4,36},{32,0},{36,68},{64,32},{68,100},{96,64},{100,132},{... | collective-permute-start | bytes 393224 | tf_op jit(solution)/shard_map/ppermute | solution.py:46
  119.0 5.2 %collective-permute-start.23 = (bf16[256,256]{1,0:T(8,128)(2,1)S(1)}, bf16[256,256]{1,0:T(8,128)(2,1)S(1)}, u32[]{:S(2)}, u32[]{:S(2)}) collective-permute-start(bf16[256,256]{1,0:T(8,128)(2,1)S(1)} %get-tuple-element.78), channel_id=1, source_target_pairs={{0,32},{4,228},{32,64},{36,4},{64,96},{68,36},{96,128},{100,68},{1... | collective-permute-start | bytes 393224 | tf_op jit(solution)/shard_map/ppermute | solution.py:46
  119.5 8.5 %collective-permute-start.30 = (bf16[256,256]{1,0:T(8,128)(2,1)S(1)}, bf16[256,256]{1,0:T(8,128)(2,1)S(1)}, u32[]{:S(2)}, u32[]{:S(2)}) collective-permute-start(bf16[256,256]{1,0:T(8,128)(2,1)S(1)} %get-tuple-element.88), channel_id=1, source_target_pairs={{0,64},{4,196},{32,96},{36,228},{64,128},{68,4},{96,160},{100,36},... | collective-permute-start | bytes 393224 | tf_op jit(solution)/shard_map/ppermute | solution.py:46
  123.2 6.5 %collective-permute-start.31 = (bf16[256,256]{1,0:T(8,128)(2,1)S(1)}, bf16[256,256]{1,0:T(8,128)(2,1)S(1)}, u32[]{:S(2)}, u32[]{:S(2)}) collective-permute-start(bf16[256,256]{1,0:T(8,128)(2,1)S(1)} %get-tuple-element.89), channel_id=1, source_target_pairs={{0,192},{4,68},{32,224},{36,100},{64,0},{68,132},{96,32},{100,164}... | collective-permute-start | bytes 393224 | tf_op jit(solution)/shard_map/ppermute | solution.py:46

commit v2 on v1

--- a/solution.py
+++ b/solution.py
@@ -333,24 +333,24 @@
     )(k, v)
 
 
-def prepare_kernel(query, grad_out, gate, after, qg_ref, gate_ref):
+def prepare_kernel(query, grad_out, after, qg_ref):
     for h in range(GROUP):
         rows = slice(h * HALF, (h + 1) * HALF)
         cols = slice(h * HEAD_DIM, (h + 1) * HEAD_DIM)
         qg_ref[0, rows, :] = query[:, cols]
         qg_ref[1, rows, :] = grad_out[:, cols]
-    gate_ref[...] = gate[...]
-
-
-def prepare(query, grad_out, gate, after):
+
+
+def prepare(query, grad_out, after):
     return pl.pallas_call(
         prepare_kernel,
-        in_specs=[VMEM] * 3 + [pl.BlockSpec(memory_space=pl.ANY)],
-        out_specs=[VMEM] * 2,
-        out_shape=[jax.ShapeDtypeStruct(PAIR, BF), jax.ShapeDtypeStruct(gate.shape, jnp.int32)],
+        in_specs=[VMEM] * 2 + [pl.BlockSpec(memory_space=pl.ANY)],
+        out_specs=VMEM,
+        out_shape=jax.ShapeDtypeStruct(PAIR, BF),
         cost_estimate=cost(100_000_000),
-        compiler_params=SMALL, name="prepare",
-    )(query, grad_out, gate, after)
+        compiler_params=SMALL,
+        name="prepare",
+    )(query, grad_out, after)
 
 
 def stack_kernel(*refs):
@@ -471,19 +471,20 @@
     low2, high2 = shift(low1, "x", 1), shift(high1, "x", 1)
     low3, high3 = shift(low0, "x", -1), shift(high0, "x", -1)
 
-    qg, gate = prepare(query, grad_out, gate_score[0], a3)
-    info = plan(gate)
+    qg = prepare(query, grad_out, a3)
+    info = plan(gate_score[0])
     qg = (qg, swap(qg))
 
-    state = forward(0, info, [low0, high0], qg, None, False)
-    state = forward(8, info, [low1, high1], qg, state, False)
+    state = forward(0, info, [low0, high0, low1, high1], qg, None, False)
     state = forward(24, info, [low3, high3], qg, state, False)
     mine, acc, acc_away = forward(16, info, [low2, high2], qg, state, True)
     other = swap(mine)
     acc_other = swap(acc_away)
 
-    dq, (low2, high2) = backward(16, info, [low2, high2], qg, mine, other, None)
-    high2, low2 = shift(high2, "x", -1), shift(low2, "x", -1)
+    dq, (high2,) = backward(20, info, [high2], qg, mine, other, None)
+    high2 = shift(high2, "x", -1)
+    dq, (low2,) = backward(16, info, [low2], qg, mine, other, dq)
+    low2 = shift(low2, "x", -1)
     dq, (low3, high3) = backward(24, info, [low3, high3], qg, mine, other, dq)
     high3, low3 = shift(high3, "x", 1), shift(low3, "x", 1)
     dq, (low1, high1) = backward(8, info, [low1, high1], qg, mine, other, dq)

time: 130 us -> 131 us (level)
  the two profiles are of different devices: /device:TPU:1 before, /device:TPU:8 now
where the time goes in v2:
time: 131 us; the launch traced here: 130 us
  starting transfers between devices  60.1 us (46%)
  waiting for transfers between devices  52.7 us (40%)
  Pallas kernels  14.5 us (11%)
    ppermute x26, starting transfers between devices, shift(): lax.ppermute(a, (axis, 'core'), [(2 * i + c, 2 * ((i + d * (1 - 2 * c)) %...  56.3 us
    ppermute x26, waiting for transfers between devices, shift(): lax.ppermute(a, (axis, 'core'), [(2 * i + c, 2 * ((i + d * (1 - 2 * c)) %...  48.7 us
    pallas_call x5, Pallas kernels, backward(): pl.pallas_call(functools.partial(backward_kernel, base, n, first, base ==...  6.45 us
    pallas_call x3, Pallas kernels, forward(): pl.pallas_call(functools.partial(forward_kernel, base, n, first, last), g...  4.21 us
    ppermute x1, waiting for transfers between devices, plan(): lax.ppermute(totals, 'head', [(0, 2), (2, 0), (1, 3), (3, 1)])  2.96 us
  transfers between devices with their start and end apart: 32, of which 17 were waited for; matrix products, arithmetic and copies ran while one was open for 1% of the time, Pallas kernels for 8%

profile of v2, /device:TPU:8, one launch (start us, length us, event | category | flops | bytes accessed | tf_op | source)
XLA Modules:
  0.0 129.8 jit_solution(16788335583681323651)
XLA Ops:
  0.6 1.5 %join.1.refs_0_ = bf16[256,256]{1,0:T(8,128)(2,1)} custom-call(bf16[256,128]{1,0:T(8,128)(2,1)} %k_ref.1, bf16[256,128]{1,0:T(8,128)(2,1)} %v_ref.1), custom_call_target="tpu_custom_call" | custom-call | tf_op jit(solution)/shard_map/join/pallas_call | solution.py:326
  2.2 6.4 %collective-permute-start.7 = (bf16[256,256]{1,0:T(8,128)(2,1)}, bf16[256,256]{1,0:T(8,128)(2,1)S(1)}, u32[]{:S(2)}, u32[]{:S(2)}) collective-permute-start(bf16[256,256]{1,0:T(8,128)(2,1)} %join.1.refs_0_), channel_id=1, source_target_pairs={{0,192},{4,68},{32,224},{36,100},{64,0},{68,132},{96,32},{100,164}... | collective-permute-start | bytes 393224 | tf_op jit(solution)/shard_map/ppermute | solution.py:46
  8.6 3.7 %collective-permute-start.3 = (bf16[256,256]{1,0:T(8,128)(2,1)}, bf16[256,256]{1,0:T(8,128)(2,1)S(1)}, u32[]{:S(2)}, u32[]{:S(2)}) collective-permute-start(bf16[256,256]{1,0:T(8,128)(2,1)} %join.1.refs_0_), channel_id=1, source_target_pairs={{0,224},{4,36},{32,0},{36,68},{64,32},{68,100},{96,64},{100,132},{... | collective-permute-start | bytes 393224 | tf_op jit(solution)/shard_map/ppermute | solution.py:46
  12.3 2.7 %collective-permute-done.7.refs_0_ = bf16[256,256]{1,0:T(8,128)(2,1)S(1)} collective-permute-done((bf16[256,256]{1,0:T(8,128)(2,1)}, bf16[256,256]{1,0:T(8,128)(2,1)S(1)}, u32[]{:S(2)}, u32[]{:S(2)}) %collective-permute-start.7) | collective-permute-done | bytes 131104 | tf_op jit(solution)/shard_map/ppermute | solution.py:46
  15.0 2.7 %collective-permute-start.9 = (bf16[256,256]{1,0:T(8,128)(2,1)S(1)}, bf16[256,256]{1,0:T(8,128)(2,1)S(1)}, u32[]{:S(2)}, u32[]{:S(2)}) collective-permute-start(bf16[256,256]{1,0:T(8,128)(2,1)S(1)} %collective-permute-done.7.refs_0_), channel_id=1, source_target_pairs={{0,224},{4,36},{32,0},{36,68},{64,32},{68,100},{96,64},{100,132},{... | collective-permute-start | bytes 393224 | tf_op jit(solution)/shard_map/ppermute | solution.py:46
  17.7 0.3 collective-permute-done.4.refs_3_
  18.0 1.1 collective-permute-start
  19.2 0.5 collective-permute-done.2.refs_1_
  19.6 0.9 copy-done
  20.6 0.0 copy-start.1
  20.6 0.0 copy-start.2
  20.6 1.6 %collective-permute-start.5 = (bf16[4,256,256]{2,1,0:T(8,128)(2,1)S(1)}, bf16[4,256,256]{2,1,0:T(8,128)(2,1)S(1)}, u32[]{:S(2)}, u32[]{:S(2)}) collective-permute-start(bf16[4,256,256]{2,1,0:T(8,128)(2,1)S(1)} %stack.2.refs_0_), channel_id=1, source_target_pairs={{0,8},{4,28},{8,16},{12,4},{16,24},{20,12},{24,0},{28,20},{1,9},{5... | collective-permute-start | bytes 1572872 | tf_op jit(solution)/shard_map/ppermute | solution.py:46
  22.2 0.5 collective-permute-done.9.refs_2_
  22.6 3.9 %collective-permute-done.10.refs_3_ = bf16[256,256]{1,0:T(8,128)(2,1)S(1)} collective-permute-done((bf16[256,256]{1,0:T(8,128)(2,1)S(1)}, bf16[256,256]{1,0:T(8,128)(2,1)S(1)}, u32[]{:S(2)}, u32[]{:S(2)}) %collective-permute-start.10) | collective-permute-done | bytes 131104 | tf_op jit(solution)/shard_map/ppermute | solution.py:46
  26.5 1.6 %collective-permute-start.11 = (bf16[4,256,256]{2,1,0:T(8,128)(2,1)S(1)}, bf16[4,256,256]{2,1,0:T(8,128)(2,1)S(1)}, u32[]{:S(2)}, u32[]{:S(2)}) collective-permute-start(bf16[4,256,256]{2,1,0:T(8,128)(2,1)S(1)} %stack.3.refs_1_), channel_id=1, source_target_pairs={{0,8},{4,28},{8,16},{12,4},{16,24},{20,12},{24,0},{28,20},{1,9},{5... | collective-permute-start | bytes 1572872 | tf_op jit(solution)/shard_map/ppermute | solution.py:46
  28.1 2.3 %collective-permute-start.1 = (s32[32,32]{1,0:T(8,128)S(1)}, s32[32,32]{1,0:T(8,128)S(1)}, u32[]{:S(2)}, u32[]{:S(2)}) collective-permute-start(s32[32,32]{1,0:T(8,128)S(1)} %bitcast_add_fusion.1), channel_id=1, source_target_pairs={{0,2},{2,0},{1,3},{3,1},{4,6},{6,4},{5,7},{7,5},{8,10},{10,8},{9,1... | collective-permute-start | bytes 12296 | tf_op jit(solution)/shard_map/ppermute | solution.py:447
  30.5 3.0 %collective-permute-done.1 = s32[32,32]{1,0:T(8,128)S(1)} collective-permute-done((s32[32,32]{1,0:T(8,128)S(1)}, s32[32,32]{1,0:T(8,128)S(1)}, u32[]{:S(2)}, u32[]{:S(2)}) %collective-permute-start.1) | collective-permute-done | bytes 4128 | tf_op jit(solution)/shard_map/ppermute | solution.py:447
  33.5 1.8 %collective-permute-start.14 = (bf16[4,256,256]{2,1,0:T(8,128)(2,1)S(1)}, bf16[4,256,256]{2,1,0:T(8,128)(2,1)S(1)}, u32[]{:S(2)}, u32[]{:S(2)}) collective-permute-start(bf16[4,256,256]{2,1,0:T(8,128)(2,1)S(1)} %stack.2.refs_0_), channel_id=1, source_target_pairs={{0,24},{4,12},{8,0},{12,20},{16,8},{20,28},{24,16},{28,4},{1,25},{... | collective-permute-start | bytes 1572872 | tf_op jit(solution)/shard_map/ppermute | solution.py:46
  35.3 1.5 %collective-permute-start.15 = (bf16[4,256,256]{2,1,0:T(8,128)(2,1)S(1)}, bf16[4,256,256]{2,1,0:T(8,128)(2,1)S(1)}, u32[]{:S(2)}, u32[]{:S(2)}) collective-permute-start(bf16[4,256,256]{2,1,0:T(8,128)(2,1)S(1)} %stack.3.refs_1_), channel_id=1, source_target_pairs={{0,24},{4,12},{8,0},{12,20},{16,8},{20,28},{24,16},{28,4},{1,25},{... | collective-permute-start | bytes 1572872 | tf_op jit(solution)/shard_map/ppermute | solution.py:46
  36.8 0.1 prepare.1.refs_4_.refs_2_.refs_1_
  36.9 0.1 collective-permute-start.13
  37.0 0.6 collective-permute-start.6
  37.6 1.3 collective-permute-done.11.refs_3_.refs_1_
  38.9 1.9 %collective-permute-start.12 = (bf16[4,256,256]{2,1,0:T(8,128)(2,1)S(1)}, bf16[4,256,256]{2,1,0:T(8,128)(2,1)S(1)}, u32[]{:S(2)}, u32[]{:S(2)}) collective-permute-start(bf16[4,256,256]{2,1,0:T(8,128)(2,1)S(1)} %collective-permute-done.11.refs_3_.refs_1_), channel_id=1, source_target_pairs={{0,8},{4,28},{8,16},{12,4},{16,24},{20,12},{24,0},{28,20},{1,9},{5... | collective-permute-start | bytes 1572872 | tf_op jit(solution)/shard_map/ppermute | solution.py:46
  40.7 0.2 convert_reduce_fusion.1
  40.9 0.1 convert_reduce_fusion
  41.0 0.1 pad_add_fusion.info
  41.1 2.2 %forward.3 = (f32[2,3,1024]{2,1,0:T(4,128)S(1)}, f32[128,1024]{1,0:T(8,128)S(1)}, f32[128,1024]{1,0:T(8,128)S(1)}) custom-call(s32[33]{0:T(128)S(1)} %pad_add_fusion.info, bf16[4,256,256]{2,1,0:T(8,128)(2,1)S(1)} %stack.2.refs_0_, bf16[4,256,256]{2,1,0:T(8,128)(2,1)S(1)} %stack.3.refs_1_, bf16[4,256,256]{2,1,0:T(8,128)(2,1)S(1)} %collective-permute-done.5.refs_2_.refs_0_, ...), custom_call_target="tpu_custom_call" | custom-call | flops 200000000 | bytes 65536 | tf_op jit(solution)/shard_map/forward/pallas_call | solution.py:244
  43.3 2.1 %collective-permute-done.14.refs_0_ = bf16[4,256,256]{2,1,0:T(8,128)(2,1)S(1)} collective-permute-done((bf16[4,256,256]{2,1,0:T(8,128)(2,1)S(1)}, bf16[4,256,256]{2,1,0:T(8,128)(2,1)S(1)}, u32[]{:S(2)}, u32[]{:S(2)}) %collective-permute-start.14) | collective-permute-done | bytes 524320 | tf_op jit(solution)/shard_map/ppermute | solution.py:46
  45.4 11.2 %collective-permute-done.15.refs_1_ = bf16[4,256,256]{2,1,0:T(8,128)(2,1)S(1)} collective-permute-done((bf16[4,256,256]{2,1,0:T(8,128)(2,1)S(1)}, bf16[4,256,256]{2,1,0:T(8,128)(2,1)S(1)}, u32[]{:S(2)}, u32[]{:S(2)}) %collective-permute-start.15) | collective-permute-done | bytes 524320 | tf_op jit(solution)/shard_map/ppermute | solution.py:46
  56.7 0.8 forward.4
  57.5 2.0 %collective-permute-done.12.refs_1_.refs_0_ = bf16[4,256,256]{2,1,0:T(8,128)(2,1)S(1)} collective-permute-done((bf16[4,256,256]{2,1,0:T(8,128)(2,1)S(1)}, bf16[4,256,256]{2,1,0:T(8,128)(2,1)S(1)}, u32[]{:S(2)}, u32[]{:S(2)}) %collective-permute-start.12) | collective-permute-done | bytes 524320 | tf_op jit(solution)/shard_map/ppermute | solution.py:46
  59.5 1.2 forward.5
  60.6 0.2 collective-permute-start.16
  60.8 1.1 collective-permute-done.16.refs_4_.refs_5_.other
  61.9 0.8 backward.5
  62.8 4.0 %collective-permute-start.24 = (bf16[4,256,256]{2,1,0:T(8,128)(2,1)S(1)}, bf16[4,256,256]{2,1,0:T(8,128)(2,1)S(1)}, u32[]{:S(2)}, u32[]{:S(2)}) collective-permute-start(bf16[4,256,256]{2,1,0:T(8,128)(2,1)S(1)} %get-tuple-element.75), channel_id=1, source_target_pairs={{0,24},{4,12},{8,0},{12,20},{16,8},{20,28},{24,16},{28,4},{1,25},{... | collective-permute-start | bytes 1572872 | tf_op jit(solution)/shard_map/ppermute | solution.py:46
  66.7 0.8 backward.6
  67.6 1.9 %collective-permute-start.19 = (bf16[4,256,256]{2,1,0:T(8,128)(2,1)S(1)}, bf16[4,256,256]{2,1,0:T(8,128)(2,1)S(1)}, u32[]{:S(2)}, u32[]{:S(2)}) collective-permute-start(bf16[4,256,256]{2,1,0:T(8,128)(2,1)S(1)} %get-tuple-element.68), channel_id=1, source_target_pairs={{0,24},{4,12},{8,0},{12,20},{16,8},{20,28},{24,16},{28,4},{1,25},{... | collective-permute-start | bytes 1572872 | tf_op jit(solution)/shard_map/ppermute | solution.py:46
  69.5 1.1 backward.7
  70.6 0.2 collective-permute-start.21
  70.8 0.3 collective-permute-start.26
  71.1 1.1 backward.8
  72.2 2.4 %collective-permute-done.24 = bf16[4,256,256]{2,1,0:T(8,128)(2,1)S(1)} collective-permute-done((bf16[4,256,256]{2,1,0:T(8,128)(2,1)S(1)}, bf16[4,256,256]{2,1,0:T(8,128)(2,1)S(1)}, u32[]{:S(2)}, u32[]{:S(2)}) %collective-permute-start.24) | collective-permute-done | bytes 524320 | tf_op jit(solution)/shard_map/ppermute | solution.py:46
  74.6 0.1 add_convert_fusion
  74.7 3.8 %collective-permute-start.25 = (bf16[4,256,256]{2,1,0:T(8,128)(2,1)S(1)}, bf16[4,256,256]{2,1,0:T(8,128)(2,1)S(1)}, u32[]{:S(2)}, u32[]{:S(2)}) collective-permute-start(bf16[4,256,256]{2,1,0:T(8,128)(2,1)S(1)} %add_convert_fusion), channel_id=1, source_target_pairs={{0,24},{4,12},{8,0},{12,20},{16,8},{20,28},{24,16},{28,4},{1,25},{... | collective-permute-start | bytes 1572872 | tf_op jit(solution)/shard_map/ppermute | solution.py:46
  78.5 7.3 %collective-permute-done.19 = bf16[4,256,256]{2,1,0:T(8,128)(2,1)S(1)} collective-permute-done((bf16[4,256,256]{2,1,0:T(8,128)(2,1)S(1)}, bf16[4,256,256]{2,1,0:T(8,128)(2,1)S(1)}, u32[]{:S(2)}, u32[]{:S(2)}) %collective-permute-start.19) | collective-permute-done | bytes 524320 | tf_op jit(solution)/shard_map/ppermute | solution.py:46
  85.8 0.1 add_convert_fusion.1
  86.0 3.8 %collective-permute-start.20 = (bf16[4,256,256]{2,1,0:T(8,128)(2,1)S(1)}, bf16[4,256,256]{2,1,0:T(8,128)(2,1)S(1)}, u32[]{:S(2)}, u32[]{:S(2)}) collective-permute-start(bf16[4,256,256]{2,1,0:T(8,128)(2,1)S(1)} %add_convert_fusion.1), channel_id=1, source_target_pairs={{0,24},{4,12},{8,0},{12,20},{16,8},{20,28},{24,16},{28,4},{1,25},{... | collective-permute-start | bytes 1572872 | tf_op jit(solution)/shard_map/ppermute | solution.py:46
  89.7 2.7 %backward.9 = (f32[128,1024]{1,0:T(8,128)S(1)}, f32[128,1024]{1,0:T(8,128)S(1)}, bf16[4,256,256]{2,1,0:T(8,128)(2,1)S(1)}, bf16[4,256,256]{2,1,0:T(8,128)(2,1)S(1)}) custom-call(s32[33]{0:T(128)S(1)} %pad_add_fusion.info, bf16[4,256,256]{2,1,0:T(8,128)(2,1)S(1)} %stack.2.refs_0_, bf16[4,256,256]{2,1,0:T(8,128)(2,1)S(1)} %stack.3.refs_1_, ...), custom_call_target="tpu_custom_call" | custom-call | flops 200000000 | bytes 65536 | tf_op jit(solution)/shard_map/backward/pallas_call | solution.py:272
  92.5 5.5 %collective-permute-done.26.three = bf16[4,256,256]{2,1,0:T(8,128)(2,1)S(1)} collective-permute-done((bf16[4,256,256]{2,1,0:T(8,128)(2,1)S(1)}, bf16[4,256,256]{2,1,0:T(8,128)(2,1)S(1)}, u32[]{:S(2)}, u32[]{:S(2)}) %collective-permute-start.26) | collective-permute-done | bytes 524320 | tf_op jit(solution)/shard_map/ppermute | solution.py:46
  98.0 0.2 sum_high.1
  98.2 11.0 %collective-permute-start.27 = (bf16[256,256]{1,0:T(8,128)(2,1)S(1)}, bf16[256,256]{1,0:T(8,128)(2,1)S(1)}, u32[]{:S(2)}, u32[]{:S(2)}) collective-permute-start(bf16[256,256]{1,0:T(8,128)(2,1)S(1)} %get-tuple-element.79), channel_id=1, source_target_pairs={{0,224},{4,36},{32,0},{36,68},{64,32},{68,100},{96,64},{100,132},{... | collective-permute-start | bytes 393224 | tf_op jit(solution)/shard_map/ppermute | solution.py:46
  109.2 1.6 %collective-permute-start.29 = (bf16[256,256]{1,0:T(8,128)(2,1)S(1)}, bf16[256,256]{1,0:T(8,128)(2,1)S(1)}, u32[]{:S(2)}, u32[]{:S(2)}) collective-permute-start(bf16[256,256]{1,0:T(8,128)(2,1)S(1)} %get-tuple-element.81), channel_id=1, source_target_pairs={{0,32},{4,228},{32,64},{36,4},{64,96},{68,36},{96,128},{100,68},{1... | collective-permute-start | bytes 393224 | tf_op jit(solution)/shard_map/ppermute | solution.py:46
  110.7 0.2 sum_low.1
  110.9 2.2 %collective-permute-done.27.down = bf16[256,256]{1,0:T(8,128)(2,1)S(1)} collective-permute-done((bf16[256,256]{1,0:T(8,128)(2,1)S(1)}, bf16[256,256]{1,0:T(8,128)(2,1)S(1)}, u32[]{:S(2)}, u32[]{:S(2)}) %collective-permute-start.27) | collective-permute-done | bytes 131104 | tf_op jit(solution)/shard_map/ppermute | solution.py:46
  113.1 3.8 %collective-permute-start.22 = (bf16[256,256]{1,0:T(8,128)(2,1)S(1)}, bf16[256,256]{1,0:T(8,128)(2,1)S(1)}, u32[]{:S(2)}, u32[]{:S(2)}) collective-permute-start(bf16[256,256]{1,0:T(8,128)(2,1)S(1)} %get-tuple-element.71), channel_id=1, source_target_pairs={{0,224},{4,36},{32,0},{36,68},{64,32},{68,100},{96,64},{100,132},{... | collective-permute-start | bytes 393224 | tf_op jit(solution)/shard_map/ppermute | solution.py:46
  117.0 0.1 sum_two.1
  117.0 0.1 collective-permute-start.30
  117.2 4.1 %collective-permute-start.31 = (bf16[256,256]{1,0:T(8,128)(2,1)S(1)}, bf16[256,256]{1,0:T(8,128)(2,1)S(1)}, u32[]{:S(2)}, u32[]{:S(2)}) collective-permute-start(bf16[256,256]{1,0:T(8,128)(2,1)S(1)} %get-tuple-element.83), channel_id=1, source_target_pairs={{0,192},{4,68},{32,224},{36,100},{64,0},{68,132},{96,32},{100,164}... | collective-permute-start | bytes 393224 | tf_op jit(solution)/shard_map/ppermute | solution.py:46
  121.3 1.0 finish.1
  122.3 1.0 collective-permute-done.23.b
  123.3 5.8 %collective-permute-done.30.c = bf16[256,256]{1,0:T(8,128)(2,1)S(1)} collective-permute-done((bf16[256,256]{1,0:T(8,128)(2,1)S(1)}, bf16[256,256]{1,0:T(8,128)(2,1)S(1)}, u32[]{:S(2)}, u32[]{:S(2)}) %collective-permute-start.30) | collective-permute-done | bytes 131104 | tf_op jit(solution)/shard_map/ppermute | solution.py:46
  129.1 0.7 close.1
  (35 shorter events, 0.2 us)
Async XLA Ops:
  0.6 17.4 %copy-start.3 = (s32[1,32,32]{2,1,0:T(8,128)S(1)}, s32[1,32,32]{2,1,0:T(8,128)}, u32[]{:S(2)}) copy-start(s32[1,32,32]{2,1,0:T(8,128)} %param.9) | copy-start | bytes 12292
  2.2 12.8 %collective-permute-start.7 = (bf16[256,256]{1,0:T(8,128)(2,1)}, bf16[256,256]{1,0:T(8,128)(2,1)S(1)}, u32[]{:S(2)}, u32[]{:S(2)}) collective-permute-start(bf16[256,256]{1,0:T(8,128)(2,1)} %join.1.refs_0_), channel_id=1, source_target_pairs={{0,192},{4,68},{32,224},{36,100},{64,0},{68,132},{96,32},{100,164}... | collective-permute-start | bytes 393224 | tf_op jit(solution)/shard_map/ppermute | solution.py:46
  8.6 9.4 %collective-permute-start.4 = (bf16[256,256]{1,0:T(8,128)(2,1)}, bf16[256,256]{1,0:T(8,128)(2,1)S(1)}, u32[]{:S(2)}, u32[]{:S(2)}) collective-permute-start(bf16[256,256]{1,0:T(8,128)(2,1)} %join.1.refs_0_), channel_id=1, source_target_pairs={{0,64},{4,196},{32,96},{36,228},{64,128},{68,4},{96,160},{100,36},... | collective-permute-start | bytes 393224 | tf_op jit(solution)/shard_map/ppermute | solution.py:46
  8.6 9.4 %collective-permute-start.3 = (bf16[256,256]{1,0:T(8,128)(2,1)}, bf16[256,256]{1,0:T(8,128)(2,1)S(1)}, u32[]{:S(2)}, u32[]{:S(2)}) collective-permute-start(bf16[256,256]{1,0:T(8,128)(2,1)} %join.1.refs_0_), channel_id=1, source_target_pairs={{0,224},{4,36},{32,0},{36,68},{64,32},{68,100},{96,64},{100,132},{... | collective-permute-start | bytes 393224 | tf_op jit(solution)/shard_map/ppermute | solution.py:46
  12.3 7.4 %collective-permute-start.2 = (bf16[256,256]{1,0:T(8,128)(2,1)}, bf16[256,256]{1,0:T(8,128)(2,1)S(1)}, u32[]{:S(2)}, u32[]{:S(2)}) collective-permute-start(bf16[256,256]{1,0:T(8,128)(2,1)} %join.1.refs_0_), channel_id=1, source_target_pairs={{0,32},{4,228},{32,64},{36,4},{64,96},{68,36},{96,128},{100,68},{1... | collective-permute-start | bytes 393224 | tf_op jit(solution)/shard_map/ppermute | solution.py:46
  15.0 7.7 %collective-permute-start.9 = (bf16[256,256]{1,0:T(8,128)(2,1)S(1)}, bf16[256,256]{1,0:T(8,128)(2,1)S(1)}, u32[]{:S(2)}, u32[]{:S(2)}) collective-permute-start(bf16[256,256]{1,0:T(8,128)(2,1)S(1)} %collective-permute-done.7.refs_0_), channel_id=1, source_target_pairs={{0,224},{4,36},{32,0},{36,68},{64,32},{68,100},{96,64},{100,132},{... | collective-permute-start | bytes 393224 | tf_op jit(solution)/shard_map/ppermute | solution.py:46
  18.0 8.5 %collective-permute-start.10 = (bf16[256,256]{1,0:T(8,128)(2,1)S(1)}, bf16[256,256]{1,0:T(8,128)(2,1)S(1)}, u32[]{:S(2)}, u32[]{:S(2)}) collective-permute-start(bf16[256,256]{1,0:T(8,128)(2,1)S(1)} %collective-permute-done.4.refs_3_), channel_id=1, source_target_pairs={{0,64},{4,196},{32,96},{36,228},{64,128},{68,4},{96,160},{100,36},... | collective-permute-start | bytes 393224 | tf_op jit(solution)/shard_map/ppermute | solution.py:46
  18.0 8.5 %collective-permute-start.8 = (bf16[256,256]{1,0:T(8,128)(2,1)S(1)}, bf16[256,256]{1,0:T(8,128)(2,1)S(1)}, u32[]{:S(2)}, u32[]{:S(2)}) collective-permute-start(bf16[256,256]{1,0:T(8,128)(2,1)S(1)} %collective-permute-done.4.refs_3_), channel_id=1, source_target_pairs={{0,32},{4,228},{32,64},{36,4},{64,96},{68,36},{96,128},{100,68},{1... | collective-permute-start | bytes 393224 | tf_op jit(solution)/shard_map/ppermute | solution.py:46
  18.0 10.1 %collective-permute-start = (s32[32,32]{1,0:T(8,128)S(1)}, s32[32,32]{1,0:T(8,128)S(1)}, u32[]{:S(2)}, u32[]{:S(2)}) collective-permute-start(s32[32,32]{1,0:T(8,128)S(1)} %bitcast.17), channel_id=1, source_target_pairs={{0,1},{1,0},{2,3},{3,2},{4,5},{5,4},{6,7},{7,6},{8,9},{9,8},{10,11... | collective-permute-start | bytes 12296 | tf_op jit(solution)/shard_map/ppermute | solution.py:446
  19.6 0.9 copy-start
  20.6 16.3 %copy-start.1 = (bf16[256,512]{1,0:T(8,128)(2,1)S(1)}, bf16[256,512]{1,0:T(8,128)(2,1)}, u32[]{:S(2)}) copy-start(bf16[256,512]{1,0:T(8,128)(2,1)} %query.1) | copy-start | bytes 786436
  20.6 16.3 %copy-start.2 = (bf16[256,512]{1,0:T(8,128)(2,1)S(1)}, bf16[256,512]{1,0:T(8,128)(2,1)}, u32[]{:S(2)}) copy-start(bf16[256,512]{1,0:T(8,128)(2,1)} %grad_out.1) | copy-start | bytes 786436
  20.6 16.4 %collective-permute-start.5 = (bf16[4,256,256]{2,1,0:T(8,128)(2,1)S(1)}, bf16[4,256,256]{2,1,0:T(8,128)(2,1)S(1)}, u32[]{:S(2)}, u32[]{:S(2)}) collective-permute-start(bf16[4,256,256]{2,1,0:T(8,128)(2,1)S(1)} %stack.2.refs_0_), channel_id=1, source_target_pairs={{0,8},{4,28},{8,16},{12,4},{16,24},{20,12},{24,0},{28,20},{1,9},{5... | collective-permute-start | bytes 1572872 | tf_op jit(solution)/shard_map/ppermute | solution.py:46
  26.5 12.3 %collective-permute-start.11 = (bf16[4,256,256]{2,1,0:T(8,128)(2,1)S(1)}, bf16[4,256,256]{2,1,0:T(8,128)(2,1)S(1)}, u32[]{:S(2)}, u32[]{:S(2)}) collective-permute-start(bf16[4,256,256]{2,1,0:T(8,128)(2,1)S(1)} %stack.3.refs_1_), channel_id=1, source_target_pairs={{0,8},{4,28},{8,16},{12,4},{16,24},{20,12},{24,0},{28,20},{1,9},{5... | collective-permute-start | bytes 1572872 | tf_op jit(solution)/shard_map/ppermute | solution.py:46
  28.1 5.3 %collective-permute-start.1 = (s32[32,32]{1,0:T(8,128)S(1)}, s32[32,32]{1,0:T(8,128)S(1)}, u32[]{:S(2)}, u32[]{:S(2)}) collective-permute-start(s32[32,32]{1,0:T(8,128)S(1)} %bitcast_add_fusion.1), channel_id=1, source_target_pairs={{0,2},{2,0},{1,3},{3,1},{4,6},{6,4},{5,7},{7,5},{8,10},{10,8},{9,1... | collective-permute-start | bytes 12296 | tf_op jit(solution)/shard_map/ppermute | solution.py:447
  33.5 12.0 %collective-permute-start.14 = (bf16[4,256,256]{2,1,0:T(8,128)(2,1)S(1)}, bf16[4,256,256]{2,1,0:T(8,128)(2,1)S(1)}, u32[]{:S(2)}, u32[]{:S(2)}) collective-permute-start(bf16[4,256,256]{2,1,0:T(8,128)(2,1)S(1)} %stack.2.refs_0_), channel_id=1, source_target_pairs={{0,24},{4,12},{8,0},{12,20},{16,8},{20,28},{24,16},{28,4},{1,25},{... | collective-permute-start | bytes 1572872 | tf_op jit(solution)/shard_map/ppermute | solution.py:46
  35.3 21.4 %collective-permute-start.15 = (bf16[4,256,256]{2,1,0:T(8,128)(2,1)S(1)}, bf16[4,256,256]{2,1,0:T(8,128)(2,1)S(1)}, u32[]{:S(2)}, u32[]{:S(2)}) collective-permute-start(bf16[4,256,256]{2,1,0:T(8,128)(2,1)S(1)} %stack.3.refs_1_), channel_id=1, source_target_pairs={{0,24},{4,12},{8,0},{12,20},{16,8},{20,28},{24,16},{28,4},{1,25},{... | collective-permute-start | bytes 1572872 | tf_op jit(solution)/shard_map/ppermute | solution.py:46
  36.9 4.2 %collective-permute-start.13 = (bf16[2,1024,128]{2,1,0:T(8,128)(2,1)S(1)}, bf16[2,1024,128]{2,1,0:T(8,128)(2,1)S(1)}, u32[]{:S(2)}, u32[]{:S(2)}) collective-permute-start(bf16[2,1024,128]{2,1,0:T(8,128)(2,1)S(1)} %prepare.1.refs_4_.refs_2_.refs_1_), channel_id=1, source_target_pairs={{0,4},{4,0},{1,5},{5,1},{2,6},{6,2},{3,7},{7,3},{8,12},{12,8},{9,1... | collective-permute-start | bytes 1572872 | tf_op jit(solution)/shard_map/ppermute | solution.py:50
  37.0 20.4 %collective-permute-start.6 = (bf16[4,256,256]{2,1,0:T(8,128)(2,1)S(1)}, bf16[4,256,256]{2,1,0:T(8,128)(2,1)S(1)}, u32[]{:S(2)}, u32[]{:S(2)}) collective-permute-start(bf16[4,256,256]{2,1,0:T(8,128)(2,1)S(1)} %collective-permute-done.5.refs_2_.refs_0_), channel_id=1, source_target_pairs={{0,8},{4,28},{8,16},{12,4},{16,24},{20,12},{24,0},{28,20},{1,9},{5... | collective-permute-start | bytes 1572872 | tf_op jit(solution)/shard_map/ppermute | solution.py:46
  38.9 20.6 %collective-permute-start.12 = (bf16[4,256,256]{2,1,0:T(8,128)(2,1)S(1)}, bf16[4,256,256]{2,1,0:T(8,128)(2,1)S(1)}, u32[]{:S(2)}, u32[]{:S(2)}) collective-permute-start(bf16[4,256,256]{2,1,0:T(8,128)(2,1)S(1)} %collective-permute-done.11.refs_3_.refs_1_), channel_id=1, source_target_pairs={{0,8},{4,28},{8,16},{12,4},{16,24},{20,12},{24,0},{28,20},{1,9},{5... | collective-permute-start | bytes 1572872 | tf_op jit(solution)/shard_map/ppermute | solution.py:46
  60.6 1.3 collective-permute-start.16
  62.8 11.8 %collective-permute-start.24 = (bf16[4,256,256]{2,1,0:T(8,128)(2,1)S(1)}, bf16[4,256,256]{2,1,0:T(8,128)(2,1)S(1)}, u32[]{:S(2)}, u32[]{:S(2)}) collective-permute-start(bf16[4,256,256]{2,1,0:T(8,128)(2,1)S(1)} %get-tuple-element.75), channel_id=1, source_target_pairs={{0,24},{4,12},{8,0},{12,20},{16,8},{20,28},{24,16},{28,4},{1,25},{... | collective-permute-start | bytes 1572872 | tf_op jit(solution)/shard_map/ppermute | solution.py:46
  67.6 18.3 %collective-permute-start.19 = (bf16[4,256,256]{2,1,0:T(8,128)(2,1)S(1)}, bf16[4,256,256]{2,1,0:T(8,128)(2,1)S(1)}, u32[]{:S(2)}, u32[]{:S(2)}) collective-permute-start(bf16[4,256,256]{2,1,0:T(8,128)(2,1)S(1)} %get-tuple-element.68), channel_id=1, source_target_pairs={{0,24},{4,12},{8,0},{12,20},{16,8},{20,28},{24,16},{28,4},{1,25},{... | collective-permute-start | bytes 1572872 | tf_op jit(solution)/shard_map/ppermute | solution.py:46
  70.6 38.6 %collective-permute-start.21 = (bf16[4,256,256]{2,1,0:T(8,128)(2,1)S(1)}, bf16[4,256,256]{2,1,0:T(8,128)(2,1)S(1)}, u32[]{:S(2)}, u32[]{:S(2)}) collective-permute-start(bf16[4,256,256]{2,1,0:T(8,128)(2,1)S(1)} %get-tuple-element.69), channel_id=1, source_target_pairs={{0,8},{4,28},{8,16},{12,4},{16,24},{20,12},{24,0},{28,20},{1,9},{5... | collective-permute-start | bytes 1572872 | tf_op jit(solution)/shard_map/ppermute | solution.py:46
  70.8 27.2 %collective-permute-start.26 = (bf16[4,256,256]{2,1,0:T(8,128)(2,1)S(1)}, bf16[4,256,256]{2,1,0:T(8,128)(2,1)S(1)}, u32[]{:S(2)}, u32[]{:S(2)}) collective-permute-start(bf16[4,256,256]{2,1,0:T(8,128)(2,1)S(1)} %get-tuple-element.76), channel_id=1, source_target_pairs={{0,8},{4,28},{8,16},{12,4},{16,24},{20,12},{24,0},{28,20},{1,9},{5... | collective-permute-start | bytes 1572872 | tf_op jit(solution)/shard_map/ppermute | solution.py:46
  74.7 23.2 %collective-permute-start.25 = (bf16[4,256,256]{2,1,0:T(8,128)(2,1)S(1)}, bf16[4,256,256]{2,1,0:T(8,128)(2,1)S(1)}, u32[]{:S(2)}, u32[]{:S(2)}) collective-permute-start(bf16[4,256,256]{2,1,0:T(8,128)(2,1)S(1)} %add_convert_fusion), channel_id=1, source_target_pairs={{0,24},{4,12},{8,0},{12,20},{16,8},{20,28},{24,16},{28,4},{1,25},{... | collective-permute-start | bytes 1572872 | tf_op jit(solution)/shard_map/ppermute | solution.py:46
  86.0 23.2 %collective-permute-start.20 = (bf16[4,256,256]{2,1,0:T(8,128)(2,1)S(1)}, bf16[4,256,256]{2,1,0:T(8,128)(2,1)S(1)}, u32[]{:S(2)}, u32[]{:S(2)}) collective-permute-start(bf16[4,256,256]{2,1,0:T(8,128)(2,1)S(1)} %add_convert_fusion.1), channel_id=1, source_target_pairs={{0,24},{4,12},{8,0},{12,20},{16,8},{20,28},{24,16},{28,4},{1,25},{... | collective-permute-start | bytes 1572872 | tf_op jit(solution)/shard_map/ppermute | solution.py:46
  89.7 27.4 %collective-permute-start.17 = (f32[128,1024]{1,0:T(8,128)S(1)}, f32[128,1024]{1,0:T(8,128)S(1)}, u32[]{:S(2)}, u32[]{:S(2)}) collective-permute-start(f32[128,1024]{1,0:T(8,128)S(1)} %get-tuple-element.53), channel_id=1, source_target_pairs={{0,4},{4,0},{1,5},{5,1},{2,6},{6,2},{3,7},{7,3},{8,12},{12,8},{9,1... | collective-permute-start | bytes 1572872 | tf_op jit(solution)/shard_map/ppermute | solution.py:50
  98.0 23.3 %collective-permute-start.18 = (f32[128,1024]{1,0:T(8,128)S(1)}, f32[128,1024]{1,0:T(8,128)S(1)}, u32[]{:S(2)}, u32[]{:S(2)}) collective-permute-start(f32[128,1024]{1,0:T(8,128)S(1)} %get-tuple-element.63), channel_id=1, source_target_pairs={{0,4},{4,0},{1,5},{5,1},{2,6},{6,2},{3,7},{7,3},{8,12},{12,8},{9,1... | collective-permute-start | bytes 1572872 | tf_op jit(solution)/shard_map/ppermute | solution.py:50
  98.2 15.0 %collective-permute-start.27 = (bf16[256,256]{1,0:T(8,128)(2,1)S(1)}, bf16[256,256]{1,0:T(8,128)(2,1)S(1)}, u32[]{:S(2)}, u32[]{:S(2)}) collective-permute-start(bf16[256,256]{1,0:T(8,128)(2,1)S(1)} %get-tuple-element.79), channel_id=1, source_target_pairs={{0,224},{4,36},{32,0},{36,68},{64,32},{68,100},{96,64},{100,132},{... | collective-permute-start | bytes 393224 | tf_op jit(solution)/shard_map/ppermute | solution.py:46
  109.1 7.8 %collective-permute-start.28 = (bf16[256,256]{1,0:T(8,128)(2,1)S(1)}, bf16[256,256]{1,0:T(8,128)(2,1)S(1)}, u32[]{:S(2)}, u32[]{:S(2)}) collective-permute-start(bf16[256,256]{1,0:T(8,128)(2,1)S(1)} %get-tuple-element.80), channel_id=1, source_target_pairs={{0,192},{4,68},{32,224},{36,100},{64,0},{68,132},{96,32},{100,164}... | collective-permute-start | bytes 393224 | tf_op jit(solution)/shard_map/ppermute | solution.py:46
  109.2 7.8 %collective-permute-start.29 = (bf16[256,256]{1,0:T(8,128)(2,1)S(1)}, bf16[256,256]{1,0:T(8,128)(2,1)S(1)}, u32[]{:S(2)}, u32[]{:S(2)}) collective-permute-start(bf16[256,256]{1,0:T(8,128)(2,1)S(1)} %get-tuple-element.81), channel_id=1, source_target_pairs={{0,32},{4,228},{32,64},{36,4},{64,96},{68,36},{96,128},{100,68},{1... | collective-permute-start | bytes 393224 | tf_op jit(solution)/shard_map/ppermute | solution.py:46
  113.1 9.2 %collective-permute-start.22 = (bf16[256,256]{1,0:T(8,128)(2,1)S(1)}, bf16[256,256]{1,0:T(8,128)(2,1)S(1)}, u32[]{:S(2)}, u32[]{:S(2)}) collective-permute-start(bf16[256,256]{1,0:T(8,128)(2,1)S(1)} %get-tuple-element.71), channel_id=1, source_target_pairs={{0,224},{4,36},{32,0},{36,68},{64,32},{68,100},{96,64},{100,132},{... | collective-permute-start | bytes 393224 | tf_op jit(solution)/shard_map/ppermute | solution.py:46
  117.0 6.3 %collective-permute-start.23 = (bf16[256,256]{1,0:T(8,128)(2,1)S(1)}, bf16[256,256]{1,0:T(8,128)(2,1)S(1)}, u32[]{:S(2)}, u32[]{:S(2)}) collective-permute-start(bf16[256,256]{1,0:T(8,128)(2,1)S(1)} %get-tuple-element.72), channel_id=1, source_target_pairs={{0,32},{4,228},{32,64},{36,4},{64,96},{68,36},{96,128},{100,68},{1... | collective-permute-start | bytes 393224 | tf_op jit(solution)/shard_map/ppermute | solution.py:46
  117.0 12.1 %collective-permute-start.30 = (bf16[256,256]{1,0:T(8,128)(2,1)S(1)}, bf16[256,256]{1,0:T(8,128)(2,1)S(1)}, u32[]{:S(2)}, u32[]{:S(2)}) collective-permute-start(bf16[256,256]{1,0:T(8,128)(2,1)S(1)} %get-tuple-element.82), channel_id=1, source_target_pairs={{0,64},{4,196},{32,96},{36,228},{64,128},{68,4},{96,160},{100,36},... | collective-permute-start | bytes 393224 | tf_op jit(solution)/shard_map/ppermute | solution.py:46
  117.2 11.9 %collective-permute-start.31 = (bf16[256,256]{1,0:T(8,128)(2,1)S(1)}, bf16[256,256]{1,0:T(8,128)(2,1)S(1)}, u32[]{:S(2)}, u32[]{:S(2)}) collective-permute-start(bf16[256,256]{1,0:T(8,128)(2,1)S(1)} %get-tuple-element.83), channel_id=1, source_target_pairs={{0,192},{4,68},{32,224},{36,100},{64,0},{68,132},{96,32},{100,164}... | collective-permute-start | bytes 393224 | tf_op jit(solution)/shard_map/ppermute | solution.py:46

commit v3 on v2

--- a/solution.py
+++ b/solution.py
@@ -56,6 +56,13 @@
     return (i - j) <= off
 
 
+def place_of(i, bases):
+    base = bases[0]
+    for a, b in enumerate(bases[1:], 1):
+        base = jnp.where(i // QUAD == a, b, base)
+    return base + i % QUAD
+
+
 def fetch(i, kv_refs, kv_buf):
     for a, ref in enumerate(kv_refs):
 
@@ -74,7 +81,8 @@
     return [ref.at[1] for ref in refs]
 
 
-def forward_kernel(base, n, first, last, info, *refs):
+def forward_kernel(bases, first, last, info, *refs):
+    n = len(bases)
     kv_refs, refs = refs[:n], refs[n:]
     q_refs, g_refs, refs = query_refs(refs[:2]), grad_refs(refs[:2]), refs[2:]
     if not first:
@@ -121,7 +129,7 @@
                 p_ref[:, flat] = p.astype(BF)
             acc[...] += dot(vt, p_ref[:, pl.ds(half * COLS, COLS)], NN)
 
-    pl.when(info[base + i] > 0)(lambda: step(first))
+    pl.when(info[place_of(i, bases)] > 0)(lambda: step(first))
 
     if last:
 
@@ -146,7 +154,8 @@
     return m + jnp.log2(total), e0 / total, e1 / total
 
 
-def backward_kernel(base, n, first, masks, info, *refs):
+def backward_kernel(bases, first, masks, info, *refs):
+    n = len(bases)
     kv_refs, refs = refs[:n], refs[n:]
     q_refs, g_refs, refs = query_refs(refs[:2]), grad_refs(refs[:2]), refs[2:]
     mine, other, refs = refs[0], refs[1], refs[2:]
@@ -195,7 +204,7 @@
         out_buf[:, :HEAD_DIM] = dk.astype(BF)
         out_buf[:, HEAD_DIM:] = dv.astype(BF)
 
-    live = info[base + i] > 0
+    live = info[place_of(i, bases)] > 0
     pl.when(live)(lambda: step(masks))
 
     @pl.when(jnp.logical_not(live))
@@ -234,7 +243,7 @@
     return pl.CostEstimate(flops=flops, bytes_accessed=1 << 16, transcendentals=0)
 
 
-def forward(base, info, kvs, qg, state, last):
+def forward(bases, info, kvs, qg, state, last):
     n = len(kvs)
     first = state is None
     ins = list(kvs) + list(qg) + ([] if first else list(state))
@@ -242,7 +251,7 @@
     if not first:
         specs += [whole(STAT), whole(ACC), whole(ACC)]
     return pl.pallas_call(
-        functools.partial(forward_kernel, base, n, first, last),
+        functools.partial(forward_kernel, bases, first, last),
         grid_spec=pltpu.PrefetchScalarGridSpec(
             num_scalar_prefetch=1,
             grid=(QUAD * n,),
@@ -261,7 +270,7 @@
     )(info, *ins)
 
 
-def backward(base, info, kvs, qg, mine, other, dq):
+def backward(bases, info, kvs, qg, mine, other, dq):
     n = len(kvs)
     first = dq is None
     ins = list(kvs) + list(qg) + [mine, other] + ([] if first else list(dq))
@@ -270,7 +279,7 @@
         specs += [whole(ACC), whole(ACC)]
     wide_shape = (HALF, 2 * COLS)
     res = pl.pallas_call(
-        functools.partial(backward_kernel, base, n, first, base == 0),
+        functools.partial(backward_kernel, bases, first, bases[0] == 0),
         grid_spec=pltpu.PrefetchScalarGridSpec(
             num_scalar_prefetch=1,
             grid=(QUAD * n,),
@@ -475,22 +484,22 @@
     info = plan(gate_score[0])
     qg = (qg, swap(qg))
 
-    state = forward(0, info, [low0, high0, low1, high1], qg, None, False)
-    state = forward(24, info, [low3, high3], qg, state, False)
-    mine, acc, acc_away = forward(16, info, [low2, high2], qg, state, True)
+    state = forward((0, 4, 8, 12), info, [low0, high0, low1, high1], qg, None, False)
+    state = forward((24, 16), info, [low3, low2], qg, state, False)
+    mine, acc, acc_away = forward((28, 20), info, [high3, high2], qg, state, True)
     other = swap(mine)
     acc_other = swap(acc_away)
 
-    dq, (high2,) = backward(20, info, [high2], qg, mine, other, None)
+    dq, (high2,) = backward((20,), info, [high2], qg, mine, other, None)
     high2 = shift(high2, "x", -1)
-    dq, (low2,) = backward(16, info, [low2], qg, mine, other, dq)
+    dq, (low2,) = backward((16,), info, [low2], qg, mine, other, dq)
     low2 = shift(low2, "x", -1)
-    dq, (low3, high3) = backward(24, info, [low3, high3], qg, mine, other, dq)
+    dq, (low3, high3) = backward((24, 28), info, [low3, high3], qg, mine, other, dq)
     high3, low3 = shift(high3, "x", 1), shift(low3, "x", 1)
-    dq, (low1, high1) = backward(8, info, [low1, high1], qg, mine, other, dq)
+    dq, (low1, high1) = backward((8, 12), info, [low1, high1], qg, mine, other, dq)
     high1 = shift((wide(high1) + wide(high2)).astype(BF), "x", -1)
     low1 = shift((wide(low1) + wide(low2)).astype(BF), "x", -1)
-    dq, (low0, high0) = backward(0, info, [low0, high0], qg, mine, other, dq)
+    dq, (low0, high0) = backward((0, 4), info, [low0, high0], qg, mine, other, dq)
 
     keep_high, up, down, far = sum_high(high0, high1, high3)
     down, far, up = shift(down, "z", -1), shift(far, "z", -2), shift(up, "z", 1)

time: 131 us -> 127 us (0.969)
  the two profiles are of different devices: /device:TPU:8 before, /device:TPU:1 now
where the time goes in v3:
time: 127 us; the launch traced here: 125 us
  starting transfers between devices  64.7 us (51%)
  waiting for transfers between devices  42.8 us (34%)
  Pallas kernels  14.9 us (12%)
    ppermute x26, starting transfers between devices, shift(): lax.ppermute(a, (axis, 'core'), [(2 * i + c, 2 * ((i + d * (1 - 2 * c)) %...  47.1 us
    ppermute x26, waiting for transfers between devices, shift(): lax.ppermute(a, (axis, 'core'), [(2 * i + c, 2 * ((i + d * (1 - 2 * c)) %...  40.8 us
    ppermute x4, starting transfers between devices, swap(): return lax.ppermute(a, 'core', [(0, 1), (1, 0)])  13.4 us
    pallas_call x5, Pallas kernels, backward(): pl.pallas_call(functools.partial(backward_kernel, bases, first, bases[0]...  6.52 us
    pallas_call x3, Pallas kernels, forward(): pl.pallas_call(functools.partial(forward_kernel, bases, first, last), gri...  4.46 us
    ppermute x1, starting transfers between devices, plan(): lax.ppermute(totals, 'head', [(0, 2), (2, 0), (1, 3), (3, 1)])  3 us
  transfers between devices with their start and end apart: 32, of which 14 were waited for; matrix products, arithmetic and copies ran while one was open for 1% of the time, Pallas kernels for 8%

profile of v3, /device:TPU:1, one launch (start us, length us, event | category | flops | bytes accessed | tf_op | source)
XLA Modules:
  0.0 124.8 jit_solution(2095058087167881345)
XLA Ops:
  0.6 1.5 %join.1.refs_0_ = bf16[256,256]{1,0:T(8,128)(2,1)} custom-call(bf16[256,128]{1,0:T(8,128)(2,1)} %k_ref.1, bf16[256,128]{1,0:T(8,128)(2,1)} %v_ref.1), custom_call_target="tpu_custom_call" | custom-call | tf_op jit(solution)/shard_map/join/pallas_call | solution.py:335
  2.2 6.9 %collective-permute-start.3 = (bf16[256,256]{1,0:T(8,128)(2,1)}, bf16[256,256]{1,0:T(8,128)(2,1)S(1)}, u32[]{:S(2)}, u32[]{:S(2)}) collective-permute-start(bf16[256,256]{1,0:T(8,128)(2,1)} %join.1.refs_0_), channel_id=1, source_target_pairs={{0,64},{4,196},{32,96},{36,228},{64,128},{68,4},{96,160},{100,36},... | collective-permute-start | bytes 393224 | tf_op jit(solution)/shard_map/ppermute | solution.py:46
  9.1 0.7 collective-permute-start.12
  9.9 2.4 %collective-permute-start.11 = (bf16[256,256]{1,0:T(8,128)(2,1)}, bf16[256,256]{1,0:T(8,128)(2,1)S(1)}, u32[]{:S(2)}, u32[]{:S(2)}) collective-permute-start(bf16[256,256]{1,0:T(8,128)(2,1)} %join.1.refs_0_), channel_id=1, source_target_pairs={{0,32},{4,228},{32,64},{36,4},{64,96},{68,36},{96,128},{100,68},{1... | collective-permute-start | bytes 393224 | tf_op jit(solution)/shard_map/ppermute | solution.py:46
  12.3 1.9 %collective-permute-done.3.refs_3_ = bf16[256,256]{1,0:T(8,128)(2,1)S(1)} collective-permute-done((bf16[256,256]{1,0:T(8,128)(2,1)}, bf16[256,256]{1,0:T(8,128)(2,1)S(1)}, u32[]{:S(2)}, u32[]{:S(2)}) %collective-permute-start.3) | collective-permute-done | bytes 131104 | tf_op jit(solution)/shard_map/ppermute | solution.py:46
  14.2 4.6 %collective-permute-start.6 = (bf16[256,256]{1,0:T(8,128)(2,1)S(1)}, bf16[256,256]{1,0:T(8,128)(2,1)S(1)}, u32[]{:S(2)}, u32[]{:S(2)}) collective-permute-start(bf16[256,256]{1,0:T(8,128)(2,1)S(1)} %collective-permute-done.3.refs_3_), channel_id=1, source_target_pairs={{0,64},{4,196},{32,96},{36,228},{64,128},{68,4},{96,160},{100,36},... | collective-permute-start | bytes 393224 | tf_op jit(solution)/shard_map/ppermute | solution.py:46
  18.8 1.5 %collective-permute-start.5 = (bf16[256,256]{1,0:T(8,128)(2,1)S(1)}, bf16[256,256]{1,0:T(8,128)(2,1)S(1)}, u32[]{:S(2)}, u32[]{:S(2)}) collective-permute-start(bf16[256,256]{1,0:T(8,128)(2,1)S(1)} %collective-permute-done.2.refs_0_), channel_id=1, source_target_pairs={{0,224},{4,36},{32,0},{36,68},{64,32},{68,100},{96,64},{100,132},{... | collective-permute-start | bytes 393224 | tf_op jit(solution)/shard_map/ppermute | solution.py:46
  20.2 1.3 %collective-permute-start = (s32[32,32]{1,0:T(8,128)S(1)}, s32[32,32]{1,0:T(8,128)S(1)}, u32[]{:S(2)}, u32[]{:S(2)}) collective-permute-start(s32[32,32]{1,0:T(8,128)S(1)} %bitcast.17), channel_id=1, source_target_pairs={{0,1},{1,0},{2,3},{3,2},{4,5},{5,4},{6,7},{7,6},{8,9},{9,8},{10,11... | collective-permute-start | bytes 12296 | tf_op jit(solution)/shard_map/ppermute | solution.py:455
  21.5 0.9 copy-done
  22.5 2.6 %collective-permute-start.14 = (bf16[4,256,256]{2,1,0:T(8,128)(2,1)S(1)}, bf16[4,256,256]{2,1,0:T(8,128)(2,1)S(1)}, u32[]{:S(2)}, u32[]{:S(2)}) collective-permute-start(bf16[4,256,256]{2,1,0:T(8,128)(2,1)S(1)} %stack.3.refs_0_), channel_id=1, source_target_pairs={{0,8},{4,28},{8,16},{12,4},{16,24},{20,12},{24,0},{28,20},{1,9},{5... | collective-permute-start | bytes 1572872 | tf_op jit(solution)/shard_map/ppermute | solution.py:46
  25.1 1.0 collective-permute-done.5.refs_2_
  26.1 2.6 %collective-permute-start.8 = (bf16[4,256,256]{2,1,0:T(8,128)(2,1)S(1)}, bf16[4,256,256]{2,1,0:T(8,128)(2,1)S(1)}, u32[]{:S(2)}, u32[]{:S(2)}) collective-permute-start(bf16[4,256,256]{2,1,0:T(8,128)(2,1)S(1)} %stack.2.refs_1_), channel_id=1, source_target_pairs={{0,8},{4,28},{8,16},{12,4},{16,24},{20,12},{24,0},{28,20},{1,9},{5... | collective-permute-start | bytes 1572872 | tf_op jit(solution)/shard_map/ppermute | solution.py:46
  28.7 3.0 %collective-permute-start.1 = (s32[32,32]{1,0:T(8,128)S(1)}, s32[32,32]{1,0:T(8,128)S(1)}, u32[]{:S(2)}, u32[]{:S(2)}) collective-permute-start(s32[32,32]{1,0:T(8,128)S(1)} %bitcast_add_fusion.1), channel_id=1, source_target_pairs={{0,2},{2,0},{1,3},{3,1},{4,6},{6,4},{5,7},{7,5},{8,10},{10,8},{9,1... | collective-permute-start | bytes 12296 | tf_op jit(solution)/shard_map/ppermute | solution.py:456
  31.7 1.1 collective-permute-done.1
  32.9 0.1 collective-permute-start.13
  32.9 0.2 collective-permute-start.7
  33.1 0.1 prepare.1.refs_4_.refs_2_.refs_1_
  33.2 4.3 %collective-permute-start.10 = (bf16[2,1024,128]{2,1,0:T(8,128)(2,1)S(1)}, bf16[2,1024,128]{2,1,0:T(8,128)(2,1)S(1)}, u32[]{:S(2)}, u32[]{:S(2)}) collective-permute-start(bf16[2,1024,128]{2,1,0:T(8,128)(2,1)S(1)} %prepare.1.refs_4_.refs_2_.refs_1_), channel_id=1, source_target_pairs={{0,4},{4,0},{1,5},{5,1},{2,6},{6,2},{3,7},{7,3},{8,12},{12,8},{9,1... | collective-permute-start | bytes 1572872 | tf_op jit(solution)/shard_map/ppermute | solution.py:50
  37.5 0.5 collective-permute-start.15
  38.1 2.4 %collective-permute-start.9 = (bf16[4,256,256]{2,1,0:T(8,128)(2,1)S(1)}, bf16[4,256,256]{2,1,0:T(8,128)(2,1)S(1)}, u32[]{:S(2)}, u32[]{:S(2)}) collective-permute-start(bf16[4,256,256]{2,1,0:T(8,128)(2,1)S(1)} %collective-permute-done.8.refs_3_.refs_1_), channel_id=1, source_target_pairs={{0,8},{4,28},{8,16},{12,4},{16,24},{20,12},{24,0},{28,20},{1,9},{5... | collective-permute-start | bytes 1572872 | tf_op jit(solution)/shard_map/ppermute | solution.py:46
  40.5 0.2 convert_reduce_fusion.1
  40.7 0.1 convert_reduce_fusion
  40.8 0.1 pad_add_fusion.info
  40.9 2.4 %forward.3 = (f32[2,3,1024]{2,1,0:T(4,128)S(1)}, f32[128,1024]{1,0:T(8,128)S(1)}, f32[128,1024]{1,0:T(8,128)S(1)}) custom-call(s32[33]{0:T(128)S(1)} %pad_add_fusion.info, bf16[4,256,256]{2,1,0:T(8,128)(2,1)S(1)} %stack.3.refs_0_, bf16[4,256,256]{2,1,0:T(8,128)(2,1)S(1)} %stack.2.refs_1_, bf16[4,256,256]{2,1,0:T(8,128)(2,1)S(1)} %collective-permute-done.14.refs_2_.refs_0_, ...), custom_call_target="tpu_custom_call" | custom-call | flops 200000000 | bytes 65536 | tf_op jit(solution)/shard_map/forward/pallas_call | solution.py:253
  43.3 4.9 %collective-permute-done.13.refs_0_ = bf16[4,256,256]{2,1,0:T(8,128)(2,1)S(1)} collective-permute-done((bf16[4,256,256]{2,1,0:T(8,128)(2,1)S(1)}, bf16[4,256,256]{2,1,0:T(8,128)(2,1)S(1)}, u32[]{:S(2)}, u32[]{:S(2)}) %collective-permute-start.13) | collective-permute-done | bytes 524320 | tf_op jit(solution)/shard_map/ppermute | solution.py:46
  48.2 3.4 %collective-permute-done.15.refs_1_.refs_0_ = bf16[4,256,256]{2,1,0:T(8,128)(2,1)S(1)} collective-permute-done((bf16[4,256,256]{2,1,0:T(8,128)(2,1)S(1)}, bf16[4,256,256]{2,1,0:T(8,128)(2,1)S(1)}, u32[]{:S(2)}, u32[]{:S(2)}) %collective-permute-start.15) | collective-permute-done | bytes 524320 | tf_op jit(solution)/shard_map/ppermute | solution.py:46
  51.5 0.9 forward.4
  52.4 7.0 %collective-permute-done.7.refs_0_.refs_1_ = bf16[4,256,256]{2,1,0:T(8,128)(2,1)S(1)} collective-permute-done((bf16[4,256,256]{2,1,0:T(8,128)(2,1)S(1)}, bf16[4,256,256]{2,1,0:T(8,128)(2,1)S(1)}, u32[]{:S(2)}, u32[]{:S(2)}) %collective-permute-start.7) | collective-permute-done | bytes 524320 | tf_op jit(solution)/shard_map/ppermute | solution.py:46
  59.4 0.3 collective-permute-done.9.refs_1_.refs_0_
  59.7 1.2 forward.5
  60.9 2.8 %collective-permute-start.16 = (f32[2,3,1024]{2,1,0:T(4,128)S(1)}, f32[2,3,1024]{2,1,0:T(4,128)S(1)}, u32[]{:S(2)}, u32[]{:S(2)}) collective-permute-start(f32[2,3,1024]{2,1,0:T(4,128)S(1)} %get-tuple-element.51.refs_3_.refs_4_.mine), channel_id=1, source_target_pairs={{0,4},{4,0},{1,5},{5,1},{2,6},{6,2},{3,7},{7,3},{8,12},{12,8},{9,1... | collective-permute-start | bytes 73736 | tf_op jit(solution)/shard_map/ppermute | solution.py:50
  63.7 0.9 collective-permute-done.16.refs_4_.refs_5_.other
  64.5 0.8 backward.5
  65.4 0.1 collective-permute-start.24
  65.5 0.8 backward.6
  66.3 1.3 %collective-permute-start.19 = (bf16[4,256,256]{2,1,0:T(8,128)(2,1)S(1)}, bf16[4,256,256]{2,1,0:T(8,128)(2,1)S(1)}, u32[]{:S(2)}, u32[]{:S(2)}) collective-permute-start(bf16[4,256,256]{2,1,0:T(8,128)(2,1)S(1)} %get-tuple-element.68), channel_id=1, source_target_pairs={{0,24},{4,12},{8,0},{12,20},{16,8},{20,28},{24,16},{28,4},{1,25},{... | collective-permute-start | bytes 1572872 | tf_op jit(solution)/shard_map/ppermute | solution.py:46
  67.6 1.1 backward.7
  68.6 4.7 %collective-permute-start.21 = (bf16[4,256,256]{2,1,0:T(8,128)(2,1)S(1)}, bf16[4,256,256]{2,1,0:T(8,128)(2,1)S(1)}, u32[]{:S(2)}, u32[]{:S(2)}) collective-permute-start(bf16[4,256,256]{2,1,0:T(8,128)(2,1)S(1)} %get-tuple-element.69), channel_id=1, source_target_pairs={{0,8},{4,28},{8,16},{12,4},{16,24},{20,12},{24,0},{28,20},{1,9},{5... | collective-permute-start | bytes 1572872 | tf_op jit(solution)/shard_map/ppermute | solution.py:46
  73.3 1.4 %collective-permute-start.26 = (bf16[4,256,256]{2,1,0:T(8,128)(2,1)S(1)}, bf16[4,256,256]{2,1,0:T(8,128)(2,1)S(1)}, u32[]{:S(2)}, u32[]{:S(2)}) collective-permute-start(bf16[4,256,256]{2,1,0:T(8,128)(2,1)S(1)} %get-tuple-element.76), channel_id=1, source_target_pairs={{0,8},{4,28},{8,16},{12,4},{16,24},{20,12},{24,0},{28,20},{1,9},{5... | collective-permute-start | bytes 1572872 | tf_op jit(solution)/shard_map/ppermute | solution.py:46
  74.8 1.1 backward.8
  75.9 0.1 add_convert_fusion
  76.0 0.1 collective-permute-start.25
  76.1 8.8 %collective-permute-done.19 = bf16[4,256,256]{2,1,0:T(8,128)(2,1)S(1)} collective-permute-done((bf16[4,256,256]{2,1,0:T(8,128)(2,1)S(1)}, bf16[4,256,256]{2,1,0:T(8,128)(2,1)S(1)}, u32[]{:S(2)}, u32[]{:S(2)}) %collective-permute-start.19) | collective-permute-done | bytes 524320 | tf_op jit(solution)/shard_map/ppermute | solution.py:46
  85.0 0.1 add_convert_fusion.1
  85.1 0.1 collective-permute-start.20
  85.2 3.7 %collective-permute-start.17 = (f32[128,1024]{1,0:T(8,128)S(1)}, f32[128,1024]{1,0:T(8,128)S(1)}, u32[]{:S(2)}, u32[]{:S(2)}) collective-permute-start(f32[128,1024]{1,0:T(8,128)S(1)} %get-tuple-element.53), channel_id=1, source_target_pairs={{0,4},{4,0},{1,5},{5,1},{2,6},{6,2},{3,7},{7,3},{8,12},{12,8},{9,1... | collective-permute-start | bytes 1572872 | tf_op jit(solution)/shard_map/ppermute | solution.py:50
  88.9 2.7 %backward.9 = (f32[128,1024]{1,0:T(8,128)S(1)}, f32[128,1024]{1,0:T(8,128)S(1)}, bf16[4,256,256]{2,1,0:T(8,128)(2,1)S(1)}, bf16[4,256,256]{2,1,0:T(8,128)(2,1)S(1)}) custom-call(s32[33]{0:T(128)S(1)} %pad_add_fusion.info, bf16[4,256,256]{2,1,0:T(8,128)(2,1)S(1)} %stack.3.refs_0_, bf16[4,256,256]{2,1,0:T(8,128)(2,1)S(1)} %stack.2.refs_1_, ...), custom_call_target="tpu_custom_call" | custom-call | flops 200000000 | bytes 65536 | tf_op jit(solution)/shard_map/backward/pallas_call | solution.py:281
  91.7 4.9 %collective-permute-done.26.three = bf16[4,256,256]{2,1,0:T(8,128)(2,1)S(1)} collective-permute-done((bf16[4,256,256]{2,1,0:T(8,128)(2,1)S(1)}, bf16[4,256,256]{2,1,0:T(8,128)(2,1)S(1)}, u32[]{:S(2)}, u32[]{:S(2)}) %collective-permute-start.26) | collective-permute-done | bytes 524320 | tf_op jit(solution)/shard_map/ppermute | solution.py:46
  96.5 2.6 %collective-permute-start.18 = (f32[128,1024]{1,0:T(8,128)S(1)}, f32[128,1024]{1,0:T(8,128)S(1)}, u32[]{:S(2)}, u32[]{:S(2)}) collective-permute-start(f32[128,1024]{1,0:T(8,128)S(1)} %get-tuple-element.63), channel_id=1, source_target_pairs={{0,4},{4,0},{1,5},{5,1},{2,6},{6,2},{3,7},{7,3},{8,12},{12,8},{9,1... | collective-permute-start | bytes 1572872 | tf_op jit(solution)/shard_map/ppermute | solution.py:50
  99.1 0.2 sum_high.1
  99.3 1.9 %collective-permute-start.27 = (bf16[256,256]{1,0:T(8,128)(2,1)S(1)}, bf16[256,256]{1,0:T(8,128)(2,1)S(1)}, u32[]{:S(2)}, u32[]{:S(2)}) collective-permute-start(bf16[256,256]{1,0:T(8,128)(2,1)S(1)} %get-tuple-element.79), channel_id=1, source_target_pairs={{0,224},{4,36},{32,0},{36,68},{64,32},{68,100},{96,64},{100,132},{... | collective-permute-start | bytes 393224 | tf_op jit(solution)/shard_map/ppermute | solution.py:46
  101.2 6.2 %collective-permute-start.28 = (bf16[256,256]{1,0:T(8,128)(2,1)S(1)}, bf16[256,256]{1,0:T(8,128)(2,1)S(1)}, u32[]{:S(2)}, u32[]{:S(2)}) collective-permute-start(bf16[256,256]{1,0:T(8,128)(2,1)S(1)} %get-tuple-element.80), channel_id=1, source_target_pairs={{0,192},{4,68},{32,224},{36,100},{64,0},{68,132},{96,32},{100,164}... | collective-permute-start | bytes 393224 | tf_op jit(solution)/shard_map/ppermute | solution.py:46
  107.4 3.2 %collective-permute-start.29 = (bf16[256,256]{1,0:T(8,128)(2,1)S(1)}, bf16[256,256]{1,0:T(8,128)(2,1)S(1)}, u32[]{:S(2)}, u32[]{:S(2)}) collective-permute-start(bf16[256,256]{1,0:T(8,128)(2,1)S(1)} %get-tuple-element.81), channel_id=1, source_target_pairs={{0,32},{4,228},{32,64},{36,4},{64,96},{68,36},{96,128},{100,68},{1... | collective-permute-start | bytes 393224 | tf_op jit(solution)/shard_map/ppermute | solution.py:46
  110.6 0.2 sum_low.1
  110.8 0.1 collective-permute-start.22
  110.9 2.6 %collective-permute-done.28.far = bf16[256,256]{1,0:T(8,128)(2,1)S(1)} collective-permute-done((bf16[256,256]{1,0:T(8,128)(2,1)S(1)}, bf16[256,256]{1,0:T(8,128)(2,1)S(1)}, u32[]{:S(2)}, u32[]{:S(2)}) %collective-permute-start.28) | collective-permute-done | bytes 131104 | tf_op jit(solution)/shard_map/ppermute | solution.py:46
  113.6 0.7 collective-permute-done.29.up
  114.3 0.1 sum_two.1
  114.3 1.7 %collective-permute-start.30 = (bf16[256,256]{1,0:T(8,128)(2,1)S(1)}, bf16[256,256]{1,0:T(8,128)(2,1)S(1)}, u32[]{:S(2)}, u32[]{:S(2)}) collective-permute-start(bf16[256,256]{1,0:T(8,128)(2,1)S(1)} %get-tuple-element.82), channel_id=1, source_target_pairs={{0,64},{4,196},{32,96},{36,228},{64,128},{68,4},{96,160},{100,36},... | collective-permute-start | bytes 393224 | tf_op jit(solution)/shard_map/ppermute | solution.py:46
  116.0 1.8 %collective-permute-start.31 = (bf16[256,256]{1,0:T(8,128)(2,1)S(1)}, bf16[256,256]{1,0:T(8,128)(2,1)S(1)}, u32[]{:S(2)}, u32[]{:S(2)}) collective-permute-start(bf16[256,256]{1,0:T(8,128)(2,1)S(1)} %get-tuple-element.83), channel_id=1, source_target_pairs={{0,192},{4,68},{32,224},{36,100},{64,0},{68,132},{96,32},{100,164}... | collective-permute-start | bytes 393224 | tf_op jit(solution)/shard_map/ppermute | solution.py:46
  117.8 1.0 finish.1
  118.9 3.4 %collective-permute-done.30.c = bf16[256,256]{1,0:T(8,128)(2,1)S(1)} collective-permute-done((bf16[256,256]{1,0:T(8,128)(2,1)S(1)}, bf16[256,256]{1,0:T(8,128)(2,1)S(1)}, u32[]{:S(2)}, u32[]{:S(2)}) %collective-permute-start.30) | collective-permute-done | bytes 131104 | tf_op jit(solution)/shard_map/ppermute | solution.py:46
  122.2 1.9 %collective-permute-done.31.d = bf16[256,256]{1,0:T(8,128)(2,1)S(1)} collective-permute-done((bf16[256,256]{1,0:T(8,128)(2,1)S(1)}, bf16[256,256]{1,0:T(8,128)(2,1)S(1)}, u32[]{:S(2)}, u32[]{:S(2)}) %collective-permute-start.31) | collective-permute-done | bytes 131104 | tf_op jit(solution)/shard_map/ppermute | solution.py:46
  124.1 0.7 close.1
  (35 shorter events, 0.2 us)
Async XLA Ops:
  0.6 19.6 %copy-start.3 = (s32[1,32,32]{2,1,0:T(8,128)S(1)}, s32[1,32,32]{2,1,0:T(8,128)}, u32[]{:S(2)}) copy-start(s32[1,32,32]{2,1,0:T(8,128)} %param.9) | copy-start | bytes 12292
  2.2 12.0 %collective-permute-start.3 = (bf16[256,256]{1,0:T(8,128)(2,1)}, bf16[256,256]{1,0:T(8,128)(2,1)S(1)}, u32[]{:S(2)}, u32[]{:S(2)}) collective-permute-start(bf16[256,256]{1,0:T(8,128)(2,1)} %join.1.refs_0_), channel_id=1, source_target_pairs={{0,64},{4,196},{32,96},{36,228},{64,128},{68,4},{96,160},{100,36},... | collective-permute-start | bytes 393224 | tf_op jit(solution)/shard_map/ppermute | solution.py:46
  9.1 9.6 %collective-permute-start.2 = (bf16[256,256]{1,0:T(8,128)(2,1)}, bf16[256,256]{1,0:T(8,128)(2,1)S(1)}, u32[]{:S(2)}, u32[]{:S(2)}) collective-permute-start(bf16[256,256]{1,0:T(8,128)(2,1)} %join.1.refs_0_), channel_id=1, source_target_pairs={{0,192},{4,68},{32,224},{36,100},{64,0},{68,132},{96,32},{100,164}... | collective-permute-start | bytes 393224 | tf_op jit(solution)/shard_map/ppermute | solution.py:46
  9.1 11.1 %collective-permute-start.12 = (bf16[256,256]{1,0:T(8,128)(2,1)}, bf16[256,256]{1,0:T(8,128)(2,1)S(1)}, u32[]{:S(2)}, u32[]{:S(2)}) collective-permute-start(bf16[256,256]{1,0:T(8,128)(2,1)} %join.1.refs_0_), channel_id=1, source_target_pairs={{0,224},{4,36},{32,0},{36,68},{64,32},{68,100},{96,64},{100,132},{... | collective-permute-start | bytes 393224 | tf_op jit(solution)/shard_map/ppermute | solution.py:46
  9.9 11.7 %collective-permute-start.11 = (bf16[256,256]{1,0:T(8,128)(2,1)}, bf16[256,256]{1,0:T(8,128)(2,1)S(1)}, u32[]{:S(2)}, u32[]{:S(2)}) collective-permute-start(bf16[256,256]{1,0:T(8,128)(2,1)} %join.1.refs_0_), channel_id=1, source_target_pairs={{0,32},{4,228},{32,64},{36,4},{64,96},{68,36},{96,128},{100,68},{1... | collective-permute-start | bytes 393224 | tf_op jit(solution)/shard_map/ppermute | solution.py:46
  14.2 10.9 %collective-permute-start.6 = (bf16[256,256]{1,0:T(8,128)(2,1)S(1)}, bf16[256,256]{1,0:T(8,128)(2,1)S(1)}, u32[]{:S(2)}, u32[]{:S(2)}) collective-permute-start(bf16[256,256]{1,0:T(8,128)(2,1)S(1)} %collective-permute-done.3.refs_3_), channel_id=1, source_target_pairs={{0,64},{4,196},{32,96},{36,228},{64,128},{68,4},{96,160},{100,36},... | collective-permute-start | bytes 393224 | tf_op jit(solution)/shard_map/ppermute | solution.py:46
  18.8 6.3 %collective-permute-start.4 = (bf16[256,256]{1,0:T(8,128)(2,1)S(1)}, bf16[256,256]{1,0:T(8,128)(2,1)S(1)}, u32[]{:S(2)}, u32[]{:S(2)}) collective-permute-start(bf16[256,256]{1,0:T(8,128)(2,1)S(1)} %collective-permute-done.3.refs_3_), channel_id=1, source_target_pairs={{0,32},{4,228},{32,64},{36,4},{64,96},{68,36},{96,128},{100,68},{1... | collective-permute-start | bytes 393224 | tf_op jit(solution)/shard_map/ppermute | solution.py:46
  18.8 7.3 %collective-permute-start.5 = (bf16[256,256]{1,0:T(8,128)(2,1)S(1)}, bf16[256,256]{1,0:T(8,128)(2,1)S(1)}, u32[]{:S(2)}, u32[]{:S(2)}) collective-permute-start(bf16[256,256]{1,0:T(8,128)(2,1)S(1)} %collective-permute-done.2.refs_0_), channel_id=1, source_target_pairs={{0,224},{4,36},{32,0},{36,68},{64,32},{68,100},{96,64},{100,132},{... | collective-permute-start | bytes 393224 | tf_op jit(solution)/shard_map/ppermute | solution.py:46
  20.2 8.4 %collective-permute-start = (s32[32,32]{1,0:T(8,128)S(1)}, s32[32,32]{1,0:T(8,128)S(1)}, u32[]{:S(2)}, u32[]{:S(2)}) collective-permute-start(s32[32,32]{1,0:T(8,128)S(1)} %bitcast.17), channel_id=1, source_target_pairs={{0,1},{1,0},{2,3},{3,2},{4,5},{5,4},{6,7},{7,6},{8,9},{9,8},{10,11... | collective-permute-start | bytes 12296 | tf_op jit(solution)/shard_map/ppermute | solution.py:455
  21.5 0.9 copy-start
  22.5 10.7 %copy-start.1 = (bf16[256,512]{1,0:T(8,128)(2,1)S(1)}, bf16[256,512]{1,0:T(8,128)(2,1)}, u32[]{:S(2)}) copy-start(bf16[256,512]{1,0:T(8,128)(2,1)} %query.1) | copy-start | bytes 786436
  22.5 10.7 %copy-start.2 = (bf16[256,512]{1,0:T(8,128)(2,1)S(1)}, bf16[256,512]{1,0:T(8,128)(2,1)}, u32[]{:S(2)}) copy-start(bf16[256,512]{1,0:T(8,128)(2,1)} %grad_out.1) | copy-start | bytes 786436
  22.5 15.0 %collective-permute-start.14 = (bf16[4,256,256]{2,1,0:T(8,128)(2,1)S(1)}, bf16[4,256,256]{2,1,0:T(8,128)(2,1)S(1)}, u32[]{:S(2)}, u32[]{:S(2)}) collective-permute-start(bf16[4,256,256]{2,1,0:T(8,128)(2,1)S(1)} %stack.3.refs_0_), channel_id=1, source_target_pairs={{0,8},{4,28},{8,16},{12,4},{16,24},{20,12},{24,0},{28,20},{1,9},{5... | collective-permute-start | bytes 1572872 | tf_op jit(solution)/shard_map/ppermute | solution.py:46
  26.1 12.0 %collective-permute-start.8 = (bf16[4,256,256]{2,1,0:T(8,128)(2,1)S(1)}, bf16[4,256,256]{2,1,0:T(8,128)(2,1)S(1)}, u32[]{:S(2)}, u32[]{:S(2)}) collective-permute-start(bf16[4,256,256]{2,1,0:T(8,128)(2,1)S(1)} %stack.2.refs_1_), channel_id=1, source_target_pairs={{0,8},{4,28},{8,16},{12,4},{16,24},{20,12},{24,0},{28,20},{1,9},{5... | collective-permute-start | bytes 1572872 | tf_op jit(solution)/shard_map/ppermute | solution.py:46
  28.7 4.2 %collective-permute-start.1 = (s32[32,32]{1,0:T(8,128)S(1)}, s32[32,32]{1,0:T(8,128)S(1)}, u32[]{:S(2)}, u32[]{:S(2)}) collective-permute-start(s32[32,32]{1,0:T(8,128)S(1)} %bitcast_add_fusion.1), channel_id=1, source_target_pairs={{0,2},{2,0},{1,3},{3,1},{4,6},{6,4},{5,7},{7,5},{8,10},{10,8},{9,1... | collective-permute-start | bytes 12296 | tf_op jit(solution)/shard_map/ppermute | solution.py:456
  32.9 15.3 %collective-permute-start.13 = (bf16[4,256,256]{2,1,0:T(8,128)(2,1)S(1)}, bf16[4,256,256]{2,1,0:T(8,128)(2,1)S(1)}, u32[]{:S(2)}, u32[]{:S(2)}) collective-permute-start(bf16[4,256,256]{2,1,0:T(8,128)(2,1)S(1)} %stack.3.refs_0_), channel_id=1, source_target_pairs={{0,24},{4,12},{8,0},{12,20},{16,8},{20,28},{24,16},{28,4},{1,25},{... | collective-permute-start | bytes 1572872 | tf_op jit(solution)/shard_map/ppermute | solution.py:46
  32.9 26.4 %collective-permute-start.7 = (bf16[4,256,256]{2,1,0:T(8,128)(2,1)S(1)}, bf16[4,256,256]{2,1,0:T(8,128)(2,1)S(1)}, u32[]{:S(2)}, u32[]{:S(2)}) collective-permute-start(bf16[4,256,256]{2,1,0:T(8,128)(2,1)S(1)} %stack.2.refs_1_), channel_id=1, source_target_pairs={{0,24},{4,12},{8,0},{12,20},{16,8},{20,28},{24,16},{28,4},{1,25},{... | collective-permute-start | bytes 1572872 | tf_op jit(solution)/shard_map/ppermute | solution.py:46
  33.2 7.6 %collective-permute-start.10 = (bf16[2,1024,128]{2,1,0:T(8,128)(2,1)S(1)}, bf16[2,1024,128]{2,1,0:T(8,128)(2,1)S(1)}, u32[]{:S(2)}, u32[]{:S(2)}) collective-permute-start(bf16[2,1024,128]{2,1,0:T(8,128)(2,1)S(1)} %prepare.1.refs_4_.refs_2_.refs_1_), channel_id=1, source_target_pairs={{0,4},{4,0},{1,5},{5,1},{2,6},{6,2},{3,7},{7,3},{8,12},{12,8},{9,1... | collective-permute-start | bytes 1572872 | tf_op jit(solution)/shard_map/ppermute | solution.py:50
  37.5 14.0 %collective-permute-start.15 = (bf16[4,256,256]{2,1,0:T(8,128)(2,1)S(1)}, bf16[4,256,256]{2,1,0:T(8,128)(2,1)S(1)}, u32[]{:S(2)}, u32[]{:S(2)}) collective-permute-start(bf16[4,256,256]{2,1,0:T(8,128)(2,1)S(1)} %collective-permute-done.14.refs_2_.refs_0_), channel_id=1, source_target_pairs={{0,8},{4,28},{8,16},{12,4},{16,24},{20,12},{24,0},{28,20},{1,9},{5... | collective-permute-start | bytes 1572872 | tf_op jit(solution)/shard_map/ppermute | solution.py:46
  38.1 21.6 %collective-permute-start.9 = (bf16[4,256,256]{2,1,0:T(8,128)(2,1)S(1)}, bf16[4,256,256]{2,1,0:T(8,128)(2,1)S(1)}, u32[]{:S(2)}, u32[]{:S(2)}) collective-permute-start(bf16[4,256,256]{2,1,0:T(8,128)(2,1)S(1)} %collective-permute-done.8.refs_3_.refs_1_), channel_id=1, source_target_pairs={{0,8},{4,28},{8,16},{12,4},{16,24},{20,12},{24,0},{28,20},{1,9},{5... | collective-permute-start | bytes 1572872 | tf_op jit(solution)/shard_map/ppermute | solution.py:46
  60.9 3.7 %collective-permute-start.16 = (f32[2,3,1024]{2,1,0:T(4,128)S(1)}, f32[2,3,1024]{2,1,0:T(4,128)S(1)}, u32[]{:S(2)}, u32[]{:S(2)}) collective-permute-start(f32[2,3,1024]{2,1,0:T(4,128)S(1)} %get-tuple-element.51.refs_3_.refs_4_.mine), channel_id=1, source_target_pairs={{0,4},{4,0},{1,5},{5,1},{2,6},{6,2},{3,7},{7,3},{8,12},{12,8},{9,1... | collective-permute-start | bytes 73736 | tf_op jit(solution)/shard_map/ppermute | solution.py:50
  65.4 10.5 %collective-permute-start.24 = (bf16[4,256,256]{2,1,0:T(8,128)(2,1)S(1)}, bf16[4,256,256]{2,1,0:T(8,128)(2,1)S(1)}, u32[]{:S(2)}, u32[]{:S(2)}) collective-permute-start(bf16[4,256,256]{2,1,0:T(8,128)(2,1)S(1)} %get-tuple-element.75), channel_id=1, source_target_pairs={{0,24},{4,12},{8,0},{12,20},{16,8},{20,28},{24,16},{28,4},{1,25},{... | collective-permute-start | bytes 1572872 | tf_op jit(solution)/shard_map/ppermute | solution.py:46
  66.3 18.7 %collective-permute-start.19 = (bf16[4,256,256]{2,1,0:T(8,128)(2,1)S(1)}, bf16[4,256,256]{2,1,0:T(8,128)(2,1)S(1)}, u32[]{:S(2)}, u32[]{:S(2)}) collective-permute-start(bf16[4,256,256]{2,1,0:T(8,128)(2,1)S(1)} %get-tuple-element.68), channel_id=1, source_target_pairs={{0,24},{4,12},{8,0},{12,20},{16,8},{20,28},{24,16},{28,4},{1,25},{... | collective-permute-start | bytes 1572872 | tf_op jit(solution)/shard_map/ppermute | solution.py:46
  68.6 32.6 %collective-permute-start.21 = (bf16[4,256,256]{2,1,0:T(8,128)(2,1)S(1)}, bf16[4,256,256]{2,1,0:T(8,128)(2,1)S(1)}, u32[]{:S(2)}, u32[]{:S(2)}) collective-permute-start(bf16[4,256,256]{2,1,0:T(8,128)(2,1)S(1)} %get-tuple-element.69), channel_id=1, source_target_pairs={{0,8},{4,28},{8,16},{12,4},{16,24},{20,12},{24,0},{28,20},{1,9},{5... | collective-permute-start | bytes 1572872 | tf_op jit(solution)/shard_map/ppermute | solution.py:46
  73.3 23.2 %collective-permute-start.26 = (bf16[4,256,256]{2,1,0:T(8,128)(2,1)S(1)}, bf16[4,256,256]{2,1,0:T(8,128)(2,1)S(1)}, u32[]{:S(2)}, u32[]{:S(2)}) collective-permute-start(bf16[4,256,256]{2,1,0:T(8,128)(2,1)S(1)} %get-tuple-element.76), channel_id=1, source_target_pairs={{0,8},{4,28},{8,16},{12,4},{16,24},{20,12},{24,0},{28,20},{1,9},{5... | collective-permute-start | bytes 1572872 | tf_op jit(solution)/shard_map/ppermute | solution.py:46
  76.0 23.1 %collective-permute-start.25 = (bf16[4,256,256]{2,1,0:T(8,128)(2,1)S(1)}, bf16[4,256,256]{2,1,0:T(8,128)(2,1)S(1)}, u32[]{:S(2)}, u32[]{:S(2)}) collective-permute-start(bf16[4,256,256]{2,1,0:T(8,128)(2,1)S(1)} %add_convert_fusion), channel_id=1, source_target_pairs={{0,24},{4,12},{8,0},{12,20},{16,8},{20,28},{24,16},{28,4},{1,25},{... | collective-permute-start | bytes 1572872 | tf_op jit(solution)/shard_map/ppermute | solution.py:46
  85.1 22.3 %collective-permute-start.20 = (bf16[4,256,256]{2,1,0:T(8,128)(2,1)S(1)}, bf16[4,256,256]{2,1,0:T(8,128)(2,1)S(1)}, u32[]{:S(2)}, u32[]{:S(2)}) collective-permute-start(bf16[4,256,256]{2,1,0:T(8,128)(2,1)S(1)} %add_convert_fusion.1), channel_id=1, source_target_pairs={{0,24},{4,12},{8,0},{12,20},{16,8},{20,28},{24,16},{28,4},{1,25},{... | collective-permute-start | bytes 1572872 | tf_op jit(solution)/shard_map/ppermute | solution.py:46
  85.2 30.8 %collective-permute-start.17 = (f32[128,1024]{1,0:T(8,128)S(1)}, f32[128,1024]{1,0:T(8,128)S(1)}, u32[]{:S(2)}, u32[]{:S(2)}) collective-permute-start(f32[128,1024]{1,0:T(8,128)S(1)} %get-tuple-element.53), channel_id=1, source_target_pairs={{0,4},{4,0},{1,5},{5,1},{2,6},{6,2},{3,7},{7,3},{8,12},{12,8},{9,1... | collective-permute-start | bytes 1572872 | tf_op jit(solution)/shard_map/ppermute | solution.py:50
  96.5 21.3 %collective-permute-start.18 = (f32[128,1024]{1,0:T(8,128)S(1)}, f32[128,1024]{1,0:T(8,128)S(1)}, u32[]{:S(2)}, u32[]{:S(2)}) collective-permute-start(f32[128,1024]{1,0:T(8,128)S(1)} %get-tuple-element.63), channel_id=1, source_target_pairs={{0,4},{4,0},{1,5},{5,1},{2,6},{6,2},{3,7},{7,3},{8,12},{12,8},{9,1... | collective-permute-start | bytes 1572872 | tf_op jit(solution)/shard_map/ppermute | solution.py:50
  99.3 11.5 %collective-permute-start.27 = (bf16[256,256]{1,0:T(8,128)(2,1)S(1)}, bf16[256,256]{1,0:T(8,128)(2,1)S(1)}, u32[]{:S(2)}, u32[]{:S(2)}) collective-permute-start(bf16[256,256]{1,0:T(8,128)(2,1)S(1)} %get-tuple-element.79), channel_id=1, source_target_pairs={{0,224},{4,36},{32,0},{36,68},{64,32},{68,100},{96,64},{100,132},{... | collective-permute-start | bytes 393224 | tf_op jit(solution)/shard_map/ppermute | solution.py:46
  101.2 12.3 %collective-permute-start.28 = (bf16[256,256]{1,0:T(8,128)(2,1)S(1)}, bf16[256,256]{1,0:T(8,128)(2,1)S(1)}, u32[]{:S(2)}, u32[]{:S(2)}) collective-permute-start(bf16[256,256]{1,0:T(8,128)(2,1)S(1)} %get-tuple-element.80), channel_id=1, source_target_pairs={{0,192},{4,68},{32,224},{36,100},{64,0},{68,132},{96,32},{100,164}... | collective-permute-start | bytes 393224 | tf_op jit(solution)/shard_map/ppermute | solution.py:46
  107.4 6.8 %collective-permute-start.29 = (bf16[256,256]{1,0:T(8,128)(2,1)S(1)}, bf16[256,256]{1,0:T(8,128)(2,1)S(1)}, u32[]{:S(2)}, u32[]{:S(2)}) collective-permute-start(bf16[256,256]{1,0:T(8,128)(2,1)S(1)} %get-tuple-element.81), channel_id=1, source_target_pairs={{0,32},{4,228},{32,64},{36,4},{64,96},{68,36},{96,128},{100,68},{1... | collective-permute-start | bytes 393224 | tf_op jit(solution)/shard_map/ppermute | solution.py:46
  110.8 8.1 %collective-permute-start.22 = (bf16[256,256]{1,0:T(8,128)(2,1)S(1)}, bf16[256,256]{1,0:T(8,128)(2,1)S(1)}, u32[]{:S(2)}, u32[]{:S(2)}) collective-permute-start(bf16[256,256]{1,0:T(8,128)(2,1)S(1)} %get-tuple-element.71), channel_id=1, source_target_pairs={{0,224},{4,36},{32,0},{36,68},{64,32},{68,100},{96,64},{100,132},{... | collective-permute-start | bytes 393224 | tf_op jit(solution)/shard_map/ppermute | solution.py:46
  113.5 5.4 %collective-permute-start.23 = (bf16[256,256]{1,0:T(8,128)(2,1)S(1)}, bf16[256,256]{1,0:T(8,128)(2,1)S(1)}, u32[]{:S(2)}, u32[]{:S(2)}) collective-permute-start(bf16[256,256]{1,0:T(8,128)(2,1)S(1)} %get-tuple-element.72), channel_id=1, source_target_pairs={{0,32},{4,228},{32,64},{36,4},{64,96},{68,36},{96,128},{100,68},{1... | collective-permute-start | bytes 393224 | tf_op jit(solution)/shard_map/ppermute | solution.py:46
  114.3 7.9 %collective-permute-start.30 = (bf16[256,256]{1,0:T(8,128)(2,1)S(1)}, bf16[256,256]{1,0:T(8,128)(2,1)S(1)}, u32[]{:S(2)}, u32[]{:S(2)}) collective-permute-start(bf16[256,256]{1,0:T(8,128)(2,1)S(1)} %get-tuple-element.82), channel_id=1, source_target_pairs={{0,64},{4,196},{32,96},{36,228},{64,128},{68,4},{96,160},{100,36},... | collective-permute-start | bytes 393224 | tf_op jit(solution)/shard_map/ppermute | solution.py:46
  116.0 8.1 %collective-permute-start.31 = (bf16[256,256]{1,0:T(8,128)(2,1)S(1)}, bf16[256,256]{1,0:T(8,128)(2,1)S(1)}, u32[]{:S(2)}, u32[]{:S(2)}) collective-permute-start(bf16[256,256]{1,0:T(8,128)(2,1)S(1)} %get-tuple-element.83), channel_id=1, source_target_pairs={{0,192},{4,68},{32,224},{36,100},{64,0},{68,132},{96,32},{100,164}... | collective-permute-start | bytes 393224 | tf_op jit(solution)/shard_map/ppermute | solution.py:46

commit v4 on v3

--- a/solution.py
+++ b/solution.py
@@ -485,8 +485,8 @@
     qg = (qg, swap(qg))
 
     state = forward((0, 4, 8, 12), info, [low0, high0, low1, high1], qg, None, False)
-    state = forward((24, 16), info, [low3, low2], qg, state, False)
-    mine, acc, acc_away = forward((28, 20), info, [high3, high2], qg, state, True)
+    state = forward((24, 16, 28), info, [low3, low2, high3], qg, state, False)
+    mine, acc, acc_away = forward((20,), info, [high2], qg, state, True)
     other = swap(mine)
     acc_other = swap(acc_away)
 

time: 127 us -> 128 us (level)
  the two profiles are of different devices: /device:TPU:1 before, /device:TPU:33 now
where the time goes in v4:
time: 128 us; the launch traced here: 126 us
  starting transfers between devices  62.1 us (49%)
  waiting for transfers between devices  36 us (28%)
  Pallas kernels  25.7 us (20%)
    ppermute x26, starting transfers between devices, shift(): lax.ppermute(a, (axis, 'core'), [(2 * i + c, 2 * ((i + d * (1 - 2 * c)) %...  46 us
    ppermute x26, waiting for transfers between devices, shift(): lax.ppermute(a, (axis, 'core'), [(2 * i + c, 2 * ((i + d * (1 - 2 * c)) %...  34 us
    pallas_call x5, Pallas kernels, backward(): pl.pallas_call(functools.partial(backward_kernel, bases, first, bases[0]...  12.9 us
    ppermute x4, starting transfers between devices, swap(): return lax.ppermute(a, 'core', [(0, 1), (1, 0)])  11.7 us
    pallas_call x3, Pallas kernels, forward(): pl.pallas_call(functools.partial(forward_kernel, bases, first, last), gri...  8.96 us
    ppermute x1, starting transfers between devices, plan(): lax.ppermute(totals, 'head', [(0, 2), (2, 0), (1, 3), (3, 1)])  2.99 us
  transfers between devices with their start and end apart: 32, of which 12 were waited for; matrix products, arithmetic and copies ran while one was open for 1% of the time, Pallas kernels for 17%

profile of v4, /device:TPU:33, one launch (start us, length us, event | category | flops | bytes accessed | tf_op | source)
XLA Modules:
  0.0 126.3 jit_solution(7662085532353929805)
XLA Ops:
  0.6 1.5 %join.1.refs_0_ = bf16[256,256]{1,0:T(8,128)(2,1)} custom-call(bf16[256,128]{1,0:T(8,128)(2,1)} %k_ref.1, bf16[256,128]{1,0:T(8,128)(2,1)} %v_ref.1), custom_call_target="tpu_custom_call" | custom-call | tf_op jit(solution)/shard_map/join/pallas_call | solution.py:335
  2.2 5.2 %collective-permute-start.3 = (bf16[256,256]{1,0:T(8,128)(2,1)}, bf16[256,256]{1,0:T(8,128)(2,1)S(1)}, u32[]{:S(2)}, u32[]{:S(2)}) collective-permute-start(bf16[256,256]{1,0:T(8,128)(2,1)} %join.1.refs_0_), channel_id=1, source_target_pairs={{0,64},{4,196},{32,96},{36,228},{64,128},{68,4},{96,160},{100,36},... | collective-permute-start | bytes 393224 | tf_op jit(solution)/shard_map/ppermute | solution.py:46
  7.4 0.8 collective-permute-start.11
  8.2 0.7 collective-permute-start.10
  8.9 1.0 collective-permute-done.3.refs_3_
  9.9 4.2 %collective-permute-start.6 = (bf16[256,256]{1,0:T(8,128)(2,1)S(1)}, bf16[256,256]{1,0:T(8,128)(2,1)S(1)}, u32[]{:S(2)}, u32[]{:S(2)}) collective-permute-start(bf16[256,256]{1,0:T(8,128)(2,1)S(1)} %collective-permute-done.3.refs_3_), channel_id=1, source_target_pairs={{0,64},{4,196},{32,96},{36,228},{64,128},{68,4},{96,160},{100,36},... | collective-permute-start | bytes 393224 | tf_op jit(solution)/shard_map/ppermute | solution.py:46
  14.1 3.7 %collective-permute-start.4 = (bf16[256,256]{1,0:T(8,128)(2,1)S(1)}, bf16[256,256]{1,0:T(8,128)(2,1)S(1)}, u32[]{:S(2)}, u32[]{:S(2)}) collective-permute-start(bf16[256,256]{1,0:T(8,128)(2,1)S(1)} %collective-permute-done.3.refs_3_), channel_id=1, source_target_pairs={{0,32},{4,228},{32,64},{36,4},{64,96},{68,36},{96,128},{100,68},{1... | collective-permute-start | bytes 393224 | tf_op jit(solution)/shard_map/ppermute | solution.py:46
  17.8 0.0 collective-permute-start.5
  17.8 1.4 %collective-permute-start = (s32[32,32]{1,0:T(8,128)S(1)}, s32[32,32]{1,0:T(8,128)S(1)}, u32[]{:S(2)}, u32[]{:S(2)}) collective-permute-start(s32[32,32]{1,0:T(8,128)S(1)} %bitcast.17), channel_id=1, source_target_pairs={{0,1},{1,0},{2,3},{3,2},{4,5},{5,4},{6,7},{7,6},{8,9},{9,8},{10,11... | collective-permute-start | bytes 12296 | tf_op jit(solution)/shard_map/ppermute | solution.py:455
  19.2 0.9 copy-done
  20.1 0.0 copy-start.1
  20.1 0.0 copy-start.2
  20.1 2.6 %collective-permute-start.13 = (bf16[4,256,256]{2,1,0:T(8,128)(2,1)S(1)}, bf16[4,256,256]{2,1,0:T(8,128)(2,1)S(1)}, u32[]{:S(2)}, u32[]{:S(2)}) collective-permute-start(bf16[4,256,256]{2,1,0:T(8,128)(2,1)S(1)} %stack.3.refs_0_), channel_id=1, source_target_pairs={{0,8},{4,28},{8,16},{12,4},{16,24},{20,12},{24,0},{28,20},{1,9},{5... | collective-permute-start | bytes 1572872 | tf_op jit(solution)/shard_map/ppermute | solution.py:46
  22.7 1.4 %collective-permute-done.5.refs_2_ = bf16[256,256]{1,0:T(8,128)(2,1)S(1)} collective-permute-done((bf16[256,256]{1,0:T(8,128)(2,1)S(1)}, bf16[256,256]{1,0:T(8,128)(2,1)S(1)}, u32[]{:S(2)}, u32[]{:S(2)}) %collective-permute-start.5) | collective-permute-done | bytes 131104 | tf_op jit(solution)/shard_map/ppermute | solution.py:46
  24.1 2.6 %collective-permute-start.7 = (bf16[4,256,256]{2,1,0:T(8,128)(2,1)S(1)}, bf16[4,256,256]{2,1,0:T(8,128)(2,1)S(1)}, u32[]{:S(2)}, u32[]{:S(2)}) collective-permute-start(bf16[4,256,256]{2,1,0:T(8,128)(2,1)S(1)} %stack.2.refs_1_), channel_id=1, source_target_pairs={{0,8},{4,28},{8,16},{12,4},{16,24},{20,12},{24,0},{28,20},{1,9},{5... | collective-permute-start | bytes 1572872 | tf_op jit(solution)/shard_map/ppermute | solution.py:46
  26.7 3.0 %collective-permute-start.1 = (s32[32,32]{1,0:T(8,128)S(1)}, s32[32,32]{1,0:T(8,128)S(1)}, u32[]{:S(2)}, u32[]{:S(2)}) collective-permute-start(s32[32,32]{1,0:T(8,128)S(1)} %bitcast_add_fusion.1), channel_id=1, source_target_pairs={{0,2},{2,0},{1,3},{3,1},{4,6},{6,4},{5,7},{7,5},{8,10},{10,8},{9,1... | collective-permute-start | bytes 12296 | tf_op jit(solution)/shard_map/ppermute | solution.py:456
  29.7 1.2 collective-permute-done.1
  30.9 0.1 collective-permute-start.12
  31.0 0.2 collective-permute-start.15
  31.2 0.1 prepare.1.refs_4_.refs_3_.refs_1_.refs_2_
  31.3 4.5 %collective-permute-start.9 = (bf16[2,1024,128]{2,1,0:T(8,128)(2,1)S(1)}, bf16[2,1024,128]{2,1,0:T(8,128)(2,1)S(1)}, u32[]{:S(2)}, u32[]{:S(2)}) collective-permute-start(bf16[2,1024,128]{2,1,0:T(8,128)(2,1)S(1)} %prepare.1.refs_4_.refs_3_.refs_1_.refs_2_), channel_id=1, source_target_pairs={{0,4},{4,0},{1,5},{5,1},{2,6},{6,2},{3,7},{7,3},{8,12},{12,8},{9,1... | collective-permute-start | bytes 1572872 | tf_op jit(solution)/shard_map/ppermute | solution.py:50
  35.8 0.5 collective-permute-start.14
  36.4 1.2 collective-permute-start.8
  37.5 0.2 convert_reduce_fusion.1
  37.7 0.1 convert_reduce_fusion
  37.9 0.1 pad_add_fusion.info
  37.9 4.7 %forward.3 = (f32[2,3,1024]{2,1,0:T(4,128)S(1)}, f32[128,1024]{1,0:T(8,128)S(1)}, f32[128,1024]{1,0:T(8,128)S(1)}) custom-call(s32[33]{0:T(128)S(1)} %pad_add_fusion.info, bf16[4,256,256]{2,1,0:T(8,128)(2,1)S(1)} %stack.3.refs_0_, bf16[4,256,256]{2,1,0:T(8,128)(2,1)S(1)} %stack.2.refs_1_, bf16[4,256,256]{2,1,0:T(8,128)(2,1)S(1)} %collective-permute-done.13.refs_2_.refs_0_, ...), custom_call_target="tpu_custom_call" | custom-call | flops 200000000 | bytes 65536 | tf_op jit(solution)/shard_map/forward/pallas_call | solution.py:253
  42.6 3.6 %collective-permute-done.12.refs_0_ = bf16[4,256,256]{2,1,0:T(8,128)(2,1)S(1)} collective-permute-done((bf16[4,256,256]{2,1,0:T(8,128)(2,1)S(1)}, bf16[4,256,256]{2,1,0:T(8,128)(2,1)S(1)}, u32[]{:S(2)}, u32[]{:S(2)}) %collective-permute-start.12) | collective-permute-done | bytes 524320 | tf_op jit(solution)/shard_map/ppermute | solution.py:46
  46.2 11.2 %collective-permute-done.15.refs_2_.refs_1_ = bf16[4,256,256]{2,1,0:T(8,128)(2,1)S(1)} collective-permute-done((bf16[4,256,256]{2,1,0:T(8,128)(2,1)S(1)}, bf16[4,256,256]{2,1,0:T(8,128)(2,1)S(1)}, u32[]{:S(2)}, u32[]{:S(2)}) %collective-permute-start.15) | collective-permute-done | bytes 524320 | tf_op jit(solution)/shard_map/ppermute | solution.py:46
  57.4 3.2 %forward.4 = (f32[2,3,1024]{2,1,0:T(4,128)S(1)}, f32[128,1024]{1,0:T(8,128)S(1)}, f32[128,1024]{1,0:T(8,128)S(1)}) custom-call(s32[33]{0:T(128)S(1)} %pad_add_fusion.info, bf16[4,256,256]{2,1,0:T(8,128)(2,1)S(1)} %collective-permute-done.12.refs_0_, bf16[4,256,256]{2,1,0:T(8,128)(2,1)S(1)} %collective-permute-done.14.refs_1_.refs_0_, ...), custom_call_target="tpu_custom_call" | custom-call | flops 200000000 | bytes 65536 | tf_op jit(solution)/shard_map/forward/pallas_call | solution.py:253
  60.7 1.1 forward.5
  61.7 0.9 collective-permute-start.16
  62.7 0.9 collective-permute-done.16.refs_4_.refs_5_.other
  63.5 0.8 backward.5
  64.4 0.1 collective-permute-start.24
  64.5 2.4 %backward.6 = (f32[128,1024]{1,0:T(8,128)S(1)}, f32[128,1024]{1,0:T(8,128)S(1)}, bf16[4,256,256]{2,1,0:T(8,128)(2,1)S(1)}) custom-call(s32[33]{0:T(128)S(1)} %pad_add_fusion.info, bf16[4,256,256]{2,1,0:T(8,128)(2,1)S(1)} %collective-permute-done.14.refs_1_.refs_0_, bf16[2,1024,128]{2,1,0:T(8,128)(2,1)S(1)} %prepare.1.refs_4_.refs_3_.refs_1_.refs_2_, ...), custom_call_target="tpu_custom_call" | custom-call | flops 200000000 | bytes 65536 | tf_op jit(solution)/shard_map/backward/pallas_call | solution.py:281
  66.9 2.3 %collective-permute-start.19 = (bf16[4,256,256]{2,1,0:T(8,128)(2,1)S(1)}, bf16[4,256,256]{2,1,0:T(8,128)(2,1)S(1)}, u32[]{:S(2)}, u32[]{:S(2)}) collective-permute-start(bf16[4,256,256]{2,1,0:T(8,128)(2,1)S(1)} %get-tuple-element.68), channel_id=1, source_target_pairs={{0,24},{4,12},{8,0},{12,20},{16,8},{20,28},{24,16},{28,4},{1,25},{... | collective-permute-start | bytes 1572872 | tf_op jit(solution)/shard_map/ppermute | solution.py:46
  69.1 2.6 %backward.7 = (f32[128,1024]{1,0:T(8,128)S(1)}, f32[128,1024]{1,0:T(8,128)S(1)}, bf16[4,256,256]{2,1,0:T(8,128)(2,1)S(1)}, bf16[4,256,256]{2,1,0:T(8,128)(2,1)S(1)}) custom-call(s32[33]{0:T(128)S(1)} %pad_add_fusion.info, bf16[4,256,256]{2,1,0:T(8,128)(2,1)S(1)} %collective-permute-done.12.refs_0_, ...), custom_call_target="tpu_custom_call" | custom-call | flops 200000000 | bytes 65536 | tf_op jit(solution)/shard_map/backward/pallas_call | solution.py:281
  71.8 3.8 %collective-permute-start.21 = (bf16[4,256,256]{2,1,0:T(8,128)(2,1)S(1)}, bf16[4,256,256]{2,1,0:T(8,128)(2,1)S(1)}, u32[]{:S(2)}, u32[]{:S(2)}) collective-permute-start(bf16[4,256,256]{2,1,0:T(8,128)(2,1)S(1)} %get-tuple-element.69), channel_id=1, source_target_pairs={{0,8},{4,28},{8,16},{12,4},{16,24},{20,12},{24,0},{28,20},{1,9},{5... | collective-permute-start | bytes 1572872 | tf_op jit(solution)/shard_map/ppermute | solution.py:46
  75.6 1.5 %collective-permute-start.26 = (bf16[4,256,256]{2,1,0:T(8,128)(2,1)S(1)}, bf16[4,256,256]{2,1,0:T(8,128)(2,1)S(1)}, u32[]{:S(2)}, u32[]{:S(2)}) collective-permute-start(bf16[4,256,256]{2,1,0:T(8,128)(2,1)S(1)} %get-tuple-element.76), channel_id=1, source_target_pairs={{0,8},{4,28},{8,16},{12,4},{16,24},{20,12},{24,0},{28,20},{1,9},{5... | collective-permute-start | bytes 1572872 | tf_op jit(solution)/shard_map/ppermute | solution.py:46
  77.0 2.6 %backward.8 = (f32[128,1024]{1,0:T(8,128)S(1)}, f32[128,1024]{1,0:T(8,128)S(1)}, bf16[4,256,256]{2,1,0:T(8,128)(2,1)S(1)}, bf16[4,256,256]{2,1,0:T(8,128)(2,1)S(1)}) custom-call(s32[33]{0:T(128)S(1)} %pad_add_fusion.info, bf16[4,256,256]{2,1,0:T(8,128)(2,1)S(1)} %collective-permute-done.13.refs_2_.refs_0_, ...), custom_call_target="tpu_custom_call" | custom-call | flops 200000000 | bytes 65536 | tf_op jit(solution)/shard_map/backward/pallas_call | solution.py:281
  79.7 0.1 add_convert_fusion
  79.8 0.1 collective-permute-start.25
  79.9 0.1 collective-permute-done.19
  80.0 0.1 add_convert_fusion.1
  80.2 1.3 %collective-permute-start.20 = (bf16[4,256,256]{2,1,0:T(8,128)(2,1)S(1)}, bf16[4,256,256]{2,1,0:T(8,128)(2,1)S(1)}, u32[]{:S(2)}, u32[]{:S(2)}) collective-permute-start(bf16[4,256,256]{2,1,0:T(8,128)(2,1)S(1)} %add_convert_fusion.1), channel_id=1, source_target_pairs={{0,24},{4,12},{8,0},{12,20},{16,8},{20,28},{24,16},{28,4},{1,25},{... | collective-permute-start | bytes 1572872 | tf_op jit(solution)/shard_map/ppermute | solution.py:46
  81.5 6.2 %collective-permute-start.17 = (f32[128,1024]{1,0:T(8,128)S(1)}, f32[128,1024]{1,0:T(8,128)S(1)}, u32[]{:S(2)}, u32[]{:S(2)}) collective-permute-start(f32[128,1024]{1,0:T(8,128)S(1)} %get-tuple-element.53), channel_id=1, source_target_pairs={{0,4},{4,0},{1,5},{5,1},{2,6},{6,2},{3,7},{7,3},{8,12},{12,8},{9,1... | collective-permute-start | bytes 1572872 | tf_op jit(solution)/shard_map/ppermute | solution.py:50
  87.7 4.4 %backward.9 = (f32[128,1024]{1,0:T(8,128)S(1)}, f32[128,1024]{1,0:T(8,128)S(1)}, bf16[4,256,256]{2,1,0:T(8,128)(2,1)S(1)}, bf16[4,256,256]{2,1,0:T(8,128)(2,1)S(1)}) custom-call(s32[33]{0:T(128)S(1)} %pad_add_fusion.info, bf16[4,256,256]{2,1,0:T(8,128)(2,1)S(1)} %stack.3.refs_0_, bf16[4,256,256]{2,1,0:T(8,128)(2,1)S(1)} %stack.2.refs_1_, ...), custom_call_target="tpu_custom_call" | custom-call | flops 200000000 | bytes 65536 | tf_op jit(solution)/shard_map/backward/pallas_call | solution.py:281
  92.1 6.3 %collective-permute-done.26.three = bf16[4,256,256]{2,1,0:T(8,128)(2,1)S(1)} collective-permute-done((bf16[4,256,256]{2,1,0:T(8,128)(2,1)S(1)}, bf16[4,256,256]{2,1,0:T(8,128)(2,1)S(1)}, u32[]{:S(2)}, u32[]{:S(2)}) %collective-permute-start.26) | collective-permute-done | bytes 524320 | tf_op jit(solution)/shard_map/ppermute | solution.py:46
  98.4 0.2 sum_high.1
  98.6 4.1 %collective-permute-start.27 = (bf16[256,256]{1,0:T(8,128)(2,1)S(1)}, bf16[256,256]{1,0:T(8,128)(2,1)S(1)}, u32[]{:S(2)}, u32[]{:S(2)}) collective-permute-start(bf16[256,256]{1,0:T(8,128)(2,1)S(1)} %get-tuple-element.79), channel_id=1, source_target_pairs={{0,224},{4,36},{32,0},{36,68},{64,32},{68,100},{96,64},{100,132},{... | collective-permute-start | bytes 393224 | tf_op jit(solution)/shard_map/ppermute | solution.py:46
  102.7 3.1 %collective-permute-start.28 = (bf16[256,256]{1,0:T(8,128)(2,1)S(1)}, bf16[256,256]{1,0:T(8,128)(2,1)S(1)}, u32[]{:S(2)}, u32[]{:S(2)}) collective-permute-start(bf16[256,256]{1,0:T(8,128)(2,1)S(1)} %get-tuple-element.80), channel_id=1, source_target_pairs={{0,192},{4,68},{32,224},{36,100},{64,0},{68,132},{96,32},{100,164}... | collective-permute-start | bytes 393224 | tf_op jit(solution)/shard_map/ppermute | solution.py:46
  105.8 1.4 %collective-permute-start.29 = (bf16[256,256]{1,0:T(8,128)(2,1)S(1)}, bf16[256,256]{1,0:T(8,128)(2,1)S(1)}, u32[]{:S(2)}, u32[]{:S(2)}) collective-permute-start(bf16[256,256]{1,0:T(8,128)(2,1)S(1)} %get-tuple-element.81), channel_id=1, source_target_pairs={{0,32},{4,228},{32,64},{36,4},{64,96},{68,36},{96,128},{100,68},{1... | collective-permute-start | bytes 393224 | tf_op jit(solution)/shard_map/ppermute | solution.py:46
  107.2 0.2 sum_low.1
  107.4 1.2 collective-permute-start.22
  108.6 1.0 collective-permute-done.28.far
  109.5 1.9 %collective-permute-start.23 = (bf16[256,256]{1,0:T(8,128)(2,1)S(1)}, bf16[256,256]{1,0:T(8,128)(2,1)S(1)}, u32[]{:S(2)}, u32[]{:S(2)}) collective-permute-start(bf16[256,256]{1,0:T(8,128)(2,1)S(1)} %get-tuple-element.72), channel_id=1, source_target_pairs={{0,32},{4,228},{32,64},{36,4},{64,96},{68,36},{96,128},{100,68},{1... | collective-permute-start | bytes 393224 | tf_op jit(solution)/shard_map/ppermute | solution.py:46
  111.4 0.5 collective-permute-done.29.up
  111.9 0.1 sum_two.1
  112.0 3.7 %collective-permute-start.30 = (bf16[256,256]{1,0:T(8,128)(2,1)S(1)}, bf16[256,256]{1,0:T(8,128)(2,1)S(1)}, u32[]{:S(2)}, u32[]{:S(2)}) collective-permute-start(bf16[256,256]{1,0:T(8,128)(2,1)S(1)} %get-tuple-element.82), channel_id=1, source_target_pairs={{0,64},{4,196},{32,96},{36,228},{64,128},{68,4},{96,160},{100,36},... | collective-permute-start | bytes 393224 | tf_op jit(solution)/shard_map/ppermute | solution.py:46
  115.7 1.0 finish.1
  116.8 2.2 %collective-permute-done.30.c = bf16[256,256]{1,0:T(8,128)(2,1)S(1)} collective-permute-done((bf16[256,256]{1,0:T(8,128)(2,1)S(1)}, bf16[256,256]{1,0:T(8,128)(2,1)S(1)}, u32[]{:S(2)}, u32[]{:S(2)}) %collective-permute-start.30) | collective-permute-done | bytes 131104 | tf_op jit(solution)/shard_map/ppermute | solution.py:46
  119.0 6.6 %collective-permute-done.31.d = bf16[256,256]{1,0:T(8,128)(2,1)S(1)} collective-permute-done((bf16[256,256]{1,0:T(8,128)(2,1)S(1)}, bf16[256,256]{1,0:T(8,128)(2,1)S(1)}, u32[]{:S(2)}, u32[]{:S(2)}) %collective-permute-start.31) | collective-permute-done | bytes 131104 | tf_op jit(solution)/shard_map/ppermute | solution.py:46
  125.6 0.7 close.1
  (35 shorter events, 0.2 us)
Async XLA Ops:
  0.6 17.1 %copy-start.3 = (s32[1,32,32]{2,1,0:T(8,128)S(1)}, s32[1,32,32]{2,1,0:T(8,128)}, u32[]{:S(2)}) copy-start(s32[1,32,32]{2,1,0:T(8,128)} %param.9) | copy-start | bytes 12292
  2.2 7.7 %collective-permute-start.3 = (bf16[256,256]{1,0:T(8,128)(2,1)}, bf16[256,256]{1,0:T(8,128)(2,1)S(1)}, u32[]{:S(2)}, u32[]{:S(2)}) collective-permute-start(bf16[256,256]{1,0:T(8,128)(2,1)} %join.1.refs_0_), channel_id=1, source_target_pairs={{0,64},{4,196},{32,96},{36,228},{64,128},{68,4},{96,160},{100,36},... | collective-permute-start | bytes 393224 | tf_op jit(solution)/shard_map/ppermute | solution.py:46
  7.4 10.4 %collective-permute-start.2 = (bf16[256,256]{1,0:T(8,128)(2,1)}, bf16[256,256]{1,0:T(8,128)(2,1)S(1)}, u32[]{:S(2)}, u32[]{:S(2)}) collective-permute-start(bf16[256,256]{1,0:T(8,128)(2,1)} %join.1.refs_0_), channel_id=1, source_target_pairs={{0,192},{4,68},{32,224},{36,100},{64,0},{68,132},{96,32},{100,164}... | collective-permute-start | bytes 393224 | tf_op jit(solution)/shard_map/ppermute | solution.py:46
  7.4 10.4 %collective-permute-start.11 = (bf16[256,256]{1,0:T(8,128)(2,1)}, bf16[256,256]{1,0:T(8,128)(2,1)S(1)}, u32[]{:S(2)}, u32[]{:S(2)}) collective-permute-start(bf16[256,256]{1,0:T(8,128)(2,1)} %join.1.refs_0_), channel_id=1, source_target_pairs={{0,224},{4,36},{32,0},{36,68},{64,32},{68,100},{96,64},{100,132},{... | collective-permute-start | bytes 393224 | tf_op jit(solution)/shard_map/ppermute | solution.py:46
  8.2 11.0 %collective-permute-start.10 = (bf16[256,256]{1,0:T(8,128)(2,1)}, bf16[256,256]{1,0:T(8,128)(2,1)S(1)}, u32[]{:S(2)}, u32[]{:S(2)}) collective-permute-start(bf16[256,256]{1,0:T(8,128)(2,1)} %join.1.refs_0_), channel_id=1, source_target_pairs={{0,32},{4,228},{32,64},{36,4},{64,96},{68,36},{96,128},{100,68},{1... | collective-permute-start | bytes 393224 | tf_op jit(solution)/shard_map/ppermute | solution.py:46
  9.9 12.8 %collective-permute-start.6 = (bf16[256,256]{1,0:T(8,128)(2,1)S(1)}, bf16[256,256]{1,0:T(8,128)(2,1)S(1)}, u32[]{:S(2)}, u32[]{:S(2)}) collective-permute-start(bf16[256,256]{1,0:T(8,128)(2,1)S(1)} %collective-permute-done.3.refs_3_), channel_id=1, source_target_pairs={{0,64},{4,196},{32,96},{36,228},{64,128},{68,4},{96,160},{100,36},... | collective-permute-start | bytes 393224 | tf_op jit(solution)/shard_map/ppermute | solution.py:46
  14.1 8.6 %collective-permute-start.4 = (bf16[256,256]{1,0:T(8,128)(2,1)S(1)}, bf16[256,256]{1,0:T(8,128)(2,1)S(1)}, u32[]{:S(2)}, u32[]{:S(2)}) collective-permute-start(bf16[256,256]{1,0:T(8,128)(2,1)S(1)} %collective-permute-done.3.refs_3_), channel_id=1, source_target_pairs={{0,32},{4,228},{32,64},{36,4},{64,96},{68,36},{96,128},{100,68},{1... | collective-permute-start | bytes 393224 | tf_op jit(solution)/shard_map/ppermute | solution.py:46
  17.8 6.3 %collective-permute-start.5 = (bf16[256,256]{1,0:T(8,128)(2,1)S(1)}, bf16[256,256]{1,0:T(8,128)(2,1)S(1)}, u32[]{:S(2)}, u32[]{:S(2)}) collective-permute-start(bf16[256,256]{1,0:T(8,128)(2,1)S(1)} %collective-permute-done.2.refs_0_), channel_id=1, source_target_pairs={{0,224},{4,36},{32,0},{36,68},{64,32},{68,100},{96,64},{100,132},{... | collective-permute-start | bytes 393224 | tf_op jit(solution)/shard_map/ppermute | solution.py:46
  17.8 8.9 %collective-permute-start = (s32[32,32]{1,0:T(8,128)S(1)}, s32[32,32]{1,0:T(8,128)S(1)}, u32[]{:S(2)}, u32[]{:S(2)}) collective-permute-start(s32[32,32]{1,0:T(8,128)S(1)} %bitcast.17), channel_id=1, source_target_pairs={{0,1},{1,0},{2,3},{3,2},{4,5},{5,4},{6,7},{7,6},{8,9},{9,8},{10,11... | collective-permute-start | bytes 12296 | tf_op jit(solution)/shard_map/ppermute | solution.py:455
  19.2 0.9 copy-start
  20.1 11.1 %copy-start.1 = (bf16[256,512]{1,0:T(8,128)(2,1)S(1)}, bf16[256,512]{1,0:T(8,128)(2,1)}, u32[]{:S(2)}) copy-start(bf16[256,512]{1,0:T(8,128)(2,1)} %query.1) | copy-start | bytes 786436
  20.1 11.1 %copy-start.2 = (bf16[256,512]{1,0:T(8,128)(2,1)S(1)}, bf16[256,512]{1,0:T(8,128)(2,1)}, u32[]{:S(2)}) copy-start(bf16[256,512]{1,0:T(8,128)(2,1)} %grad_out.1) | copy-start | bytes 786436
  20.1 15.7 %collective-permute-start.13 = (bf16[4,256,256]{2,1,0:T(8,128)(2,1)S(1)}, bf16[4,256,256]{2,1,0:T(8,128)(2,1)S(1)}, u32[]{:S(2)}, u32[]{:S(2)}) collective-permute-start(bf16[4,256,256]{2,1,0:T(8,128)(2,1)S(1)} %stack.3.refs_0_), channel_id=1, source_target_pairs={{0,8},{4,28},{8,16},{12,4},{16,24},{20,12},{24,0},{28,20},{1,9},{5... | collective-permute-start | bytes 1572872 | tf_op jit(solution)/shard_map/ppermute | solution.py:46
  24.1 12.2 %collective-permute-start.7 = (bf16[4,256,256]{2,1,0:T(8,128)(2,1)S(1)}, bf16[4,256,256]{2,1,0:T(8,128)(2,1)S(1)}, u32[]{:S(2)}, u32[]{:S(2)}) collective-permute-start(bf16[4,256,256]{2,1,0:T(8,128)(2,1)S(1)} %stack.2.refs_1_), channel_id=1, source_target_pairs={{0,8},{4,28},{8,16},{12,4},{16,24},{20,12},{24,0},{28,20},{1,9},{5... | collective-permute-start | bytes 1572872 | tf_op jit(solution)/shard_map/ppermute | solution.py:46
  26.7 4.2 %collective-permute-start.1 = (s32[32,32]{1,0:T(8,128)S(1)}, s32[32,32]{1,0:T(8,128)S(1)}, u32[]{:S(2)}, u32[]{:S(2)}) collective-permute-start(s32[32,32]{1,0:T(8,128)S(1)} %bitcast_add_fusion.1), channel_id=1, source_target_pairs={{0,2},{2,0},{1,3},{3,1},{4,6},{6,4},{5,7},{7,5},{8,10},{10,8},{9,1... | collective-permute-start | bytes 12296 | tf_op jit(solution)/shard_map/ppermute | solution.py:456
  30.9 15.3 %collective-permute-start.12 = (bf16[4,256,256]{2,1,0:T(8,128)(2,1)S(1)}, bf16[4,256,256]{2,1,0:T(8,128)(2,1)S(1)}, u32[]{:S(2)}, u32[]{:S(2)}) collective-permute-start(bf16[4,256,256]{2,1,0:T(8,128)(2,1)S(1)} %stack.3.refs_0_), channel_id=1, source_target_pairs={{0,24},{4,12},{8,0},{12,20},{16,8},{20,28},{24,16},{28,4},{1,25},{... | collective-permute-start | bytes 1572872 | tf_op jit(solution)/shard_map/ppermute | solution.py:46
  31.0 26.4 %collective-permute-start.15 = (bf16[4,256,256]{2,1,0:T(8,128)(2,1)S(1)}, bf16[4,256,256]{2,1,0:T(8,128)(2,1)S(1)}, u32[]{:S(2)}, u32[]{:S(2)}) collective-permute-start(bf16[4,256,256]{2,1,0:T(8,128)(2,1)S(1)} %stack.2.refs_1_), channel_id=1, source_target_pairs={{0,24},{4,12},{8,0},{12,20},{16,8},{20,28},{24,16},{28,4},{1,25},{... | collective-permute-start | bytes 1572872 | tf_op jit(solution)/shard_map/ppermute | solution.py:46
  31.3 6.7 %collective-permute-start.9 = (bf16[2,1024,128]{2,1,0:T(8,128)(2,1)S(1)}, bf16[2,1024,128]{2,1,0:T(8,128)(2,1)S(1)}, u32[]{:S(2)}, u32[]{:S(2)}) collective-permute-start(bf16[2,1024,128]{2,1,0:T(8,128)(2,1)S(1)} %prepare.1.refs_4_.refs_3_.refs_1_.refs_2_), channel_id=1, source_target_pairs={{0,4},{4,0},{1,5},{5,1},{2,6},{6,2},{3,7},{7,3},{8,12},{12,8},{9,1... | collective-permute-start | bytes 1572872 | tf_op jit(solution)/shard_map/ppermute | solution.py:50
  35.8 21.6 %collective-permute-start.14 = (bf16[4,256,256]{2,1,0:T(8,128)(2,1)S(1)}, bf16[4,256,256]{2,1,0:T(8,128)(2,1)S(1)}, u32[]{:S(2)}, u32[]{:S(2)}) collective-permute-start(bf16[4,256,256]{2,1,0:T(8,128)(2,1)S(1)} %collective-permute-done.13.refs_2_.refs_0_), channel_id=1, source_target_pairs={{0,8},{4,28},{8,16},{12,4},{16,24},{20,12},{24,0},{28,20},{1,9},{5... | collective-permute-start | bytes 1572872 | tf_op jit(solution)/shard_map/ppermute | solution.py:46
  36.4 24.3 %collective-permute-start.8 = (bf16[4,256,256]{2,1,0:T(8,128)(2,1)S(1)}, bf16[4,256,256]{2,1,0:T(8,128)(2,1)S(1)}, u32[]{:S(2)}, u32[]{:S(2)}) collective-permute-start(bf16[4,256,256]{2,1,0:T(8,128)(2,1)S(1)} %collective-permute-done.7.refs_3_.refs_1_), channel_id=1, source_target_pairs={{0,8},{4,28},{8,16},{12,4},{16,24},{20,12},{24,0},{28,20},{1,9},{5... | collective-permute-start | bytes 1572872 | tf_op jit(solution)/shard_map/ppermute | solution.py:46
  61.7 1.8 %collective-permute-start.16 = (f32[2,3,1024]{2,1,0:T(4,128)S(1)}, f32[2,3,1024]{2,1,0:T(4,128)S(1)}, u32[]{:S(2)}, u32[]{:S(2)}) collective-permute-start(f32[2,3,1024]{2,1,0:T(4,128)S(1)} %get-tuple-element.51.refs_3_.refs_4_.mine), channel_id=1, source_target_pairs={{0,4},{4,0},{1,5},{5,1},{2,6},{6,2},{3,7},{7,3},{8,12},{12,8},{9,1... | collective-permute-start | bytes 73736 | tf_op jit(solution)/shard_map/ppermute | solution.py:50
  64.4 15.3 %collective-permute-start.24 = (bf16[4,256,256]{2,1,0:T(8,128)(2,1)S(1)}, bf16[4,256,256]{2,1,0:T(8,128)(2,1)S(1)}, u32[]{:S(2)}, u32[]{:S(2)}) collective-permute-start(bf16[4,256,256]{2,1,0:T(8,128)(2,1)S(1)} %get-tuple-element.75), channel_id=1, source_target_pairs={{0,24},{4,12},{8,0},{12,20},{16,8},{20,28},{24,16},{28,4},{1,25},{... | collective-permute-start | bytes 1572872 | tf_op jit(solution)/shard_map/ppermute | solution.py:46
  66.9 13.2 %collective-permute-start.19 = (bf16[4,256,256]{2,1,0:T(8,128)(2,1)S(1)}, bf16[4,256,256]{2,1,0:T(8,128)(2,1)S(1)}, u32[]{:S(2)}, u32[]{:S(2)}) collective-permute-start(bf16[4,256,256]{2,1,0:T(8,128)(2,1)S(1)} %get-tuple-element.68), channel_id=1, source_target_pairs={{0,24},{4,12},{8,0},{12,20},{16,8},{20,28},{24,16},{28,4},{1,25},{... | collective-permute-start | bytes 1572872 | tf_op jit(solution)/shard_map/ppermute | solution.py:46
  71.8 30.9 %collective-permute-start.21 = (bf16[4,256,256]{2,1,0:T(8,128)(2,1)S(1)}, bf16[4,256,256]{2,1,0:T(8,128)(2,1)S(1)}, u32[]{:S(2)}, u32[]{:S(2)}) collective-permute-start(bf16[4,256,256]{2,1,0:T(8,128)(2,1)S(1)} %get-tuple-element.69), channel_id=1, source_target_pairs={{0,8},{4,28},{8,16},{12,4},{16,24},{20,12},{24,0},{28,20},{1,9},{5... | collective-permute-start | bytes 1572872 | tf_op jit(solution)/shard_map/ppermute | solution.py:46
  75.6 22.8 %collective-permute-start.26 = (bf16[4,256,256]{2,1,0:T(8,128)(2,1)S(1)}, bf16[4,256,256]{2,1,0:T(8,128)(2,1)S(1)}, u32[]{:S(2)}, u32[]{:S(2)}) collective-permute-start(bf16[4,256,256]{2,1,0:T(8,128)(2,1)S(1)} %get-tuple-element.76), channel_id=1, source_target_pairs={{0,8},{4,28},{8,16},{12,4},{16,24},{20,12},{24,0},{28,20},{1,9},{5... | collective-permute-start | bytes 1572872 | tf_op jit(solution)/shard_map/ppermute | solution.py:46
  79.8 18.6 %collective-permute-start.25 = (bf16[4,256,256]{2,1,0:T(8,128)(2,1)S(1)}, bf16[4,256,256]{2,1,0:T(8,128)(2,1)S(1)}, u32[]{:S(2)}, u32[]{:S(2)}) collective-permute-start(bf16[4,256,256]{2,1,0:T(8,128)(2,1)S(1)} %add_convert_fusion), channel_id=1, source_target_pairs={{0,24},{4,12},{8,0},{12,20},{16,8},{20,28},{24,16},{28,4},{1,25},{... | collective-permute-start | bytes 1572872 | tf_op jit(solution)/shard_map/ppermute | solution.py:46
  80.2 25.6 %collective-permute-start.20 = (bf16[4,256,256]{2,1,0:T(8,128)(2,1)S(1)}, bf16[4,256,256]{2,1,0:T(8,128)(2,1)S(1)}, u32[]{:S(2)}, u32[]{:S(2)}) collective-permute-start(bf16[4,256,256]{2,1,0:T(8,128)(2,1)S(1)} %add_convert_fusion.1), channel_id=1, source_target_pairs={{0,24},{4,12},{8,0},{12,20},{16,8},{20,28},{24,16},{28,4},{1,25},{... | collective-permute-start | bytes 1572872 | tf_op jit(solution)/shard_map/ppermute | solution.py:46
  81.5 34.2 %collective-permute-start.17 = (f32[128,1024]{1,0:T(8,128)S(1)}, f32[128,1024]{1,0:T(8,128)S(1)}, u32[]{:S(2)}, u32[]{:S(2)}) collective-permute-start(f32[128,1024]{1,0:T(8,128)S(1)} %get-tuple-element.53), channel_id=1, source_target_pairs={{0,4},{4,0},{1,5},{5,1},{2,6},{6,2},{3,7},{7,3},{8,12},{12,8},{9,1... | collective-permute-start | bytes 1572872 | tf_op jit(solution)/shard_map/ppermute | solution.py:50
  98.4 17.4 %collective-permute-start.18 = (f32[128,1024]{1,0:T(8,128)S(1)}, f32[128,1024]{1,0:T(8,128)S(1)}, u32[]{:S(2)}, u32[]{:S(2)}) collective-permute-start(f32[128,1024]{1,0:T(8,128)S(1)} %get-tuple-element.63), channel_id=1, source_target_pairs={{0,4},{4,0},{1,5},{5,1},{2,6},{6,2},{3,7},{7,3},{8,12},{12,8},{9,1... | collective-permute-start | bytes 1572872 | tf_op jit(solution)/shard_map/ppermute | solution.py:50
  98.6 8.8 %collective-permute-start.27 = (bf16[256,256]{1,0:T(8,128)(2,1)S(1)}, bf16[256,256]{1,0:T(8,128)(2,1)S(1)}, u32[]{:S(2)}, u32[]{:S(2)}) collective-permute-start(bf16[256,256]{1,0:T(8,128)(2,1)S(1)} %get-tuple-element.79), channel_id=1, source_target_pairs={{0,224},{4,36},{32,0},{36,68},{64,32},{68,100},{96,64},{100,132},{... | collective-permute-start | bytes 393224 | tf_op jit(solution)/shard_map/ppermute | solution.py:46
  102.7 6.9 %collective-permute-start.28 = (bf16[256,256]{1,0:T(8,128)(2,1)S(1)}, bf16[256,256]{1,0:T(8,128)(2,1)S(1)}, u32[]{:S(2)}, u32[]{:S(2)}) collective-permute-start(bf16[256,256]{1,0:T(8,128)(2,1)S(1)} %get-tuple-element.80), channel_id=1, source_target_pairs={{0,192},{4,68},{32,224},{36,100},{64,0},{68,132},{96,32},{100,164}... | collective-permute-start | bytes 393224 | tf_op jit(solution)/shard_map/ppermute | solution.py:46
  105.8 6.1 %collective-permute-start.29 = (bf16[256,256]{1,0:T(8,128)(2,1)S(1)}, bf16[256,256]{1,0:T(8,128)(2,1)S(1)}, u32[]{:S(2)}, u32[]{:S(2)}) collective-permute-start(bf16[256,256]{1,0:T(8,128)(2,1)S(1)} %get-tuple-element.81), channel_id=1, source_target_pairs={{0,32},{4,228},{32,64},{36,4},{64,96},{68,36},{96,128},{100,68},{1... | collective-permute-start | bytes 393224 | tf_op jit(solution)/shard_map/ppermute | solution.py:46
  107.4 9.4 %collective-permute-start.22 = (bf16[256,256]{1,0:T(8,128)(2,1)S(1)}, bf16[256,256]{1,0:T(8,128)(2,1)S(1)}, u32[]{:S(2)}, u32[]{:S(2)}) collective-permute-start(bf16[256,256]{1,0:T(8,128)(2,1)S(1)} %get-tuple-element.71), channel_id=1, source_target_pairs={{0,224},{4,36},{32,0},{36,68},{64,32},{68,100},{96,64},{100,132},{... | collective-permute-start | bytes 393224 | tf_op jit(solution)/shard_map/ppermute | solution.py:46
  109.5 7.2 %collective-permute-start.23 = (bf16[256,256]{1,0:T(8,128)(2,1)S(1)}, bf16[256,256]{1,0:T(8,128)(2,1)S(1)}, u32[]{:S(2)}, u32[]{:S(2)}) collective-permute-start(bf16[256,256]{1,0:T(8,128)(2,1)S(1)} %get-tuple-element.72), channel_id=1, source_target_pairs={{0,32},{4,228},{32,64},{36,4},{64,96},{68,36},{96,128},{100,68},{1... | collective-permute-start | bytes 393224 | tf_op jit(solution)/shard_map/ppermute | solution.py:46
  112.0 7.0 %collective-permute-start.30 = (bf16[256,256]{1,0:T(8,128)(2,1)S(1)}, bf16[256,256]{1,0:T(8,128)(2,1)S(1)}, u32[]{:S(2)}, u32[]{:S(2)}) collective-permute-start(bf16[256,256]{1,0:T(8,128)(2,1)S(1)} %get-tuple-element.82), channel_id=1, source_target_pairs={{0,64},{4,196},{32,96},{36,228},{64,128},{68,4},{96,160},{100,36},... | collective-permute-start | bytes 393224 | tf_op jit(solution)/shard_map/ppermute | solution.py:46
  115.7 9.8 %collective-permute-start.31 = (bf16[256,256]{1,0:T(8,128)(2,1)S(1)}, bf16[256,256]{1,0:T(8,128)(2,1)S(1)}, u32[]{:S(2)}, u32[]{:S(2)}) collective-permute-start(bf16[256,256]{1,0:T(8,128)(2,1)S(1)} %get-tuple-element.83), channel_id=1, source_target_pairs={{0,192},{4,68},{32,224},{36,100},{64,0},{68,132},{96,32},{100,164}... | collective-permute-start | bytes 393224 | tf_op jit(solution)/shard_map/ppermute | solution.py:46

commit v5 on v3

--- a/solution.py
+++ b/solution.py
@@ -494,9 +494,9 @@
     high2 = shift(high2, "x", -1)
     dq, (low2,) = backward((16,), info, [low2], qg, mine, other, dq)
     low2 = shift(low2, "x", -1)
+    dq, (low1, high1) = backward((8, 12), info, [low1, high1], qg, mine, other, dq)
     dq, (low3, high3) = backward((24, 28), info, [low3, high3], qg, mine, other, dq)
     high3, low3 = shift(high3, "x", 1), shift(low3, "x", 1)
-    dq, (low1, high1) = backward((8, 12), info, [low1, high1], qg, mine, other, dq)
     high1 = shift((wide(high1) + wide(high2)).astype(BF), "x", -1)
     low1 = shift((wide(low1) + wide(low2)).astype(BF), "x", -1)
     dq, (low0, high0) = backward((0, 4), info, [low0, high0], qg, mine, other, dq)

time: 127 us -> 136 us (1.071); the launches traced: 125 us -> 137 us
  starting transfers between devices: 64.7 us -> 71.5 us
  waiting for transfers between devices: 42.8 us -> 48.2 us
    ppermute x26, starting transfers between devices: 47.1 us -> 56 us  [shift(): lax.ppermute(a, (axis, 'core'), [(2 * i + c, 2 * ((i + d * (1 - 2 * c)) %...]
    ppermute x26, waiting for transfers between devices: 40.8 us -> 46.1 us  [shift(): lax.ppermute(a, (axis, 'core'), [(2 * i + c, 2 * ((i + d * (1 - 2 * c)) %...]
    ppermute x4, starting transfers between devices: 13.4 us -> 11.3 us  [swap(): return lax.ppermute(a, 'core', [(0, 1), (1, 0)])]
where the time goes in v5:
time: 136 us; the launch traced here: 137 us
  starting transfers between devices  71.5 us (53%)
  waiting for transfers between devices  48.2 us (35%)
  Pallas kernels  14.9 us (11%)
    ppermute x26, starting transfers between devices, shift(): lax.ppermute(a, (axis, 'core'), [(2 * i + c, 2 * ((i + d * (1 - 2 * c)) %...  56 us
    ppermute x26, waiting for transfers between devices, shift(): lax.ppermute(a, (axis, 'core'), [(2 * i + c, 2 * ((i + d * (1 - 2 * c)) %...  46.1 us
    ppermute x4, starting transfers between devices, swap(): return lax.ppermute(a, 'core', [(0, 1), (1, 0)])  11.3 us
    pallas_call x5, Pallas kernels, backward(): pl.pallas_call(functools.partial(backward_kernel, bases, first, bases[0]...  6.53 us
    pallas_call x3, Pallas kernels, forward(): pl.pallas_call(functools.partial(forward_kernel, bases, first, last), gri...  4.46 us
    ppermute x1, starting transfers between devices, plan(): lax.ppermute(totals, 'head', [(0, 2), (2, 0), (1, 3), (3, 1)])  3 us
  transfers between devices with their start and end apart: 32, of which 14 were waited for; matrix products, arithmetic and copies ran while one was open for 1% of the time, Pallas kernels for 8%

profile of v5, /device:TPU:1, one launch (start us, length us, event | category | flops | bytes accessed | tf_op | source)
XLA Modules:
  0.0 137.0 jit_solution(9198239228051724072)
XLA Ops:
  0.6 1.5 %join.1.refs_0_ = bf16[256,256]{1,0:T(8,128)(2,1)} custom-call(bf16[256,128]{1,0:T(8,128)(2,1)} %k_ref.1, bf16[256,128]{1,0:T(8,128)(2,1)} %v_ref.1), custom_call_target="tpu_custom_call" | custom-call | tf_op jit(solution)/shard_map/join/pallas_call | solution.py:335
  2.2 6.9 %collective-permute-start.3 = (bf16[256,256]{1,0:T(8,128)(2,1)}, bf16[256,256]{1,0:T(8,128)(2,1)S(1)}, u32[]{:S(2)}, u32[]{:S(2)}) collective-permute-start(bf16[256,256]{1,0:T(8,128)(2,1)} %join.1.refs_0_), channel_id=1, source_target_pairs={{0,64},{4,196},{32,96},{36,228},{64,128},{68,4},{96,160},{100,36},... | collective-permute-start | bytes 393224 | tf_op jit(solution)/shard_map/ppermute | solution.py:46
  9.1 0.7 collective-permute-start.12
  9.9 2.4 %collective-permute-start.11 = (bf16[256,256]{1,0:T(8,128)(2,1)}, bf16[256,256]{1,0:T(8,128)(2,1)S(1)}, u32[]{:S(2)}, u32[]{:S(2)}) collective-permute-start(bf16[256,256]{1,0:T(8,128)(2,1)} %join.1.refs_0_), channel_id=1, source_target_pairs={{0,32},{4,228},{32,64},{36,4},{64,96},{68,36},{96,128},{100,68},{1... | collective-permute-start | bytes 393224 | tf_op jit(solution)/shard_map/ppermute | solution.py:46
  12.3 1.9 %collective-permute-done.3.refs_3_ = bf16[256,256]{1,0:T(8,128)(2,1)S(1)} collective-permute-done((bf16[256,256]{1,0:T(8,128)(2,1)}, bf16[256,256]{1,0:T(8,128)(2,1)S(1)}, u32[]{:S(2)}, u32[]{:S(2)}) %collective-permute-start.3) | collective-permute-done | bytes 131104 | tf_op jit(solution)/shard_map/ppermute | solution.py:46
  14.2 4.6 %collective-permute-start.6 = (bf16[256,256]{1,0:T(8,128)(2,1)S(1)}, bf16[256,256]{1,0:T(8,128)(2,1)S(1)}, u32[]{:S(2)}, u32[]{:S(2)}) collective-permute-start(bf16[256,256]{1,0:T(8,128)(2,1)S(1)} %collective-permute-done.3.refs_3_), channel_id=1, source_target_pairs={{0,64},{4,196},{32,96},{36,228},{64,128},{68,4},{96,160},{100,36},... | collective-permute-start | bytes 393224 | tf_op jit(solution)/shard_map/ppermute | solution.py:46
  18.8 1.5 %collective-permute-start.5 = (bf16[256,256]{1,0:T(8,128)(2,1)S(1)}, bf16[256,256]{1,0:T(8,128)(2,1)S(1)}, u32[]{:S(2)}, u32[]{:S(2)}) collective-permute-start(bf16[256,256]{1,0:T(8,128)(2,1)S(1)} %collective-permute-done.2.refs_0_), channel_id=1, source_target_pairs={{0,224},{4,36},{32,0},{36,68},{64,32},{68,100},{96,64},{100,132},{... | collective-permute-start | bytes 393224 | tf_op jit(solution)/shard_map/ppermute | solution.py:46
  20.2 1.3 collective-permute-start
  21.5 0.9 copy-done
  22.5 0.0 copy-start.2
  22.5 2.6 %collective-permute-start.14 = (bf16[4,256,256]{2,1,0:T(8,128)(2,1)S(1)}, bf16[4,256,256]{2,1,0:T(8,128)(2,1)S(1)}, u32[]{:S(2)}, u32[]{:S(2)}) collective-permute-start(bf16[4,256,256]{2,1,0:T(8,128)(2,1)S(1)} %stack.3.refs_0_), channel_id=1, source_target_pairs={{0,8},{4,28},{8,16},{12,4},{16,24},{20,12},{24,0},{28,20},{1,9},{5... | collective-permute-start | bytes 1572872 | tf_op jit(solution)/shard_map/ppermute | solution.py:46
  25.1 1.0 collective-permute-done.5.refs_2_
  26.1 2.6 %collective-permute-start.8 = (bf16[4,256,256]{2,1,0:T(8,128)(2,1)S(1)}, bf16[4,256,256]{2,1,0:T(8,128)(2,1)S(1)}, u32[]{:S(2)}, u32[]{:S(2)}) collective-permute-start(bf16[4,256,256]{2,1,0:T(8,128)(2,1)S(1)} %stack.2.refs_1_), channel_id=1, source_target_pairs={{0,8},{4,28},{8,16},{12,4},{16,24},{20,12},{24,0},{28,20},{1,9},{5... | collective-permute-start | bytes 1572872 | tf_op jit(solution)/shard_map/ppermute | solution.py:46
  28.7 3.0 %collective-permute-start.1 = (s32[32,32]{1,0:T(8,128)S(1)}, s32[32,32]{1,0:T(8,128)S(1)}, u32[]{:S(2)}, u32[]{:S(2)}) collective-permute-start(s32[32,32]{1,0:T(8,128)S(1)} %bitcast_add_fusion.1), channel_id=1, source_target_pairs={{0,2},{2,0},{1,3},{3,1},{4,6},{6,4},{5,7},{7,5},{8,10},{10,8},{9,1... | collective-permute-start | bytes 12296 | tf_op jit(solution)/shard_map/ppermute | solution.py:456
  31.7 1.1 collective-permute-done.1
  32.9 0.1 collective-permute-start.13
  32.9 0.2 collective-permute-start.7
  33.1 0.1 prepare.1.refs_4_.refs_2_.refs_1_
  33.2 4.3 %collective-permute-start.10 = (bf16[2,1024,128]{2,1,0:T(8,128)(2,1)S(1)}, bf16[2,1024,128]{2,1,0:T(8,128)(2,1)S(1)}, u32[]{:S(2)}, u32[]{:S(2)}) collective-permute-start(bf16[2,1024,128]{2,1,0:T(8,128)(2,1)S(1)} %prepare.1.refs_4_.refs_2_.refs_1_), channel_id=1, source_target_pairs={{0,4},{4,0},{1,5},{5,1},{2,6},{6,2},{3,7},{7,3},{8,12},{12,8},{9,1... | collective-permute-start | bytes 1572872 | tf_op jit(solution)/shard_map/ppermute | solution.py:50
  37.5 0.5 collective-permute-start.15
  38.1 2.4 %collective-permute-start.9 = (bf16[4,256,256]{2,1,0:T(8,128)(2,1)S(1)}, bf16[4,256,256]{2,1,0:T(8,128)(2,1)S(1)}, u32[]{:S(2)}, u32[]{:S(2)}) collective-permute-start(bf16[4,256,256]{2,1,0:T(8,128)(2,1)S(1)} %collective-permute-done.8.refs_3_.refs_1_), channel_id=1, source_target_pairs={{0,8},{4,28},{8,16},{12,4},{16,24},{20,12},{24,0},{28,20},{1,9},{5... | collective-permute-start | bytes 1572872 | tf_op jit(solution)/shard_map/ppermute | solution.py:46
  40.5 0.2 convert_reduce_fusion.1
  40.7 0.1 convert_reduce_fusion
  40.8 0.1 pad_add_fusion.info
  40.9 2.4 %forward.3 = (f32[2,3,1024]{2,1,0:T(4,128)S(1)}, f32[128,1024]{1,0:T(8,128)S(1)}, f32[128,1024]{1,0:T(8,128)S(1)}) custom-call(s32[33]{0:T(128)S(1)} %pad_add_fusion.info, bf16[4,256,256]{2,1,0:T(8,128)(2,1)S(1)} %stack.3.refs_0_, bf16[4,256,256]{2,1,0:T(8,128)(2,1)S(1)} %stack.2.refs_1_, bf16[4,256,256]{2,1,0:T(8,128)(2,1)S(1)} %collective-permute-done.14.refs_2_.refs_0_, ...), custom_call_target="tpu_custom_call" | custom-call | flops 200000000 | bytes 65536 | tf_op jit(solution)/shard_map/forward/pallas_call | solution.py:253
  43.3 4.9 %collective-permute-done.13.refs_0_ = bf16[4,256,256]{2,1,0:T(8,128)(2,1)S(1)} collective-permute-done((bf16[4,256,256]{2,1,0:T(8,128)(2,1)S(1)}, bf16[4,256,256]{2,1,0:T(8,128)(2,1)S(1)}, u32[]{:S(2)}, u32[]{:S(2)}) %collective-permute-start.13) | collective-permute-done | bytes 524320 | tf_op jit(solution)/shard_map/ppermute | solution.py:46
  48.2 3.4 %collective-permute-done.15.refs_1_.refs_0_ = bf16[4,256,256]{2,1,0:T(8,128)(2,1)S(1)} collective-permute-done((bf16[4,256,256]{2,1,0:T(8,128)(2,1)S(1)}, bf16[4,256,256]{2,1,0:T(8,128)(2,1)S(1)}, u32[]{:S(2)}, u32[]{:S(2)}) %collective-permute-start.15) | collective-permute-done | bytes 524320 | tf_op jit(solution)/shard_map/ppermute | solution.py:46
  51.5 0.9 forward.4
  52.4 7.0 %collective-permute-done.7.refs_0_.refs_1_ = bf16[4,256,256]{2,1,0:T(8,128)(2,1)S(1)} collective-permute-done((bf16[4,256,256]{2,1,0:T(8,128)(2,1)S(1)}, bf16[4,256,256]{2,1,0:T(8,128)(2,1)S(1)}, u32[]{:S(2)}, u32[]{:S(2)}) %collective-permute-start.7) | collective-permute-done | bytes 524320 | tf_op jit(solution)/shard_map/ppermute | solution.py:46
  59.4 0.3 collective-permute-done.9.refs_1_.refs_0_
  59.7 1.2 forward.5
  60.9 2.8 %collective-permute-start.16 = (f32[2,3,1024]{2,1,0:T(4,128)S(1)}, f32[2,3,1024]{2,1,0:T(4,128)S(1)}, u32[]{:S(2)}, u32[]{:S(2)}) collective-permute-start(f32[2,3,1024]{2,1,0:T(4,128)S(1)} %get-tuple-element.51.refs_3_.refs_4_.mine), channel_id=1, source_target_pairs={{0,4},{4,0},{1,5},{5,1},{2,6},{6,2},{3,7},{7,3},{8,12},{12,8},{9,1... | collective-permute-start | bytes 73736 | tf_op jit(solution)/shard_map/ppermute | solution.py:50
  63.7 0.9 collective-permute-done.16.refs_4_.refs_5_.other
  64.5 0.8 backward.5
  65.4 0.1 collective-permute-start.24
  65.5 0.8 backward.6
  66.3 1.3 collective-permute-start.19
  67.6 1.1 backward.7
  68.6 1.1 backward.8
  69.7 6.5 %collective-permute-start.21 = (bf16[4,256,256]{2,1,0:T(8,128)(2,1)S(1)}, bf16[4,256,256]{2,1,0:T(8,128)(2,1)S(1)}, u32[]{:S(2)}, u32[]{:S(2)}) collective-permute-start(bf16[4,256,256]{2,1,0:T(8,128)(2,1)S(1)} %get-tuple-element.69), channel_id=1, source_target_pairs={{0,8},{4,28},{8,16},{12,4},{16,24},{20,12},{24,0},{28,20},{1,9},{5... | collective-permute-start | bytes 1572872 | tf_op jit(solution)/shard_map/ppermute | solution.py:46
  76.2 0.1 collective-permute-start.26
  76.3 0.1 add_convert_fusion
  76.4 1.5 %collective-permute-start.25 = (bf16[4,256,256]{2,1,0:T(8,128)(2,1)S(1)}, bf16[4,256,256]{2,1,0:T(8,128)(2,1)S(1)}, u32[]{:S(2)}, u32[]{:S(2)}) collective-permute-start(bf16[4,256,256]{2,1,0:T(8,128)(2,1)S(1)} %add_convert_fusion), channel_id=1, source_target_pairs={{0,24},{4,12},{8,0},{12,20},{16,8},{20,28},{24,16},{28,4},{1,25},{... | collective-permute-start | bytes 1572872 | tf_op jit(solution)/shard_map/ppermute | solution.py:46
  77.9 5.3 %collective-permute-done.19 = bf16[4,256,256]{2,1,0:T(8,128)(2,1)S(1)} collective-permute-done((bf16[4,256,256]{2,1,0:T(8,128)(2,1)S(1)}, bf16[4,256,256]{2,1,0:T(8,128)(2,1)S(1)}, u32[]{:S(2)}, u32[]{:S(2)}) %collective-permute-start.19) | collective-permute-done | bytes 524320 | tf_op jit(solution)/shard_map/ppermute | solution.py:46
  83.2 0.1 add_convert_fusion.1
  83.4 0.1 collective-permute-start.20
  83.4 2.6 %collective-permute-start.17 = (f32[128,1024]{1,0:T(8,128)S(1)}, f32[128,1024]{1,0:T(8,128)S(1)}, u32[]{:S(2)}, u32[]{:S(2)}) collective-permute-start(f32[128,1024]{1,0:T(8,128)S(1)} %get-tuple-element.53), channel_id=1, source_target_pairs={{0,4},{4,0},{1,5},{5,1},{2,6},{6,2},{3,7},{7,3},{8,12},{12,8},{9,1... | collective-permute-start | bytes 1572872 | tf_op jit(solution)/shard_map/ppermute | solution.py:50
  86.1 2.7 %backward.9 = (f32[128,1024]{1,0:T(8,128)S(1)}, f32[128,1024]{1,0:T(8,128)S(1)}, bf16[4,256,256]{2,1,0:T(8,128)(2,1)S(1)}, bf16[4,256,256]{2,1,0:T(8,128)(2,1)S(1)}) custom-call(s32[33]{0:T(128)S(1)} %pad_add_fusion.info, bf16[4,256,256]{2,1,0:T(8,128)(2,1)S(1)} %stack.3.refs_0_, bf16[4,256,256]{2,1,0:T(8,128)(2,1)S(1)} %stack.2.refs_1_, ...), custom_call_target="tpu_custom_call" | custom-call | flops 200000000 | bytes 65536 | tf_op jit(solution)/shard_map/backward/pallas_call | solution.py:281
  88.8 10.5 %collective-permute-done.26.three = bf16[4,256,256]{2,1,0:T(8,128)(2,1)S(1)} collective-permute-done((bf16[4,256,256]{2,1,0:T(8,128)(2,1)S(1)}, bf16[4,256,256]{2,1,0:T(8,128)(2,1)S(1)}, u32[]{:S(2)}, u32[]{:S(2)}) %collective-permute-start.26) | collective-permute-done | bytes 524320 | tf_op jit(solution)/shard_map/ppermute | solution.py:46
  99.2 1.6 %collective-permute-start.18 = (f32[128,1024]{1,0:T(8,128)S(1)}, f32[128,1024]{1,0:T(8,128)S(1)}, u32[]{:S(2)}, u32[]{:S(2)}) collective-permute-start(f32[128,1024]{1,0:T(8,128)S(1)} %get-tuple-element.63), channel_id=1, source_target_pairs={{0,4},{4,0},{1,5},{5,1},{2,6},{6,2},{3,7},{7,3},{8,12},{12,8},{9,1... | collective-permute-start | bytes 1572872 | tf_op jit(solution)/shard_map/ppermute | solution.py:50
  100.8 0.2 sum_high.1
  101.0 3.7 %collective-permute-start.27 = (bf16[256,256]{1,0:T(8,128)(2,1)S(1)}, bf16[256,256]{1,0:T(8,128)(2,1)S(1)}, u32[]{:S(2)}, u32[]{:S(2)}) collective-permute-start(bf16[256,256]{1,0:T(8,128)(2,1)S(1)} %get-tuple-element.79), channel_id=1, source_target_pairs={{0,224},{4,36},{32,0},{36,68},{64,32},{68,100},{96,64},{100,132},{... | collective-permute-start | bytes 393224 | tf_op jit(solution)/shard_map/ppermute | solution.py:46
  104.8 11.2 %collective-permute-start.28 = (bf16[256,256]{1,0:T(8,128)(2,1)S(1)}, bf16[256,256]{1,0:T(8,128)(2,1)S(1)}, u32[]{:S(2)}, u32[]{:S(2)}) collective-permute-start(bf16[256,256]{1,0:T(8,128)(2,1)S(1)} %get-tuple-element.80), channel_id=1, source_target_pairs={{0,192},{4,68},{32,224},{36,100},{64,0},{68,132},{96,32},{100,164}... | collective-permute-start | bytes 393224 | tf_op jit(solution)/shard_map/ppermute | solution.py:46
  115.9 0.2 sum_low.1
  116.1 0.0 collective-permute-done.27.down
  116.2 2.5 %collective-permute-start.22 = (bf16[256,256]{1,0:T(8,128)(2,1)S(1)}, bf16[256,256]{1,0:T(8,128)(2,1)S(1)}, u32[]{:S(2)}, u32[]{:S(2)}) collective-permute-start(bf16[256,256]{1,0:T(8,128)(2,1)S(1)} %get-tuple-element.71), channel_id=1, source_target_pairs={{0,224},{4,36},{32,0},{36,68},{64,32},{68,100},{96,64},{100,132},{... | collective-permute-start | bytes 393224 | tf_op jit(solution)/shard_map/ppermute | solution.py:46
  118.6 1.5 %collective-permute-done.28.far = bf16[256,256]{1,0:T(8,128)(2,1)S(1)} collective-permute-done((bf16[256,256]{1,0:T(8,128)(2,1)S(1)}, bf16[256,256]{1,0:T(8,128)(2,1)S(1)}, u32[]{:S(2)}, u32[]{:S(2)}) %collective-permute-start.28) | collective-permute-done | bytes 131104 | tf_op jit(solution)/shard_map/ppermute | solution.py:46
  120.2 2.6 %collective-permute-done.29.up = bf16[256,256]{1,0:T(8,128)(2,1)S(1)} collective-permute-done((bf16[256,256]{1,0:T(8,128)(2,1)S(1)}, bf16[256,256]{1,0:T(8,128)(2,1)S(1)}, u32[]{:S(2)}, u32[]{:S(2)}) %collective-permute-start.29) | collective-permute-done | bytes 131104 | tf_op jit(solution)/shard_map/ppermute | solution.py:46
  122.8 0.1 sum_two.1
  122.9 4.7 %collective-permute-start.30 = (bf16[256,256]{1,0:T(8,128)(2,1)S(1)}, bf16[256,256]{1,0:T(8,128)(2,1)S(1)}, u32[]{:S(2)}, u32[]{:S(2)}) collective-permute-start(bf16[256,256]{1,0:T(8,128)(2,1)S(1)} %get-tuple-element.82), channel_id=1, source_target_pairs={{0,64},{4,196},{32,96},{36,228},{64,128},{68,4},{96,160},{100,36},... | collective-permute-start | bytes 393224 | tf_op jit(solution)/shard_map/ppermute | solution.py:46
  127.6 1.0 finish.1
  128.6 3.2 %collective-permute-done.30.c = bf16[256,256]{1,0:T(8,128)(2,1)S(1)} collective-permute-done((bf16[256,256]{1,0:T(8,128)(2,1)S(1)}, bf16[256,256]{1,0:T(8,128)(2,1)S(1)}, u32[]{:S(2)}, u32[]{:S(2)}) %collective-permute-start.30) | collective-permute-done | bytes 131104 | tf_op jit(solution)/shard_map/ppermute | solution.py:46
  131.8 4.4 %collective-permute-done.31.d = bf16[256,256]{1,0:T(8,128)(2,1)S(1)} collective-permute-done((bf16[256,256]{1,0:T(8,128)(2,1)S(1)}, bf16[256,256]{1,0:T(8,128)(2,1)S(1)}, u32[]{:S(2)}, u32[]{:S(2)}) %collective-permute-start.31) | collective-permute-done | bytes 131104 | tf_op jit(solution)/shard_map/ppermute | solution.py:46
  136.3 0.7 close.1
  (35 shorter events, 0.2 us)
Async XLA Ops:
  0.6 19.6 %copy-start.3 = (s32[1,32,32]{2,1,0:T(8,128)S(1)}, s32[1,32,32]{2,1,0:T(8,128)}, u32[]{:S(2)}) copy-start(s32[1,32,32]{2,1,0:T(8,128)} %param.9) | copy-start | bytes 12292
  2.2 12.0 %collective-permute-start.3 = (bf16[256,256]{1,0:T(8,128)(2,1)}, bf16[256,256]{1,0:T(8,128)(2,1)S(1)}, u32[]{:S(2)}, u32[]{:S(2)}) collective-permute-start(bf16[256,256]{1,0:T(8,128)(2,1)} %join.1.refs_0_), channel_id=1, source_target_pairs={{0,64},{4,196},{32,96},{36,228},{64,128},{68,4},{96,160},{100,36},... | collective-permute-start | bytes 393224 | tf_op jit(solution)/shard_map/ppermute | solution.py:46
  9.1 9.6 %collective-permute-start.2 = (bf16[256,256]{1,0:T(8,128)(2,1)}, bf16[256,256]{1,0:T(8,128)(2,1)S(1)}, u32[]{:S(2)}, u32[]{:S(2)}) collective-permute-start(bf16[256,256]{1,0:T(8,128)(2,1)} %join.1.refs_0_), channel_id=1, source_target_pairs={{0,192},{4,68},{32,224},{36,100},{64,0},{68,132},{96,32},{100,164}... | collective-permute-start | bytes 393224 | tf_op jit(solution)/shard_map/ppermute | solution.py:46
  9.1 11.1 %collective-permute-start.12 = (bf16[256,256]{1,0:T(8,128)(2,1)}, bf16[256,256]{1,0:T(8,128)(2,1)S(1)}, u32[]{:S(2)}, u32[]{:S(2)}) collective-permute-start(bf16[256,256]{1,0:T(8,128)(2,1)} %join.1.refs_0_), channel_id=1, source_target_pairs={{0,224},{4,36},{32,0},{36,68},{64,32},{68,100},{96,64},{100,132},{... | collective-permute-start | bytes 393224 | tf_op jit(solution)/shard_map/ppermute | solution.py:46
  9.9 11.7 %collective-permute-start.11 = (bf16[256,256]{1,0:T(8,128)(2,1)}, bf16[256,256]{1,0:T(8,128)(2,1)S(1)}, u32[]{:S(2)}, u32[]{:S(2)}) collective-permute-start(bf16[256,256]{1,0:T(8,128)(2,1)} %join.1.refs_0_), channel_id=1, source_target_pairs={{0,32},{4,228},{32,64},{36,4},{64,96},{68,36},{96,128},{100,68},{1... | collective-permute-start | bytes 393224 | tf_op jit(solution)/shard_map/ppermute | solution.py:46
  14.2 10.9 %collective-permute-start.6 = (bf16[256,256]{1,0:T(8,128)(2,1)S(1)}, bf16[256,256]{1,0:T(8,128)(2,1)S(1)}, u32[]{:S(2)}, u32[]{:S(2)}) collective-permute-start(bf16[256,256]{1,0:T(8,128)(2,1)S(1)} %collective-permute-done.3.refs_3_), channel_id=1, source_target_pairs={{0,64},{4,196},{32,96},{36,228},{64,128},{68,4},{96,160},{100,36},... | collective-permute-start | bytes 393224 | tf_op jit(solution)/shard_map/ppermute | solution.py:46
  18.8 6.3 %collective-permute-start.4 = (bf16[256,256]{1,0:T(8,128)(2,1)S(1)}, bf16[256,256]{1,0:T(8,128)(2,1)S(1)}, u32[]{:S(2)}, u32[]{:S(2)}) collective-permute-start(bf16[256,256]{1,0:T(8,128)(2,1)S(1)} %collective-permute-done.3.refs_3_), channel_id=1, source_target_pairs={{0,32},{4,228},{32,64},{36,4},{64,96},{68,36},{96,128},{100,68},{1... | collective-permute-start | bytes 393224 | tf_op jit(solution)/shard_map/ppermute | solution.py:46
  18.8 7.3 %collective-permute-start.5 = (bf16[256,256]{1,0:T(8,128)(2,1)S(1)}, bf16[256,256]{1,0:T(8,128)(2,1)S(1)}, u32[]{:S(2)}, u32[]{:S(2)}) collective-permute-start(bf16[256,256]{1,0:T(8,128)(2,1)S(1)} %collective-permute-done.2.refs_0_), channel_id=1, source_target_pairs={{0,224},{4,36},{32,0},{36,68},{64,32},{68,100},{96,64},{100,132},{... | collective-permute-start | bytes 393224 | tf_op jit(solution)/shard_map/ppermute | solution.py:46
  20.2 8.4 %collective-permute-start = (s32[32,32]{1,0:T(8,128)S(1)}, s32[32,32]{1,0:T(8,128)S(1)}, u32[]{:S(2)}, u32[]{:S(2)}) collective-permute-start(s32[32,32]{1,0:T(8,128)S(1)} %bitcast.17), channel_id=1, source_target_pairs={{0,1},{1,0},{2,3},{3,2},{4,5},{5,4},{6,7},{7,6},{8,9},{9,8},{10,11... | collective-permute-start | bytes 12296 | tf_op jit(solution)/shard_map/ppermute | solution.py:455
  21.5 0.9 copy-start
  22.5 10.7 %copy-start.1 = (bf16[256,512]{1,0:T(8,128)(2,1)S(1)}, bf16[256,512]{1,0:T(8,128)(2,1)}, u32[]{:S(2)}) copy-start(bf16[256,512]{1,0:T(8,128)(2,1)} %query.1) | copy-start | bytes 786436
  22.5 10.7 %copy-start.2 = (bf16[256,512]{1,0:T(8,128)(2,1)S(1)}, bf16[256,512]{1,0:T(8,128)(2,1)}, u32[]{:S(2)}) copy-start(bf16[256,512]{1,0:T(8,128)(2,1)} %grad_out.1) | copy-start | bytes 786436
  22.5 15.0 %collective-permute-start.14 = (bf16[4,256,256]{2,1,0:T(8,128)(2,1)S(1)}, bf16[4,256,256]{2,1,0:T(8,128)(2,1)S(1)}, u32[]{:S(2)}, u32[]{:S(2)}) collective-permute-start(bf16[4,256,256]{2,1,0:T(8,128)(2,1)S(1)} %stack.3.refs_0_), channel_id=1, source_target_pairs={{0,8},{4,28},{8,16},{12,4},{16,24},{20,12},{24,0},{28,20},{1,9},{5... | collective-permute-start | bytes 1572872 | tf_op jit(solution)/shard_map/ppermute | solution.py:46
  26.1 12.0 %collective-permute-start.8 = (bf16[4,256,256]{2,1,0:T(8,128)(2,1)S(1)}, bf16[4,256,256]{2,1,0:T(8,128)(2,1)S(1)}, u32[]{:S(2)}, u32[]{:S(2)}) collective-permute-start(bf16[4,256,256]{2,1,0:T(8,128)(2,1)S(1)} %stack.2.refs_1_), channel_id=1, source_target_pairs={{0,8},{4,28},{8,16},{12,4},{16,24},{20,12},{24,0},{28,20},{1,9},{5... | collective-permute-start | bytes 1572872 | tf_op jit(solution)/shard_map/ppermute | solution.py:46
  28.7 4.2 %collective-permute-start.1 = (s32[32,32]{1,0:T(8,128)S(1)}, s32[32,32]{1,0:T(8,128)S(1)}, u32[]{:S(2)}, u32[]{:S(2)}) collective-permute-start(s32[32,32]{1,0:T(8,128)S(1)} %bitcast_add_fusion.1), channel_id=1, source_target_pairs={{0,2},{2,0},{1,3},{3,1},{4,6},{6,4},{5,7},{7,5},{8,10},{10,8},{9,1... | collective-permute-start | bytes 12296 | tf_op jit(solution)/shard_map/ppermute | solution.py:456
  32.9 15.3 %collective-permute-start.13 = (bf16[4,256,256]{2,1,0:T(8,128)(2,1)S(1)}, bf16[4,256,256]{2,1,0:T(8,128)(2,1)S(1)}, u32[]{:S(2)}, u32[]{:S(2)}) collective-permute-start(bf16[4,256,256]{2,1,0:T(8,128)(2,1)S(1)} %stack.3.refs_0_), channel_id=1, source_target_pairs={{0,24},{4,12},{8,0},{12,20},{16,8},{20,28},{24,16},{28,4},{1,25},{... | collective-permute-start | bytes 1572872 | tf_op jit(solution)/shard_map/ppermute | solution.py:46
  32.9 26.4 %collective-permute-start.7 = (bf16[4,256,256]{2,1,0:T(8,128)(2,1)S(1)}, bf16[4,256,256]{2,1,0:T(8,128)(2,1)S(1)}, u32[]{:S(2)}, u32[]{:S(2)}) collective-permute-start(bf16[4,256,256]{2,1,0:T(8,128)(2,1)S(1)} %stack.2.refs_1_), channel_id=1, source_target_pairs={{0,24},{4,12},{8,0},{12,20},{16,8},{20,28},{24,16},{28,4},{1,25},{... | collective-permute-start | bytes 1572872 | tf_op jit(solution)/shard_map/ppermute | solution.py:46
  33.2 7.6 %collective-permute-start.10 = (bf16[2,1024,128]{2,1,0:T(8,128)(2,1)S(1)}, bf16[2,1024,128]{2,1,0:T(8,128)(2,1)S(1)}, u32[]{:S(2)}, u32[]{:S(2)}) collective-permute-start(bf16[2,1024,128]{2,1,0:T(8,128)(2,1)S(1)} %prepare.1.refs_4_.refs_2_.refs_1_), channel_id=1, source_target_pairs={{0,4},{4,0},{1,5},{5,1},{2,6},{6,2},{3,7},{7,3},{8,12},{12,8},{9,1... | collective-permute-start | bytes 1572872 | tf_op jit(solution)/shard_map/ppermute | solution.py:50
  37.5 14.0 %collective-permute-start.15 = (bf16[4,256,256]{2,1,0:T(8,128)(2,1)S(1)}, bf16[4,256,256]{2,1,0:T(8,128)(2,1)S(1)}, u32[]{:S(2)}, u32[]{:S(2)}) collective-permute-start(bf16[4,256,256]{2,1,0:T(8,128)(2,1)S(1)} %collective-permute-done.14.refs_2_.refs_0_), channel_id=1, source_target_pairs={{0,8},{4,28},{8,16},{12,4},{16,24},{20,12},{24,0},{28,20},{1,9},{5... | collective-permute-start | bytes 1572872 | tf_op jit(solution)/shard_map/ppermute | solution.py:46
  38.1 21.6 %collective-permute-start.9 = (bf16[4,256,256]{2,1,0:T(8,128)(2,1)S(1)}, bf16[4,256,256]{2,1,0:T(8,128)(2,1)S(1)}, u32[]{:S(2)}, u32[]{:S(2)}) collective-permute-start(bf16[4,256,256]{2,1,0:T(8,128)(2,1)S(1)} %collective-permute-done.8.refs_3_.refs_1_), channel_id=1, source_target_pairs={{0,8},{4,28},{8,16},{12,4},{16,24},{20,12},{24,0},{28,20},{1,9},{5... | collective-permute-start | bytes 1572872 | tf_op jit(solution)/shard_map/ppermute | solution.py:46
  60.9 3.7 %collective-permute-start.16 = (f32[2,3,1024]{2,1,0:T(4,128)S(1)}, f32[2,3,1024]{2,1,0:T(4,128)S(1)}, u32[]{:S(2)}, u32[]{:S(2)}) collective-permute-start(f32[2,3,1024]{2,1,0:T(4,128)S(1)} %get-tuple-element.51.refs_3_.refs_4_.mine), channel_id=1, source_target_pairs={{0,4},{4,0},{1,5},{5,1},{2,6},{6,2},{3,7},{7,3},{8,12},{12,8},{9,1... | collective-permute-start | bytes 73736 | tf_op jit(solution)/shard_map/ppermute | solution.py:50
  65.4 10.9 %collective-permute-start.24 = (bf16[4,256,256]{2,1,0:T(8,128)(2,1)S(1)}, bf16[4,256,256]{2,1,0:T(8,128)(2,1)S(1)}, u32[]{:S(2)}, u32[]{:S(2)}) collective-permute-start(bf16[4,256,256]{2,1,0:T(8,128)(2,1)S(1)} %get-tuple-element.75), channel_id=1, source_target_pairs={{0,24},{4,12},{8,0},{12,20},{16,8},{20,28},{24,16},{28,4},{1,25},{... | collective-permute-start | bytes 1572872 | tf_op jit(solution)/shard_map/ppermute | solution.py:46
  66.3 16.9 %collective-permute-start.19 = (bf16[4,256,256]{2,1,0:T(8,128)(2,1)S(1)}, bf16[4,256,256]{2,1,0:T(8,128)(2,1)S(1)}, u32[]{:S(2)}, u32[]{:S(2)}) collective-permute-start(bf16[4,256,256]{2,1,0:T(8,128)(2,1)S(1)} %get-tuple-element.68), channel_id=1, source_target_pairs={{0,24},{4,12},{8,0},{12,20},{16,8},{20,28},{24,16},{28,4},{1,25},{... | collective-permute-start | bytes 1572872 | tf_op jit(solution)/shard_map/ppermute | solution.py:46
  69.7 35.0 %collective-permute-start.21 = (bf16[4,256,256]{2,1,0:T(8,128)(2,1)S(1)}, bf16[4,256,256]{2,1,0:T(8,128)(2,1)S(1)}, u32[]{:S(2)}, u32[]{:S(2)}) collective-permute-start(bf16[4,256,256]{2,1,0:T(8,128)(2,1)S(1)} %get-tuple-element.69), channel_id=1, source_target_pairs={{0,8},{4,28},{8,16},{12,4},{16,24},{20,12},{24,0},{28,20},{1,9},{5... | collective-permute-start | bytes 1572872 | tf_op jit(solution)/shard_map/ppermute | solution.py:46
  76.2 23.0 %collective-permute-start.26 = (bf16[4,256,256]{2,1,0:T(8,128)(2,1)S(1)}, bf16[4,256,256]{2,1,0:T(8,128)(2,1)S(1)}, u32[]{:S(2)}, u32[]{:S(2)}) collective-permute-start(bf16[4,256,256]{2,1,0:T(8,128)(2,1)S(1)} %get-tuple-element.76), channel_id=1, source_target_pairs={{0,8},{4,28},{8,16},{12,4},{16,24},{20,12},{24,0},{28,20},{1,9},{5... | collective-permute-start | bytes 1572872 | tf_op jit(solution)/shard_map/ppermute | solution.py:46
  76.4 24.4 %collective-permute-start.25 = (bf16[4,256,256]{2,1,0:T(8,128)(2,1)S(1)}, bf16[4,256,256]{2,1,0:T(8,128)(2,1)S(1)}, u32[]{:S(2)}, u32[]{:S(2)}) collective-permute-start(bf16[4,256,256]{2,1,0:T(8,128)(2,1)S(1)} %add_convert_fusion), channel_id=1, source_target_pairs={{0,24},{4,12},{8,0},{12,20},{16,8},{20,28},{24,16},{28,4},{1,25},{... | collective-permute-start | bytes 1572872 | tf_op jit(solution)/shard_map/ppermute | solution.py:46
  83.4 32.6 %collective-permute-start.20 = (bf16[4,256,256]{2,1,0:T(8,128)(2,1)S(1)}, bf16[4,256,256]{2,1,0:T(8,128)(2,1)S(1)}, u32[]{:S(2)}, u32[]{:S(2)}) collective-permute-start(bf16[4,256,256]{2,1,0:T(8,128)(2,1)S(1)} %add_convert_fusion.1), channel_id=1, source_target_pairs={{0,24},{4,12},{8,0},{12,20},{16,8},{20,28},{24,16},{28,4},{1,25},{... | collective-permute-start | bytes 1572872 | tf_op jit(solution)/shard_map/ppermute | solution.py:46
  83.4 44.1 %collective-permute-start.17 = (f32[128,1024]{1,0:T(8,128)S(1)}, f32[128,1024]{1,0:T(8,128)S(1)}, u32[]{:S(2)}, u32[]{:S(2)}) collective-permute-start(f32[128,1024]{1,0:T(8,128)S(1)} %get-tuple-element.53), channel_id=1, source_target_pairs={{0,4},{4,0},{1,5},{5,1},{2,6},{6,2},{3,7},{7,3},{8,12},{12,8},{9,1... | collective-permute-start | bytes 1572872 | tf_op jit(solution)/shard_map/ppermute | solution.py:50
  99.2 28.3 %collective-permute-start.18 = (f32[128,1024]{1,0:T(8,128)S(1)}, f32[128,1024]{1,0:T(8,128)S(1)}, u32[]{:S(2)}, u32[]{:S(2)}) collective-permute-start(f32[128,1024]{1,0:T(8,128)S(1)} %get-tuple-element.63), channel_id=1, source_target_pairs={{0,4},{4,0},{1,5},{5,1},{2,6},{6,2},{3,7},{7,3},{8,12},{12,8},{9,1... | collective-permute-start | bytes 1572872 | tf_op jit(solution)/shard_map/ppermute | solution.py:50
  101.0 15.1 %collective-permute-start.27 = (bf16[256,256]{1,0:T(8,128)(2,1)S(1)}, bf16[256,256]{1,0:T(8,128)(2,1)S(1)}, u32[]{:S(2)}, u32[]{:S(2)}) collective-permute-start(bf16[256,256]{1,0:T(8,128)(2,1)S(1)} %get-tuple-element.79), channel_id=1, source_target_pairs={{0,224},{4,36},{32,0},{36,68},{64,32},{68,100},{96,64},{100,132},{... | collective-permute-start | bytes 393224 | tf_op jit(solution)/shard_map/ppermute | solution.py:46
  104.8 15.4 %collective-permute-start.28 = (bf16[256,256]{1,0:T(8,128)(2,1)S(1)}, bf16[256,256]{1,0:T(8,128)(2,1)S(1)}, u32[]{:S(2)}, u32[]{:S(2)}) collective-permute-start(bf16[256,256]{1,0:T(8,128)(2,1)S(1)} %get-tuple-element.80), channel_id=1, source_target_pairs={{0,192},{4,68},{32,224},{36,100},{64,0},{68,132},{96,32},{100,164}... | collective-permute-start | bytes 393224 | tf_op jit(solution)/shard_map/ppermute | solution.py:46
  115.9 6.9 %collective-permute-start.29 = (bf16[256,256]{1,0:T(8,128)(2,1)S(1)}, bf16[256,256]{1,0:T(8,128)(2,1)S(1)}, u32[]{:S(2)}, u32[]{:S(2)}) collective-permute-start(bf16[256,256]{1,0:T(8,128)(2,1)S(1)} %get-tuple-element.81), channel_id=1, source_target_pairs={{0,32},{4,228},{32,64},{36,4},{64,96},{68,36},{96,128},{100,68},{1... | collective-permute-start | bytes 393224 | tf_op jit(solution)/shard_map/ppermute | solution.py:46
  116.2 12.4 %collective-permute-start.22 = (bf16[256,256]{1,0:T(8,128)(2,1)S(1)}, bf16[256,256]{1,0:T(8,128)(2,1)S(1)}, u32[]{:S(2)}, u32[]{:S(2)}) collective-permute-start(bf16[256,256]{1,0:T(8,128)(2,1)S(1)} %get-tuple-element.71), channel_id=1, source_target_pairs={{0,224},{4,36},{32,0},{36,68},{64,32},{68,100},{96,64},{100,132},{... | collective-permute-start | bytes 393224 | tf_op jit(solution)/shard_map/ppermute | solution.py:46
  120.2 8.5 %collective-permute-start.23 = (bf16[256,256]{1,0:T(8,128)(2,1)S(1)}, bf16[256,256]{1,0:T(8,128)(2,1)S(1)}, u32[]{:S(2)}, u32[]{:S(2)}) collective-permute-start(bf16[256,256]{1,0:T(8,128)(2,1)S(1)} %get-tuple-element.72), channel_id=1, source_target_pairs={{0,32},{4,228},{32,64},{36,4},{64,96},{68,36},{96,128},{100,68},{1... | collective-permute-start | bytes 393224 | tf_op jit(solution)/shard_map/ppermute | solution.py:46
  122.9 9.0 %collective-permute-start.30 = (bf16[256,256]{1,0:T(8,128)(2,1)S(1)}, bf16[256,256]{1,0:T(8,128)(2,1)S(1)}, u32[]{:S(2)}, u32[]{:S(2)}) collective-permute-start(bf16[256,256]{1,0:T(8,128)(2,1)S(1)} %get-tuple-element.82), channel_id=1, source_target_pairs={{0,64},{4,196},{32,96},{36,228},{64,128},{68,4},{96,160},{100,36},... | collective-permute-start | bytes 393224 | tf_op jit(solution)/shard_map/ppermute | solution.py:46
  127.6 8.7 %collective-permute-start.31 = (bf16[256,256]{1,0:T(8,128)(2,1)S(1)}, bf16[256,256]{1,0:T(8,128)(2,1)S(1)}, u32[]{:S(2)}, u32[]{:S(2)}) collective-permute-start(bf16[256,256]{1,0:T(8,128)(2,1)S(1)} %get-tuple-element.83), channel_id=1, source_target_pairs={{0,192},{4,68},{32,224},{36,100},{64,0},{68,132},{96,32},{100,164}... | collective-permute-start | bytes 393224 | tf_op jit(solution)/shard_map/ppermute | solution.py:46
